TPU v7x, 32 devices: a whole 2x2x4 slice. The times are simulated.
32 devices in a mesh: row: 4 (over y, x), col: 8 (over z, core).
Axes of the slice: x: 2, y: 2, z: 4, core: 2. Of those that a mesh axis runs over, the one named last changes fastest.
Arguments:
- fitting: bfloat16 [64, 512, 256], P(('row', 'col')), may hold values from -6 to 6
- coefficients: bfloat16 [16, 16, 6, 256, 128], P('row', 'col'), may hold values from -0.375 to 0.375
- amplitudes: bfloat16 [16, 16, 4096], P('row', 'col'), may hold values from -6 to 6
- intersections: bfloat16 [16, 16, 8, 4096], P('row', 'col'), may hold values from -0.33 to 1.33
- virtual_energy: float32 [16, 16, 64], P('row', 'col'), may hold values from 0.2 to 2
- occupied_energy: float32 [16], replicated, may hold values from -1.5 to -0.3
- kept_count: int32 [16, 16], P('row', 'col'), may hold values from 16 to 64
- orbital_atoms: int32 [16, 3], replicated, may hold values from 0 to 63, as said below
- fock_partner: int32 [16, 4], replicated, may hold values from 0 to 15, as said below
- fock_value: float32 [16, 4], replicated, may hold values from -3 to 3
Outputs:
- residual: float32 [16, 16, 4096], P('row', 'col')
Inputs may be any that keep to these rules, and one draw needn't show every extreme that they name: `orbital_atoms`: the 3 atoms of orbital i are different and lie in [(i // 4) * 16, (i // 4 + 1) * 16). fock_partner[i, n] differs from i by at most 2.
All inputs are finite; a program needn't handle non-finite values.
Results may differ from a plain program's by a relative error of at most 0.0029.
Values may be sent and summed in bfloat16 or wider, within the bound.
No kernel may reach another device: no remote copies, remote signals or barrier semaphores. Data moves between devices by JAX's collectives and lax.ppermute only.
A program may use at most 128 MiB of HBM per device.

v0:
```python
import jax
import jax.numpy as jnp
from jax import lax
from jax.sharding import PartitionSpec as P

AUX = 512
NPNO = 64
DOMAIN = 3
PARTNERS = 4


def from_root(value, axis, source):
    kept = jnp.where(lax.axis_index(axis) == source, value, 0).astype(value.dtype)
    return lax.psum(kept, axis)


def passed_along(block, axis, distance):
    devices = range(lax.axis_size(axis))
    route = [(i - distance, i) for i in devices if i - distance in devices]
    return lax.ppermute(block, axis, route)


def on_device(
    fitting,
    coefficients,
    amplitudes,
    intersections,
    virtual_energy,
    occupied_energy,
    kept_count,
    orbital_atoms,
    fock_partner,
    fock_value,
):
    row_count = amplitudes.shape[0]
    column_count = amplitudes.shape[1]
    domain_size = orbital_atoms.shape[1]
    row_place = lax.axis_index("row")
    column_place = lax.axis_index("col")
    row_atoms = fitting.shape[0] * lax.axis_size("col")
    first_row = row_place * row_count
    first_column = column_place * column_count
    wanted = (
        lax.dynamic_slice_in_dim(orbital_atoms, first_row, row_count, 0) - row_place * row_atoms
    )
    piece = lax.all_gather(fitting, "col", axis=0, tiled=True)
    labels = jnp.arange(piece.shape[0], dtype=jnp.int32)
    picker = (wanted[:, :, None] == labels[None, None, :]).astype(jnp.bfloat16)
    added = jnp.einsum("ism,map->isap", picker, piece, preferred_element_type=jnp.float32)
    row_fit = added.astype(jnp.bfloat16)
    source_row = first_column // row_count
    offset = first_column - source_row * row_count
    own_part = lax.dynamic_slice_in_dim(row_fit, offset, column_count, 0)
    column_fit = from_root(own_part, "row", source_row)
    own_side = jnp.einsum(
        "isap,ijspq->ijsaq",
        row_fit,
        coefficients[:, :, :domain_size],
        preferred_element_type=jnp.float32,
    ).astype(jnp.bfloat16)
    other_side = jnp.einsum(
        "jsap,ijspq->ijsaq",
        column_fit,
        coefficients[:, :, domain_size:],
        preferred_element_type=jnp.float32,
    ).astype(jnp.bfloat16)
    exchange_part = jnp.einsum(
        "ijsaq,ijsar->ijqr",
        own_side[..., :NPNO],
        own_side[..., NPNO:],
        preferred_element_type=jnp.float32,
    )
    exchange_part = exchange_part + jnp.einsum(
        "ijsaq,ijsar->ijqr",
        other_side[..., :NPNO],
        other_side[..., NPNO:],
        preferred_element_type=jnp.float32,
    )
    exchange_part = exchange_part * (2 * DOMAIN * AUX) ** (-0.5)
    row_partner = lax.dynamic_slice_in_dim(fock_partner, first_row, row_count, 0)
    column_partner = lax.dynamic_slice_in_dim(fock_partner, first_column, column_count, 0)
    below_rows = passed_along(amplitudes[row_count - column_count :], "row", 1)
    above_rows = passed_along(amplitudes[:column_count], "row", -1)
    row_source = jnp.concatenate([below_rows, amplitudes, above_rows], axis=0)
    below_columns = passed_along(amplitudes, "col", 1)
    above_columns = passed_along(amplitudes, "col", -1)
    column_source = jnp.concatenate([below_columns, amplitudes, above_columns], axis=1)
    row_pick = row_partner - (first_row - column_count)
    column_pick = column_partner - (first_column - column_count)
    from_rows = jnp.transpose(jnp.take(row_source, row_pick, axis=0), (0, 2, 1, 3))
    from_columns = jnp.take(column_source, column_pick, axis=1)
    partners = jnp.concatenate([from_rows, from_columns], axis=2).reshape(
        row_count, column_count, 2 * PARTNERS, NPNO, NPNO
    )
    intersection_mats = intersections.reshape(row_count, column_count, 2 * PARTNERS, NPNO, NPNO)
    half = jnp.einsum(
        "ijnab,ijnbc->ijnac", intersection_mats, partners, preferred_element_type=jnp.float32
    ).astype(jnp.bfloat16)
    sandwich = jnp.einsum(
        "ijnac,ijndc->ijnad", half, intersection_mats, preferred_element_type=jnp.float32
    )
    row_weight = lax.dynamic_slice_in_dim(fock_value, first_row, row_count, 0)
    column_weight = lax.dynamic_slice_in_dim(fock_value, first_column, column_count, 0)
    weights = jnp.concatenate(
        [
            jnp.broadcast_to(row_weight[:, None, :], (row_count, column_count, PARTNERS)),
            jnp.broadcast_to(column_weight[None, :, :], (row_count, column_count, PARTNERS)),
        ],
        axis=2,
    )
    coupling = jnp.einsum("ijn,ijnad->ijad", weights, sandwich)
    row_occupied = lax.dynamic_slice_in_dim(occupied_energy, first_row, row_count, 0)
    column_occupied = lax.dynamic_slice_in_dim(occupied_energy, first_column, column_count, 0)
    shift = (
        virtual_energy[:, :, :, None]
        + virtual_energy[:, :, None, :]
        - row_occupied[:, None, None, None]
        - column_occupied[None, :, None, None]
    )
    current = amplitudes.reshape(row_count, column_count, NPNO, NPNO).astype(jnp.float32)
    result = exchange_part + shift * current - coupling
    levels = jnp.arange(NPNO, dtype=jnp.int32)
    count = kept_count[:, :, None, None]
    keep = (levels[None, None, :, None] < count) & (levels[None, None, None, :] < count)
    masked = jnp.where(keep, result, jnp.zeros_like(result))
    return masked.reshape(row_count, column_count, NPNO * NPNO)


def solution(mesh):
    placed = (
        P(("row", "col"), None, None),
        P("row", "col", None, None, None),
        P("row", "col", None),
        P("row", "col", None, None),
        P("row", "col", None),
        P(),
        P("row", "col"),
        P(),
        P(),
        P(),
    )
    return jax.shard_map(
        on_device, mesh=mesh, in_specs=placed, out_specs=P("row", "col", None), check_vma=False
    )
```

profile of v0, /device:TPU:0, one launch (start us, length us, event | category | flops | bytes accessed | tf_op | source)
XLA Modules:
  0.0 140.4 jit_solution(9856351104734373126)
XLA Ops:
  6.5 0.7 all-gather.2.cloned.1.call-update
  7.3 0.9 copy.83
  8.2 2.4 %collective-permute-start.2 = (bf16[4,2,4096]{2,0,1:T(4,128)(2,1)S(1)}, bf16[4,2,4096]{2,0,1:T(4,128)(2,1)S(1)}, u32[]{:S(2)}, u32[]{:S(2)}) collective-permute-start(bf16[4,2,4096]{2,0,1:T(4,128)(2,1)S(1)} %copy.83), channel_id=1, source_target_pairs={{0,1},{1,2},{2,3},{3,4},{4,5},{5,6},{6,7},{8,9},{9,10},{10,11},{11... | collective-permute-start | bytes 196616 | tf_op jit(solution)/shard_map/ppermute | solution.py:20
  10.6 1.3 collective-permute-start.3
  11.9 0.8 fusion.65
  12.7 4.2 %collective-permute-start = (bf16[2,2,4096]{2,1,0:T(2,128)(2,1)S(1)}, bf16[2,2,4096]{2,1,0:T(2,128)(2,1)S(1)}, u32[]{:S(2)}, u32[]{:S(2)}) collective-permute-start(bf16[2,2,4096]{2,1,0:T(2,128)(2,1)S(1)} %get-tuple-element.15), channel_id=1, source_target_pairs={{0,8},{8,16},{16,24},{1,9},{9,17},{17,25},{2,10},{10,18},{18,26},{... | collective-permute-start | bytes 98312 | tf_op jit(solution)/shard_map/ppermute | solution.py:20
  16.9 1.3 collective-permute-start.1
  18.2 0.8 compare_and_fusion
  19.0 0.1 copy.86
  19.2 0.8 compare_and_fusion.1
  20.0 0.1 copy.80
  20.0 0.1 reshape.50
  20.2 0.1 copy.78
  20.4 0.1 copy.77
  20.5 0.8 copy.67
  21.2 0.6 pad_clamp_fusion
  21.9 0.6 iota_compare_fusion.1
  22.5 3.4 %fusion.63 = (bf16[4,2,3,256,128]{4,3,2,1,0:T(8,128)(2,1)S(1)}, bf16[4,2,3,256,128]{4,3,2,1,0:T(8,128)(2,1)}) fusion(bf16[4,2,6,256,128]{4,3,2,1,0:T(8,128)(2,1)} %param.11), kind=kLoop, calls=%fused_computation.53 | loop fusion | bytes 6291456 | tf_op jit(solution)/shard_map/slice | solution.py:64
  26.0 0.6 dynamic_slice.27
  26.6 0.6 dynamic_slice.26
  27.2 0.9 reshape.47
  28.1 0.7 copy.82
  28.7 0.6 copy.79
  29.4 1.1 reshape.45
  30.5 0.6 copy-done.5
  31.2 1.0 pad_maximum_fusion.2
  32.1 1.1 gather_fusion
  33.2 0.9 fusion.58
  34.1 1.0 pad_maximum_fusion.1
  35.1 0.9 gather_fusion.1
  36.0 0.4 fusion.57
  36.4 0.3 pad_maximum_fusion
  36.6 2.1 %reshape.44 = bf16[4,2,8,64,64]{4,3,2,1,0:T(8,128)(2,1)} reshape(bf16[4,2,8,4096]{3,2,1,0:T(8,128)(2,1)S(1)} %pad_maximum_fusion) | data formatting | bytes 1048576 | tf_op jit(solution)/shard_map/reshape | solution.py:92
  38.7 20.1 %all-gather.2.cloned.1.call-done = bf16[16,512,256]{2,1,0:T(8,128)(2,1)} async-done(((bf16[2,512,256]{2,1,0:T(8,128)(2,1)}), bf16[16,512,256]{2,1,0:T(8,128)(2,1)}) %all-gather.2.cloned.1.call-update) | async-done | bytes 4194320 | tf_op jit(solution)/shard_map/all_gather | solution.py:46
  58.8 5.3 %fusion.7 = bf16[4,3,512,256]{3,0,2,1:T(4,128)(2,1)S(1)} fusion(bf16[16,512,256]{2,1,0:T(8,128)(2,1)} %all-gather.2.cloned.1.call-done, s32[4,3]{0,1:T(4,128)S(1)} %dynamic-slice_subtract_fusion), kind=kOutput, calls=%fused_computation.10 | convolution fusion | flops 51904704 | bytes 7340080 | tf_op jit(solution)/shard_map/ism,map->isap/dot_general | solution.py:49
  64.1 1.6 %copy-done.1 = bf16[4,3,512,256]{3,0,2,1:T(4,128)(2,1)} copy-done((bf16[4,3,512,256]{3,0,2,1:T(4,128)(2,1)}, bf16[4,3,512,256]{3,0,2,1:T(4,128)(2,1)S(1)}, u32[]{:S(2)}) %copy-start.1) | copy-done | bytes 3145752
  65.7 3.2 %broadcast_select_fusion = bf16[2,3,512,256]{3,0,2,1:T(2,128)(2,1)} fusion(pred[]{:T(512)S(6)} %eq.19, bf16[4,3,512,256]{3,0,2,1:T(4,128)(2,1)S(1)} %fusion.7, s32[]{:T(128)S(6)} %select_n.56), kind=kLoop, calls=%fused_computation.9 | loop fusion | flops 786432 | bytes 3145733 | tf_op jit(solution)/shard_map/jit(_where)/select_n | solution.py:13
  69.0 3.5 %fusion.21 = bf16[4,2,8,64,64]{4,3,2,1,0:T(8,128)(2,1)} fusion(bf16[4,2,8,64,64]{4,3,2,1,0:T(8,128)(2,1)S(1)} %reshape.45, bf16[4,2,8,64,64]{4,3,2,1,0:T(8,128)(2,1)} %reshape.44), kind=kOutput, calls=%fused_computation.23 | convolution fusion | flops 67371008 | bytes 1572864 | tf_op jit(solution)/shard_map/ijnac,ijndc->ijnad/dot_general | solution.py:99
  72.5 2.3 %fusion.10 = f32[4,2,1,64,64]{4,2,3,1,0:T(1,128)S(1)} fusion(f32[4,2,8,1,1]{2,3,4,1,0:T(1,128)S(1)} %bitcast.58, bf16[4,2,8,64,64]{4,3,2,1,0:T(8,128)(2,1)} %fusion.21), kind=kOutput, calls=%fused_computation.11 | convolution fusion | flops 524288 | bytes 655616 | tf_op jit(solution)/shard_map/ijn,ijnad->ijad/dot_general | solution.py:111
  74.7 3.6 %convert_bitcast_fusion.1 = bf16[4,2,3,512,128]{3,4,1,2,0:T(8,128)(2,1)S(1)} fusion(bf16[4,3,512,256,1]{3,0,2,1,4:T(4,128)(2,1)} %bitcast.53, bf16[4,2,3,256,128]{4,3,2,1,0:T(8,128)(2,1)} %get-tuple-element.12), kind=kOutput, calls=%fused_computation.8 | convolution fusion | flops 806879232 | bytes 7864320 | tf_op jit(solution)/shard_map/isap,ijspq->ijsaq/dot_general | solution.py:55
  78.3 0.3 fusion.64
  78.7 0.6 fusion.22
  79.2 49.5 %all-reduce.2.cloned.1.call-done = bf16[2,3,512,256]{3,0,2,1:T(2,128)(2,1)} async-done(((bf16[2,3,512,256]{3,0,2,1:T(2,128)(2,1)}), bf16[2,3,512,256]{3,0,2,1:T(2,128)(2,1)}) %all-reduce.2.cloned.1.call-update) | async-done | bytes 1572880 | tf_op jit(solution)/shard_map/psum | solution.py:14
  128.8 2.5 %convert_bitcast_fusion = bf16[4,2,3,512,128]{3,4,0,2,1:T(8,128)(2,1)S(1)} fusion(bf16[4,2,3,256,128]{4,3,2,1,0:T(8,128)(2,1)S(1)} %get-tuple-element.11, bf16[2,3,512,256,1]{3,0,2,1,4:T(2,128)(2,1)} %bitcast.54), kind=kOutput, calls=%fused_computation.7 | convolution fusion | flops 806879232 | bytes 6291456 | tf_op jit(solution)/shard_map/jsap,ijspq->ijsaq/dot_general | solution.py:61
  131.3 0.4 fusion.62
  131.6 0.5 copy-done.4
  132.2 0.6 fusion.52
  132.8 0.8 reshape.46
  (38 shorter events, 0.5 us)
Async XLA Ops:
  6.5 13.6 %copy-start = (f32[16,4]{0,1:T(4,128)S(1)}, f32[16,4]{0,1:T(4,128)}, u32[]{:S(2)}) copy-start(f32[16,4]{0,1:T(4,128)} %param.19) | copy-start | bytes 772
  6.5 52.3 %all-gather.2.cloned.1.call-start = ((), (), s32[]{:S(2)}) async-start(), calls=%async_computation | async-start | bytes 4718592 | tf_op jit(solution)/shard_map/all_gather | solution.py:46
  7.3 121.5 %all-reduce.2.cloned.1.call-start = ((), (), s32[]{:S(2)}) async-start(), calls=%async_computation.1 | async-start | bytes 3145728 | tf_op jit(solution)/shard_map/psum | solution.py:14
  8.2 25.9 %collective-permute-start.2 = (bf16[4,2,4096]{2,0,1:T(4,128)(2,1)S(1)}, bf16[4,2,4096]{2,0,1:T(4,128)(2,1)S(1)}, u32[]{:S(2)}, u32[]{:S(2)}) collective-permute-start(bf16[4,2,4096]{2,0,1:T(4,128)(2,1)S(1)} %copy.83), channel_id=1, source_target_pairs={{0,1},{1,2},{2,3},{3,4},{4,5},{5,6},{6,7},{8,9},{9,10},{10,11},{11... | collective-permute-start | bytes 196616 | tf_op jit(solution)/shard_map/ppermute | solution.py:20
  10.6 23.5 %collective-permute-start.3 = (bf16[4,2,4096]{2,0,1:T(4,128)(2,1)S(1)}, bf16[4,2,4096]{2,0,1:T(4,128)(2,1)}, u32[]{:S(2)}, u32[]{:S(2)}) collective-permute-start(bf16[4,2,4096]{2,0,1:T(4,128)(2,1)S(1)} %copy.83), channel_id=1, source_target_pairs={{1,0},{2,1},{3,2},{4,3},{5,4},{6,5},{7,6},{9,8},{10,9},{11,10},{12... | collective-permute-start | bytes 196616 | tf_op jit(solution)/shard_map/ppermute | solution.py:20
  12.7 17.8 %collective-permute-start = (bf16[2,2,4096]{2,1,0:T(2,128)(2,1)S(1)}, bf16[2,2,4096]{2,1,0:T(2,128)(2,1)S(1)}, u32[]{:S(2)}, u32[]{:S(2)}) collective-permute-start(bf16[2,2,4096]{2,1,0:T(2,128)(2,1)S(1)} %get-tuple-element.15), channel_id=1, source_target_pairs={{0,8},{8,16},{16,24},{1,9},{9,17},{17,25},{2,10},{10,18},{18,26},{... | collective-permute-start | bytes 98312 | tf_op jit(solution)/shard_map/ppermute | solution.py:20
  16.9 14.2 %collective-permute-start.1 = (bf16[2,2,4096]{2,1,0:T(2,128)(2,1)S(1)}, bf16[2,2,4096]{2,1,0:T(2,128)(2,1)}, u32[]{:S(2)}, u32[]{:S(2)}) collective-permute-start(bf16[2,2,4096]{2,1,0:T(2,128)(2,1)S(1)} %get-tuple-element.16), channel_id=1, source_target_pairs={{8,0},{16,8},{24,16},{9,1},{17,9},{25,17},{10,2},{18,10},{26,18},{... | collective-permute-start | bytes 98312 | tf_op jit(solution)/shard_map/ppermute | solution.py:20
  22.5 3.4 %copy-start.6 = (s32[16,3]{0,1:T(4,128)S(1)}, s32[16,3]{0,1:T(4,128)}, u32[]{:S(2)}) copy-start(s32[16,3]{0,1:T(4,128)} %param.17) | copy-start | bytes 580
  22.5 3.5 %copy-start.10 = (f32[16]{0:T(128)S(1)}, f32[16]{0:T(128)}, u32[]{:S(2)}) copy-start(f32[16]{0:T(128)} %param.15) | copy-start | bytes 196
  22.5 4.7 %copy-start.2 = (bf16[4,2,4096]{2,1,0:T(2,128)(2,1)S(1)}, bf16[4,2,4096]{2,1,0:T(2,128)(2,1)}, u32[]{:S(2)}) copy-start(bf16[4,2,4096]{2,1,0:T(2,128)(2,1)} %param.12) | copy-start | bytes 196612
  22.5 6.8 %copy-start.3 = (bf16[4,2,8,4096]{3,2,1,0:T(8,128)(2,1)S(1)}, bf16[4,2,8,4096]{3,2,1,0:T(8,128)(2,1)}, u32[]{:S(2)}) copy-start(bf16[4,2,8,4096]{3,2,1,0:T(8,128)(2,1)} %param.13) | copy-start | bytes 1572868
  30.5 5.5 %copy-start.8 = (pred[2,4]{1,0:T(4,128)(4,1)S(1)}, pred[2,4]{1,0:T(4,128)(4,1)}, u32[]{:S(2)}) copy-start(pred[2,4]{1,0:T(4,128)(4,1)} %copy.82) | copy-start | bytes 28
  30.5 0.6 copy-start.5
  64.1 1.6 %copy-start.1 = (bf16[4,3,512,256]{3,0,2,1:T(4,128)(2,1)}, bf16[4,3,512,256]{3,0,2,1:T(4,128)(2,1)S(1)}, u32[]{:S(2)}) copy-start(bf16[4,3,512,256]{3,0,2,1:T(4,128)(2,1)S(1)} %fusion.7) | copy-start | bytes 9437188
  131.2 1.0 copy-start.4
  131.2 0.9 copy-start.7
  131.2 0.9 copy-start.9
  131.3 0.9 copy-start.11
  131.3 0.9 copy-start.12
Sparse Core Ops, SparseCore 0:
  9.0 49.8 all-gather.1
  69.1 59.5 all-reduce.1
where the time goes:
time: 141 us; the launch traced here: 140 us
  waiting for transfers between devices  70.4 us (50%)
  local copies, waits for them, and re-layouts  19.4 us (14%)
  matrix products  18.2 us (13%)
  between operations  13.7 us (10%)
  other arithmetic  9.55 us (7%)
  starting transfers between devices  9.21 us (7%)
    psum x1, waiting for transfers between devices, from_root(): return lax.psum(kept, axis)  49.5 us
    all_gather x1, waiting for transfers between devices, on_device(): piece = lax.all_gather(fitting, 'col', axis=0, tiled=True)  20.1 us
    ppermute x4, starting transfers between devices, passed_along(): return lax.ppermute(block, axis, route)  9.17 us
    dot_general x1, matrix products, on_device(): jnp.einsum('ism,map->isap', picker, piece, preferred_element_type=jnp.flo...  5.27 us
    unnamed x28, local copies, waits for them, and re-layouts  4.48 us
    dot_general x1, matrix products, on_device(): jnp.einsum('isap,ijspq->ijsaq', row_fit, coefficients[:, :, :domain_size]...  3.59 us
    dot_general x1, matrix products, on_device(): jnp.einsum('ijnac,ijndc->ijnad', half, intersection_mats, preferred_eleme...  3.46 us
    slice x1, local copies, waits for them, and re-layouts, on_device(): coefficients[:, :, domain_size:]  3.42 us
  transfers between devices with their start and end apart: 6, of which 2 were waited for; matrix products, arithmetic and copies ran while one was open for 23% of the time, Pallas kernels for 0%

commit v1 on v0

v1 whole, which is shorter than its diff:
```python
import functools

import jax
import jax.numpy as jnp
from jax import lax
from jax.experimental import pallas as pl
from jax.experimental.pallas import tpu as pltpu
from jax.sharding import PartitionSpec as P

F32 = jnp.float32
BF16 = jnp.bfloat16
EXTRA = 16
VMEM = pl.BlockSpec(memory_space=pltpu.VMEM)
SMEM = pl.BlockSpec(memory_space=pltpu.SMEM)


def dot(a, b):
    return jnp.dot(a, b, preferred_element_type=F32)


def dot_nt(a, b):
    return lax.dot_general(a, b, (((1,), (1,)), ((), ())), preferred_element_type=F32)


def square_iota(n):
    return (
        lax.broadcasted_iota(jnp.int32, (n, n), 0),
        lax.broadcasted_iota(jnp.int32, (n, n), 1),
    )


def pack_kernel(fit_ref, out_ref):
    half = fit_ref.shape[2] // 2
    row, col = square_iota(half)
    place = lax.broadcasted_iota(jnp.int32, (EXTRA, half), 0)
    for atom in range(fit_ref.shape[0]):
        fit = fit_ref[atom]
        metric = lax.dot_general(fit, fit, (((0,), (0,)), ((), ())), preferred_element_type=F32)
        first, second = metric[:half, :half], metric[half:, half:]
        out_ref[atom, :half] = metric[:half, half:].astype(BF16)
        out_ref[atom, half : 2 * half] = jnp.where(row <= col, first, second).astype(BF16)
        lines = [jnp.sum(jnp.where(row == col, m, 0.0), axis=0, keepdims=True) for m in (first, second)]
        high = [line.astype(BF16).astype(F32) for line in lines]
        extra = jnp.where(
            place == 0,
            high[1],
            jnp.where(
                place == 1,
                lines[0] - high[0],
                jnp.where(place == 2, lines[1] - high[1], 0.0),
            ),
        )
        out_ref[atom, 2 * half :] = extra.astype(BF16)


def unpack(packed, metric_ref):
    half = packed.shape[1]
    row, col = square_iota(half)
    corner = packed[:half]
    both = packed[half : 2 * half].astype(F32)
    extra = packed[2 * half :].astype(F32)
    turned = both.T
    metric_ref[:half, :half] = jnp.where(row <= col, both, turned).astype(BF16)
    metric_ref[:half, half:] = corner
    metric_ref[half:, :half] = corner.astype(F32).T.astype(BF16)
    metric_ref[half:, half:] = jnp.where(
        row > col, both, jnp.where(row == col, extra[0:1], turned)
    ).astype(BF16)
    return jnp.concatenate([extra[1:2], extra[2:3]], axis=1)


def ring_order(units):
    return [0] + list(range(1, units, 2)) + list(range(units - units % 2 - (0 if units % 2 else 2), 0, -2))


def ring_place(unit, units):
    return jnp.where(unit % 2 == 1, (unit + 1) // 2, (units - unit // 2) % units)


def pick_place(atom, row_place, col_place, cores, units, held):
    label = jnp.clip(atom - row_place * (units * cores * held), 0, units * cores * held - 1)
    owner, slot = label // held, label % held
    turn = (ring_place(col_place // cores, units) - ring_place(owner // cores, units) + units) % units
    side = (col_place % cores - owner % cores + cores) % cores
    return (turn * cores + side) * held + slot


def collect(buffers, all_ref):
    held = buffers[0].shape[0]
    for index, buffer in enumerate(buffers):
        all_ref[index * held : (index + 1) * held] = buffer[...]


def select_kernel(cores, units, pieces, atoms_ref, *refs):
    count = units * cores
    buffers, outs, all_ref = refs[:count], refs[count:-1], refs[-1]
    held = buffers[0].shape[0]
    row_place, col_place = lax.axis_index("row"), lax.axis_index("col")
    domain = atoms_ref.shape[0]
    columns = sum(pieces) // domain
    collect(buffers, all_ref)
    targets = [(out, n) for out in outs for n in range(out.shape[0])]
    for index, (out, n) in enumerate(targets):
        atom = atoms_ref[index % domain, col_place * columns + index // domain]
        place = pick_place(atom, row_place, col_place, cores, units, held)
        out[n] = all_ref[place]


def neighbour_place(place, turn):
    return jnp.where(turn == 0, 0, jnp.where((place + turn) == jnp.bitwise_xor(place, 1), 1, 2))


def couple_kernel(
    partner_ref, value_ref, occupied_ref, coef_ref, inter_ref, virtual_ref, *refs,
):
    blocks = refs[:5]
    base_ref, turned_ref, flat_ref, wide_ref, mats_ref, inters_ref = refs[5:]
    row_count, column_count, terms, size = inter_ref.shape
    npno = base_ref.shape[2]
    lanes = 2 * npno
    chunks = size // lanes
    domain = coef_ref.shape[2] // 2
    partners = terms // 2
    row_place, col_place = lax.axis_index("row"), lax.axis_index("col")
    first_row = row_place * row_count
    first_col = col_place * column_count

    def square(lines):
        wide_ref[pl.ds(0, chunks, 2), :] = lines
        wide_ref[pl.ds(1, chunks, 2), :] = pltpu.roll(lines, npno, 1)
        return wide_ref[:, :npno].astype(BF16)

    for index, block in enumerate(blocks):

        def one_block(i, carry, index=index, block=block):
            for q in range(chunks):
                flat_ref[q, :column_count] = block[i, :, q * lanes : (q + 1) * lanes].astype(F32)
            for j in range(column_count):
                mats_ref[index * row_count + i, j] = square(flat_ref[:, j, :])
            return carry

        lax.fori_loop(0, row_count, one_block, 0)

    def one_row(i, carry):
        for j in range(column_count):
            for q in range(chunks):
                flat_ref[q] = inter_ref[i, j, :, q * lanes : (q + 1) * lanes].astype(F32)
            for n in range(terms):
                inters_ref[n] = square(flat_ref[:, n, :])
            total = jnp.zeros((npno, npno), F32)
            for n in range(terms):
                if n < partners:
                    away = partner_ref[n, first_row + i] - first_row + row_count
                    turn = away // row_count - 1
                    index = neighbour_place(row_place, turn) * row_count + away % row_count
                    weight = value_ref[n, first_row + i]
                    partner = mats_ref[index, j]
                else:
                    away = partner_ref[n - partners, first_col + j] - first_col + column_count
                    turn = away // column_count - 1
                    index = neighbour_place(col_place, turn)
                    index = jnp.where(index == 0, 0, index + 2) * row_count + i
                    weight = value_ref[n - partners, first_col + j]
                    partner = mats_ref[index, away % column_count]
                inter = inters_ref[n]
                half = dot(inter, partner).astype(BF16)
                total = total + weight * dot_nt(half, inter)
            levels = jnp.broadcast_to(virtual_ref[i, pl.ds(j, 1)], (npno, npno))
            shift = levels + levels.T - occupied_ref[first_row + i] - occupied_ref[first_col + j]
            base_ref[i, j] = shift * mats_ref[i, j].astype(F32) - total
            for s in range(domain):
                turned = coef_ref[i, j, domain + s].T
                turned_ref[j, s, pl.ds(pl.multiple_of(i * npno, npno), npno)] = turned[:npno]
        return carry

    lax.fori_loop(0, row_count, one_row, 0)


def row_kernel(cores, units, scale, atoms_ref, coef_ref, base_ref, *refs):
    count = units * cores
    buffers = refs[:count]
    out_ref, all_ref, metric_ref = refs[count:]
    held = buffers[0].shape[0]
    row_count, column_count = coef_ref.shape[:2]
    domain = coef_ref.shape[2] // 2
    npno = base_ref.shape[2]
    row_place, col_place = lax.axis_index("row"), lax.axis_index("col")
    collect(buffers, all_ref)

    def one_row(i, carry):
        totals = [None] * column_count
        for s in range(domain):
            atom = atoms_ref[s, row_place * row_count + i]
            place = pick_place(atom, row_place, col_place, cores, units, held)
            low = unpack(all_ref[place], metric_ref)
            left = jnp.concatenate([coef_ref[i, j, s].T[:npno] for j in range(column_count)], axis=0)
            product = dot(left, metric_ref[...]) + left.astype(F32) * low
            product = product.astype(BF16)
            for j in range(column_count):
                part = dot(product[j * npno : (j + 1) * npno], coef_ref[i, j, s])
                totals[j] = part if s == 0 else totals[j] + part
        for j in range(column_count):
            out_ref[i, j] = base_ref[i, j] + totals[j][:, npno:] * scale
        return carry

    lax.fori_loop(0, row_count, one_row, 0)


def column_kernel(routes, pieces, scale, kept_ref, coef_ref, turned_ref, base_ref, *refs):
    own_count = len(pieces)
    own_pieces = refs[:own_count]
    arrived = refs[own_count : own_count + len(routes)]
    out_ref, packed_ref, metric_ref, wide_ref, flat_ref = refs[own_count + len(routes) :]
    row_count, column_count = coef_ref.shape[:2]
    domain = coef_ref.shape[2] // 2
    npno = base_ref.shape[2]
    lanes = 2 * npno
    source = lax.axis_index("col") * column_count // row_count
    away = jnp.bitwise_xor(lax.axis_index("row"), source)
    starts = [sum(pieces[:p]) for p in range(own_count)]

    for p in range(own_count):

        @pl.when(away == 0)
        def _(p=p):
            packed_ref[starts[p] : starts[p] + pieces[p]] = own_pieces[p][...]

    for (p, takers), buffer in zip(routes, arrived):
        meant = functools.reduce(jnp.logical_or, [away == taker for taker in takers])

        @pl.when(meant)
        def _(p=p, buffer=buffer):
            packed_ref[starts[p] : starts[p] + pieces[p]] = buffer[...]

    totals = {}
    for index in range(column_count * domain):
        j, s = index // domain, index % domain
        low = unpack(packed_ref[index], metric_ref)
        left = turned_ref[j, s]
        product = dot(left, metric_ref[...]) + left.astype(F32) * low
        product = product.astype(BF16)
        for i in range(row_count):
            part = dot(product[i * npno : (i + 1) * npno], coef_ref[i, j, domain + s])
            totals[i, j] = part if s == 0 else totals[i, j] + part
    row, col = square_iota(npno)
    lane = lax.broadcasted_iota(jnp.int32, (npno // 2, lanes), 1)
    for i in range(row_count):
        for j in range(column_count):
            result = base_ref[i, j] + totals[i, j][:, npno:] * scale
            kept = kept_ref[j, i]
            result = jnp.where((row < kept) & (col < kept), result, 0.0)
            wide_ref[:, :npno] = result
            even = wide_ref[pl.ds(0, npno // 2, 2), :]
            odd = wide_ref[pl.ds(1, npno // 2, 2), :]
            flat_ref[i, j] = jnp.where(lane < npno, even, pltpu.roll(odd, npno, 1))
    for i in range(row_count):
        for q in range(npno // 2):
            out_ref[i, :, q * lanes : (q + 1) * lanes] = flat_ref[i, :, q, :]


def call(kernel, out_shape, in_specs, out_specs, scratch, name, flops, moved):
    return pl.pallas_call(
        kernel,
        out_shape=out_shape,
        in_specs=in_specs,
        out_specs=out_specs,
        scratch_shapes=scratch,
        compiler_params=pltpu.CompilerParams(vmem_limit_bytes=48 * 2**20),
        cost_estimate=pl.CostEstimate(flops=flops, bytes_accessed=moved, transcendentals=0),
        name=name,
    )


def swapped(block, axis, first):
    size = lax.axis_size(axis)
    pairs = [(n, n + 1) for n in range(first, size - 1, 2)]
    return lax.ppermute(block, axis, pairs + [(b, a) for a, b in pairs])


def gather_metrics(packed, cores, units):
    order = ring_order(units)
    forward = [
        (order[n] * cores + k, order[(n + 1) % units] * cores + k)
        for n in range(units)
        for k in range(cores)
    ]
    backward = [(b, a) for a, b in forward]
    turns = [packed] + [None] * (units - 1)
    up = down = packed
    for step in range(1, units // 2 + 1):
        up = lax.ppermute(up, "col", forward)
        turns[step] = up
        if units - step > units // 2:
            down = lax.ppermute(down, "col", backward)
            turns[units - step] = down
    buffers = []
    for turn in turns:
        buffers.append(turn)
        for side in range(1, cores):
            swap = [
                (u * cores + k, u * cores + (k + side) % cores)
                for u in range(units)
                for k in range(cores)
            ]
            buffers.append(lax.ppermute(turn, "col", swap))
    return buffers


def spread(own_pieces, sources):
    rows, columns = lax.axis_size("row"), len(sources)
    bits = rows.bit_length() - 1
    assert rows == 1 << bits
    held = [{0: own_pieces[p]} for p in range(bits)]
    reached = [{0: [0]} for p in range(bits)]
    routes, arrived = [], []
    for step in range(bits):
        for p in range(bits):
            bit = 1 << ((p + step) % bits)
            got, takers = [], []
            for since in sorted(held[p]):
                pairs = [
                    ((sources[c] ^ away) * columns + c, (sources[c] ^ away ^ bit) * columns + c)
                    for c in range(columns)
                    for away in reached[p][since]
                ]
                got.append(lax.ppermute(held[p][since], ("row", "col"), pairs))
                takers.append([away ^ bit for away in reached[p][since]])
            for block, who in zip(got, takers):
                routes.append((p, who))
                arrived.append(block)
                key = len(held[p])
                held[p][key] = block
                reached[p][key] = who
    return routes, arrived


def on_device(
    fitting,
    coefficients,
    amplitudes,
    intersections,
    virtual_energy,
    occupied_energy,
    kept_count,
    orbital_atoms,
    fock_partner,
    fock_value,
):
    row_count, column_count = amplitudes.shape[:2]
    held, aux, pao = fitting.shape
    domain = orbital_atoms.shape[1]
    npno = virtual_energy.shape[2]
    terms = intersections.shape[2]
    rows, columns = lax.axis_size("row"), lax.axis_size("col")
    cores = row_count // column_count
    units = columns // cores
    scale = (2 * domain * aux) ** (-0.5)
    depth = pao + EXTRA
    half = pao // 2

    packed = call(
        pack_kernel,
        jax.ShapeDtypeStruct((held, depth, half), BF16),
        [VMEM],
        VMEM,
        [],
        "pack_metric",
        2 * held * aux * pao * pao,
        fitting.size * 2,
    )(fitting)
    buffers = gather_metrics(packed, cores, units)

    blocks = [amplitudes] + [
        swapped(amplitudes, axis, first) for axis in ("row", "col") for first in (0, 1)
    ]
    chunks = npno // 2
    base, turned = call(
        couple_kernel,
        (
            jax.ShapeDtypeStruct((row_count, column_count, npno, npno), F32),
            jax.ShapeDtypeStruct((column_count, domain, row_count * npno, pao), BF16),
        ),
        [SMEM] * 3 + [VMEM] * (3 + len(blocks)),
        (VMEM, VMEM),
        [
            pltpu.VMEM((chunks, terms, 2 * npno), F32),
            pltpu.VMEM((npno, 2 * npno), F32),
            pltpu.VMEM((len(blocks) * row_count, column_count, npno, npno), BF16),
            pltpu.VMEM((terms, npno, npno), BF16),
        ],
        "couple",
        4 * row_count * column_count * terms * npno**3,
        intersections.size * 4 + coefficients.size,
    )(fock_partner.T, fock_value.T, occupied_energy, coefficients, intersections, virtual_energy, *blocks)

    bits = rows.bit_length() - 1
    wanted = column_count * domain
    pieces = [wanted * (p + 1) // bits - wanted * p // bits for p in range(bits)]
    own_pieces = call(
        functools.partial(select_kernel, cores, units, pieces),
        tuple(jax.ShapeDtypeStruct((n, depth, half), BF16) for n in pieces),
        [SMEM] + [VMEM] * len(buffers),
        (VMEM,) * bits,
        [pltpu.VMEM((len(buffers) * held, depth, half), BF16)],
        "select_column_atoms",
        0,
        wanted * depth * half * 4,
    )(orbital_atoms.T, *buffers)
    sources = [c * column_count // row_count for c in range(columns)]
    routes, arrived = spread(own_pieces, sources)

    base = call(
        functools.partial(row_kernel, cores, units, scale),
        jax.ShapeDtypeStruct(base.shape, F32),
        [SMEM] + [VMEM] * (2 + len(buffers)),
        VMEM,
        [
            pltpu.VMEM((len(buffers) * held, depth, half), BF16),
            pltpu.VMEM((pao, pao), BF16),
        ],
        "row_exchange",
        2 * row_count * column_count * domain * pao * npno * (pao + npno),
        coefficients.size,
    )(orbital_atoms.T, coefficients, base, *buffers)

    return call(
        functools.partial(column_kernel, routes, pieces, scale),
        jax.ShapeDtypeStruct(amplitudes.shape, F32),
        [SMEM] + [VMEM] * (3 + bits + len(arrived)),
        VMEM,
        [
            pltpu.VMEM((wanted, depth, half), BF16),
            pltpu.VMEM((pao, pao), BF16),
            pltpu.VMEM((npno, 2 * npno), F32),
            pltpu.VMEM((row_count, column_count, npno // 2, 2 * npno), F32),
        ],
        "column_exchange",
        2 * row_count * column_count * domain * pao * npno * (pao + npno),
        coefficients.size,
    )(kept_count.T, coefficients, turned, base, *own_pieces, *arrived)


def solution(mesh):
    placed = (
        P(("row", "col"), None, None),
        P("row", "col", None, None, None),
        P("row", "col", None),
        P("row", "col", None, None),
        P("row", "col", None),
        P(),
        P("row", "col"),
        P(),
        P(),
        P(),
    )
    return jax.shard_map(
        on_device, mesh=mesh, in_specs=placed, out_specs=P("row", "col", None), check_vma=False
    )
```

time: 141 us -> 63.5 us (0.45)
  the two profiles are of different devices: /device:TPU:0 before, /device:TPU:21 now
where the time goes in v1:
time: 63.5 us; the launch traced here: 62.9 us
  starting transfers between devices  26.5 us (42%)
  Pallas kernels  15.6 us (25%)
  waiting for transfers between devices  12.4 us (20%)
  local copies, waits for them, and re-layouts  8.21 us (13%)
    ppermute x6, starting transfers between devices, spread(): got.append(lax.ppermute(held[p][since], ('row', 'col'), pairs))  11.1 us
    unnamed x24, local copies, waits for them, and re-layouts  8.21 us
    pallas_call x1, Pallas kernels, on_device(): call(couple_kernel, (jax.ShapeDtypeStruct((row_count, column_count, npno,...  8 us
    ppermute x4, starting transfers between devices, swapped(): return lax.ppermute(block, axis, pairs + [(b, a) for a, b in pairs])  6.82 us
    ppermute x4, starting transfers between devices, gather_metrics(): buffers.append(lax.ppermute(turn, 'col', swap))  6.12 us
    ppermute x2, waiting for transfers between devices, gather_metrics(): up = lax.ppermute(up, 'col', forward)  6.03 us
    ppermute x4, waiting for transfers between devices, swapped(): return lax.ppermute(block, axis, pairs + [(b, a) for a, b in pairs])  5.34 us
    pallas_call x1, Pallas kernels, on_device(): call(functools.partial(row_kernel, cores, units, scale), jax.ShapeDtypeSt...  3.82 us
  transfers between devices with their start and end apart: 17, of which 6 were waited for; matrix products, arithmetic and copies ran while one was open for 0% of the time, Pallas kernels for 19%

profile of v1, /device:TPU:21, one launch (start us, length us, event | category | flops | bytes accessed | tf_op | source)
XLA Modules:
  0.0 62.9 jit_solution(10518061183570929166)
XLA Ops:
  0.0 1.0 %copy-done.3 = bf16[2,512,256]{2,1,0:T(8,128)(2,1)S(1)} copy-done((bf16[2,512,256]{2,1,0:T(8,128)(2,1)S(1)}, bf16[2,512,256]{2,1,0:T(8,128)(2,1)}, u32[]{:S(2)}) %copy-start.3) | copy-done | bytes 524312
  1.0 0.4 pack_metric.1.refs_0_
  1.4 0.1 collective-permute-start.5
  1.5 1.4 %collective-permute-start.9 = (bf16[2,272,128]{2,1,0:T(8,128)(2,1)S(1)}, bf16[2,272,128]{2,1,0:T(8,128)(2,1)S(1)}, u32[]{:S(2)}, u32[]{:S(2)}) collective-permute-start(bf16[2,272,128]{2,1,0:T(8,128)(2,1)S(1)} %pack_metric.1.refs_0_), channel_id=1, source_target_pairs={{2,0},{3,1},{6,2},{7,3},{4,6},{5,7},{0,4},{1,5},{10,8},{11,9},{14,... | collective-permute-start | bytes 417800 | tf_op jit(solution)/shard_map/ppermute | solution.py:294
  2.9 3.1 %collective-permute-done.5.refs_2_ = bf16[2,272,128]{2,1,0:T(8,128)(2,1)S(1)} collective-permute-done((bf16[2,272,128]{2,1,0:T(8,128)(2,1)S(1)}, bf16[2,272,128]{2,1,0:T(8,128)(2,1)S(1)}, u32[]{:S(2)}, u32[]{:S(2)}) %collective-permute-start.5) | collective-permute-done | bytes 139296 | tf_op jit(solution)/shard_map/ppermute | solution.py:291
  6.0 1.0 %collective-permute-start.7 = (bf16[2,272,128]{2,1,0:T(8,128)(2,1)S(1)}, bf16[2,272,128]{2,1,0:T(8,128)(2,1)S(1)}, u32[]{:S(2)}, u32[]{:S(2)}) collective-permute-start(bf16[2,272,128]{2,1,0:T(8,128)(2,1)S(1)} %collective-permute-done.5.refs_2_), channel_id=1, source_target_pairs={{0,2},{1,3},{2,6},{3,7},{6,4},{7,5},{4,0},{5,1},{8,10},{9,11},{10,... | collective-permute-start | bytes 417800 | tf_op jit(solution)/shard_map/ppermute | solution.py:291
  7.0 1.9 %collective-permute-start.4 = (bf16[2,272,128]{2,1,0:T(8,128)(2,1)S(1)}, bf16[2,272,128]{2,1,0:T(8,128)(2,1)S(1)}, u32[]{:S(2)}, u32[]{:S(2)}) collective-permute-start(bf16[2,272,128]{2,1,0:T(8,128)(2,1)S(1)} %pack_metric.1.refs_0_), channel_id=1, source_target_pairs={{0,1},{1,0},{2,3},{3,2},{4,5},{5,4},{6,7},{7,6},{8,9},{9,8},{10,11... | collective-permute-start | bytes 417800 | tf_op jit(solution)/shard_map/ppermute | solution.py:305
  8.9 0.0 collective-permute-start.6
  8.9 0.0 collective-permute-done.9.refs_6_
  8.9 1.8 %collective-permute-start.10 = (bf16[2,272,128]{2,1,0:T(8,128)(2,1)S(1)}, bf16[2,272,128]{2,1,0:T(8,128)(2,1)S(1)}, u32[]{:S(2)}, u32[]{:S(2)}) collective-permute-start(bf16[2,272,128]{2,1,0:T(8,128)(2,1)S(1)} %collective-permute-done.9.refs_6_), channel_id=1, source_target_pairs={{0,1},{1,0},{2,3},{3,2},{4,5},{5,4},{6,7},{7,6},{8,9},{9,8},{10,11... | collective-permute-start | bytes 417800 | tf_op jit(solution)/shard_map/ppermute | solution.py:305
  10.7 3.0 %collective-permute-done.7.refs_4_ = bf16[2,272,128]{2,1,0:T(8,128)(2,1)S(1)} collective-permute-done((bf16[2,272,128]{2,1,0:T(8,128)(2,1)S(1)}, bf16[2,272,128]{2,1,0:T(8,128)(2,1)S(1)}, u32[]{:S(2)}, u32[]{:S(2)}) %collective-permute-start.7) | collective-permute-done | bytes 139296 | tf_op jit(solution)/shard_map/ppermute | solution.py:291
  13.7 2.3 %collective-permute-start.8 = (bf16[2,272,128]{2,1,0:T(8,128)(2,1)S(1)}, bf16[2,272,128]{2,1,0:T(8,128)(2,1)S(1)}, u32[]{:S(2)}, u32[]{:S(2)}) collective-permute-start(bf16[2,272,128]{2,1,0:T(8,128)(2,1)S(1)} %collective-permute-done.7.refs_4_), channel_id=1, source_target_pairs={{0,1},{1,0},{2,3},{3,2},{4,5},{5,4},{6,7},{7,6},{8,9},{9,8},{10,11... | collective-permute-start | bytes 417800 | tf_op jit(solution)/shard_map/ppermute | solution.py:305
  16.0 0.0 collective-permute-done.4.refs_1_
  16.0 0.0 collective-permute-done.6.refs_3_
  16.1 0.0 collective-permute-done.10.refs_7_
  16.1 1.0 %collective-permute-done.8.refs_5_ = bf16[2,272,128]{2,1,0:T(8,128)(2,1)S(1)} collective-permute-done((bf16[2,272,128]{2,1,0:T(8,128)(2,1)S(1)}, bf16[2,272,128]{2,1,0:T(8,128)(2,1)S(1)}, u32[]{:S(2)}, u32[]{:S(2)}) %collective-permute-start.8) | collective-permute-done | bytes 139296 | tf_op jit(solution)/shard_map/ppermute | solution.py:305
  17.0 0.7 %copy-done.5 = s32[16,3]{0,1:T(4,128)S(1)} copy-done((s32[16,3]{0,1:T(4,128)S(1)}, s32[16,3]{0,1:T(4,128)}, u32[]{:S(2)}) %copy-start.5) | copy-done | bytes 216
  17.7 0.8 %select_column_atoms.1 = (bf16[3,272,128]{2,1,0:T(8,128)(2,1)S(1)}, bf16[3,272,128]{2,1,0:T(8,128)(2,1)S(1)}) custom-call(s32[3,16]{1,0:T(4,128)S(1)} %bitcast.4, bf16[2,272,128]{2,1,0:T(8,128)(2,1)S(1)} %pack_metric.1.refs_0_, bf16[2,272,128]{2,1,0:T(8,128)(2,1)S(1)} %collective-permute-done.4.refs_1_, ...), custom_call_target="tpu_custom_call" | custom-call | bytes 835584 | tf_op jit(solution)/shard_map/select_column_atoms/pallas_call | solution.py:399
  18.5 3.1 %collective-permute-start.11 = (bf16[3,272,128]{2,1,0:T(8,128)(2,1)S(1)}, bf16[3,272,128]{2,1,0:T(8,128)(2,1)S(1)}, u32[]{:S(2)}, u32[]{:S(2)}) collective-permute-start(bf16[3,272,128]{2,1,0:T(8,128)(2,1)S(1)} %get-tuple-element.11.refs_0_), channel_id=1, source_target_pairs={{0,8},{1,9},{10,2},{11,3},{20,28},{21,29},{30,22},{31,23}} | collective-permute-start | bytes 626696 | tf_op jit(solution)/shard_map/ppermute | solution.py:326
  21.7 1.3 %collective-permute-start.12 = (bf16[3,272,128]{2,1,0:T(8,128)(2,1)S(1)}, bf16[3,272,128]{2,1,0:T(8,128)(2,1)S(1)}, u32[]{:S(2)}, u32[]{:S(2)}) collective-permute-start(bf16[3,272,128]{2,1,0:T(8,128)(2,1)S(1)} %get-tuple-element.12.refs_1_), channel_id=1, source_target_pairs={{0,16},{1,17},{10,26},{11,27},{20,4},{21,5},{30,14},{31,15}} | collective-permute-start | bytes 626696 | tf_op jit(solution)/shard_map/ppermute | solution.py:326
  23.0 0.1 collective-permute-start
  23.1 1.9 %collective-permute-start.1 = (bf16[4,2,4096]{2,1,0:T(2,128)(2,1)}, bf16[4,2,4096]{2,1,0:T(2,128)(2,1)S(1)}, u32[]{:S(2)}, u32[]{:S(2)}) collective-permute-start(bf16[4,2,4096]{2,1,0:T(2,128)(2,1)} %refs_0_.1), channel_id=1, source_target_pairs={{8,16},{16,8},{9,17},{17,9},{10,18},{18,10},{11,19},{19,11},{12,20... | collective-permute-start | bytes 196616 | tf_op jit(solution)/shard_map/ppermute | solution.py:277
  25.0 1.3 %collective-permute-start.13 = (bf16[3,272,128]{2,1,0:T(8,128)(2,1)S(1)}, bf16[3,272,128]{2,1,0:T(8,128)(2,1)S(1)}, u32[]{:S(2)}, u32[]{:S(2)}) collective-permute-start(bf16[3,272,128]{2,1,0:T(8,128)(2,1)S(1)} %get-tuple-element.11.refs_0_), channel_id=1, source_target_pairs={{0,16},{1,17},{10,26},{11,27},{20,4},{21,5},{30,14},{31,15}} | collective-permute-start | bytes 626696 | tf_op jit(solution)/shard_map/ppermute | solution.py:326
  26.3 1.0 %collective-permute-done.refs_1_ = bf16[4,2,4096]{2,1,0:T(2,128)(2,1)S(1)} collective-permute-done((bf16[4,2,4096]{2,1,0:T(2,128)(2,1)}, bf16[4,2,4096]{2,1,0:T(2,128)(2,1)S(1)}, u32[]{:S(2)}, u32[]{:S(2)}) %collective-permute-start) | collective-permute-done | bytes 65568 | tf_op jit(solution)/shard_map/ppermute | solution.py:277
  27.3 4.0 %collective-permute-start.15 = (bf16[3,272,128]{2,1,0:T(8,128)(2,1)S(1)}, bf16[3,272,128]{2,1,0:T(8,128)(2,1)S(1)}, u32[]{:S(2)}, u32[]{:S(2)}) collective-permute-start(bf16[3,272,128]{2,1,0:T(8,128)(2,1)S(1)} %get-tuple-element.12.refs_1_), channel_id=1, source_target_pairs={{0,8},{1,9},{10,2},{11,3},{20,28},{21,29},{30,22},{31,23}} | collective-permute-start | bytes 626696 | tf_op jit(solution)/shard_map/ppermute | solution.py:326
  31.4 0.0 collective-permute-done.11.refs_2_
  31.4 0.7 %collective-permute-start.14 = (bf16[3,272,128]{2,1,0:T(8,128)(2,1)S(1)}, bf16[3,272,128]{2,1,0:T(8,128)(2,1)S(1)}, u32[]{:S(2)}, u32[]{:S(2)}) collective-permute-start(bf16[3,272,128]{2,1,0:T(8,128)(2,1)S(1)} %collective-permute-done.11.refs_2_), channel_id=1, source_target_pairs={{8,24},{9,25},{2,18},{3,19},{28,12},{29,13},{22,6},{23,7}} | collective-permute-start | bytes 626696 | tf_op jit(solution)/shard_map/ppermute | solution.py:326
  32.0 0.0 collective-permute-done.12.refs_3_
  32.1 0.7 %collective-permute-start.16 = (bf16[3,272,128]{2,1,0:T(8,128)(2,1)S(1)}, bf16[3,272,128]{2,1,0:T(8,128)(2,1)S(1)}, u32[]{:S(2)}, u32[]{:S(2)}) collective-permute-start(bf16[3,272,128]{2,1,0:T(8,128)(2,1)S(1)} %collective-permute-done.12.refs_3_), channel_id=1, source_target_pairs={{16,24},{17,25},{26,18},{27,19},{4,12},{5,13},{14,6},{15,7}} | collective-permute-start | bytes 626696 | tf_op jit(solution)/shard_map/ppermute | solution.py:326
  32.7 0.0 collective-permute-done.1.refs_2_
  32.7 2.2 %collective-permute-start.2 = (bf16[4,2,4096]{2,1,0:T(2,128)(2,1)}, bf16[4,2,4096]{2,1,0:T(2,128)(2,1)S(1)}, u32[]{:S(2)}, u32[]{:S(2)}) collective-permute-start(bf16[4,2,4096]{2,1,0:T(2,128)(2,1)} %refs_0_.1), channel_id=1, source_target_pairs={{0,1},{2,3},{4,5},{6,7},{1,0},{3,2},{5,4},{7,6},{8,9},{10,11},{12,... | collective-permute-start | bytes 196616 | tf_op jit(solution)/shard_map/ppermute | solution.py:277
  35.0 1.1 %collective-permute-done.2.refs_3_ = bf16[4,2,4096]{2,1,0:T(2,128)(2,1)S(1)} collective-permute-done((bf16[4,2,4096]{2,1,0:T(2,128)(2,1)}, bf16[4,2,4096]{2,1,0:T(2,128)(2,1)S(1)}, u32[]{:S(2)}, u32[]{:S(2)}) %collective-permute-start.2) | collective-permute-done | bytes 65568 | tf_op jit(solution)/shard_map/ppermute | solution.py:277
  36.1 2.6 %collective-permute-start.3 = (bf16[4,2,4096]{2,1,0:T(2,128)(2,1)}, bf16[4,2,4096]{2,1,0:T(2,128)(2,1)S(1)}, u32[]{:S(2)}, u32[]{:S(2)}) collective-permute-start(bf16[4,2,4096]{2,1,0:T(2,128)(2,1)} %refs_0_.1), channel_id=1, source_target_pairs={{1,2},{3,4},{5,6},{2,1},{4,3},{6,5},{9,10},{11,12},{13,14},{10,9},... | collective-permute-start | bytes 196616 | tf_op jit(solution)/shard_map/ppermute | solution.py:277
  38.7 3.2 %collective-permute-done.3.refs_4_ = bf16[4,2,4096]{2,1,0:T(2,128)(2,1)S(1)} collective-permute-done((bf16[4,2,4096]{2,1,0:T(2,128)(2,1)}, bf16[4,2,4096]{2,1,0:T(2,128)(2,1)S(1)}, u32[]{:S(2)}, u32[]{:S(2)}) %collective-permute-start.3) | collective-permute-done | bytes 65568 | tf_op jit(solution)/shard_map/ppermute | solution.py:277
  41.9 1.9 %copy-done = bf16[4,2,6,256,128]{4,3,2,1,0:T(8,128)(2,1)S(1)} copy-done((bf16[4,2,6,256,128]{4,3,2,1,0:T(8,128)(2,1)S(1)}, bf16[4,2,6,256,128]{4,3,2,1,0:T(8,128)(2,1)}, u32[]{:S(2)}) %copy-start) | copy-done | bytes 3145752
  43.8 1.0 %copy-done.2 = bf16[4,2,8,4096]{3,2,1,0:T(8,128)(2,1)S(1)} copy-done((bf16[4,2,8,4096]{3,2,1,0:T(8,128)(2,1)S(1)}, bf16[4,2,8,4096]{3,2,1,0:T(8,128)(2,1)}, u32[]{:S(2)}) %copy-start.2) | copy-done | bytes 524312
  44.8 0.8 %copy-done.4 = bf16[4,2,4096]{2,1,0:T(2,128)(2,1)S(1)} copy-done((bf16[4,2,4096]{2,1,0:T(2,128)(2,1)S(1)}, bf16[4,2,4096]{2,1,0:T(2,128)(2,1)}, u32[]{:S(2)}) %copy-start.4) | copy-done | bytes 65560
  45.7 0.7 %copy-done.7 = f32[4,2,64]{2,1,0:T(2,128)S(1)} copy-done((f32[4,2,64]{2,1,0:T(2,128)S(1)}, f32[4,2,64]{2,1,0:T(2,128)}, u32[]{:S(2)}) %copy-start.7) | copy-done | bytes 2072
  46.4 0.7 %copy-done.8 = s32[16,4]{0,1:T(4,128)S(1)} copy-done((s32[16,4]{0,1:T(4,128)S(1)}, s32[16,4]{0,1:T(4,128)}, u32[]{:S(2)}) %copy-start.8) | copy-done | bytes 280
  47.0 0.7 %copy-done.9 = f32[16,4]{0,1:T(4,128)S(1)} copy-done((f32[16,4]{0,1:T(4,128)S(1)}, f32[16,4]{0,1:T(4,128)}, u32[]{:S(2)}) %copy-start.9) | copy-done | bytes 280
  47.7 0.7 %copy-done.11 = f32[16]{0:T(128)S(1)} copy-done((f32[16]{0:T(128)S(1)}, f32[16]{0:T(128)}, u32[]{:S(2)}) %copy-start.11) | copy-done | bytes 88
  48.4 8.0 %couple.1 = (f32[4,2,64,64]{3,2,1,0:T(8,128)S(1)}, bf16[2,3,256,256]{3,2,1,0:T(8,128)(2,1)S(1)}) custom-call(s32[4,16]{1,0:T(4,128)S(1)} %bitcast.6, f32[4,16]{1,0:T(4,128)S(1)} %bitcast.7, f32[16]{0:T(128)S(1)} %copy-done.11, bf16[4,2,6,256,128]{4,3,2,1,0:T(8,128)(2,1)S(1)} %copy-done, bf16[4,2,8,4096]{3,2,1,0:T(8,128)(2,1)S(1)} %copy-done.2, ...), custom_call_target="tpu_custom_call" | custom-call | flops 67108864 | bytes 2621440 | tf_op jit(solution)/shard_map/couple/pallas_call | solution.py:377
  56.4 0.0 copy-start.10
  56.4 3.8 %row_exchange.1.base_ref = f32[4,2,64,64]{3,2,1,0:T(8,128)S(1)} custom-call(s32[3,16]{1,0:T(4,128)S(1)} %bitcast.5, bf16[4,2,6,256,128]{4,3,2,1,0:T(8,128)(2,1)S(1)} %copy-done.1, f32[4,2,64,64]{3,2,1,0:T(8,128)S(1)} %get-tuple-element.10.base_ref, bf16[2,272,128]{2,1,0:T(8,128)(2,1)S(1)} %pack_metric.1.refs_0_, ...), custom_call_target="tpu_custom_call" | custom-call | flops 251658240 | bytes 1572864 | tf_op jit(solution)/shard_map/row_exchange/pallas_call | solution.py:412
  60.2 0.0 collective-permute-done.13.refs_4_
  60.3 0.0 collective-permute-done.15.refs_6_
  60.3 0.0 collective-permute-done.14.refs_5_
  60.3 2.6 %column_exchange.1 = f32[4,2,4096]{2,1,0:T(2,128)} custom-call(s32[2,4]{1,0:T(2,128)S(1)} %bitcast.8, bf16[4,2,6,256,128]{4,3,2,1,0:T(8,128)(2,1)S(1)} %copy-done.1, bf16[2,3,256,256]{3,2,1,0:T(8,128)(2,1)S(1)} %get-tuple-element.9.turned_ref, f32[4,2,64,64]{3,2,1,0:T(8,128)S(1)} %row_exchange.1.base_ref, ...), custom_call_target="tpu_custom_call" | custom-call | flops 251658240 | bytes 1572864 | tf_op jit(solution)/shard_map/column_exchange/pallas_call | solution.py:426
  (15 shorter events, 0.0 us)
Async XLA Ops:
  0.0 1.0 %copy-start.3 = (bf16[2,512,256]{2,1,0:T(8,128)(2,1)S(1)}, bf16[2,512,256]{2,1,0:T(8,128)(2,1)}, u32[]{:S(2)}) copy-start(bf16[2,512,256]{2,1,0:T(8,128)(2,1)} %fit_ref.1) | copy-start | bytes 1572868
  1.0 55.4 %copy-start.6 = (s32[16,3]{0,1:T(4,128)S(1)}, s32[16,3]{0,1:T(4,128)}, u32[]{:S(2)}) copy-start(s32[16,3]{0,1:T(4,128)} %param.17) | copy-start | bytes 580
  1.4 4.6 %collective-permute-start.5 = (bf16[2,272,128]{2,1,0:T(8,128)(2,1)S(1)}, bf16[2,272,128]{2,1,0:T(8,128)(2,1)S(1)}, u32[]{:S(2)}, u32[]{:S(2)}) collective-permute-start(bf16[2,272,128]{2,1,0:T(8,128)(2,1)S(1)} %pack_metric.1.refs_0_), channel_id=1, source_target_pairs={{0,2},{1,3},{2,6},{3,7},{6,4},{7,5},{4,0},{5,1},{8,10},{9,11},{10,... | collective-permute-start | bytes 417800 | tf_op jit(solution)/shard_map/ppermute | solution.py:291
  1.5 7.4 %collective-permute-start.9 = (bf16[2,272,128]{2,1,0:T(8,128)(2,1)S(1)}, bf16[2,272,128]{2,1,0:T(8,128)(2,1)S(1)}, u32[]{:S(2)}, u32[]{:S(2)}) collective-permute-start(bf16[2,272,128]{2,1,0:T(8,128)(2,1)S(1)} %pack_metric.1.refs_0_), channel_id=1, source_target_pairs={{2,0},{3,1},{6,2},{7,3},{4,6},{5,7},{0,4},{1,5},{10,8},{11,9},{14,... | collective-permute-start | bytes 417800 | tf_op jit(solution)/shard_map/ppermute | solution.py:294
  6.0 7.7 %collective-permute-start.7 = (bf16[2,272,128]{2,1,0:T(8,128)(2,1)S(1)}, bf16[2,272,128]{2,1,0:T(8,128)(2,1)S(1)}, u32[]{:S(2)}, u32[]{:S(2)}) collective-permute-start(bf16[2,272,128]{2,1,0:T(8,128)(2,1)S(1)} %collective-permute-done.5.refs_2_), channel_id=1, source_target_pairs={{0,2},{1,3},{2,6},{3,7},{6,4},{7,5},{4,0},{5,1},{8,10},{9,11},{10,... | collective-permute-start | bytes 417800 | tf_op jit(solution)/shard_map/ppermute | solution.py:291
  7.0 9.1 %collective-permute-start.4 = (bf16[2,272,128]{2,1,0:T(8,128)(2,1)S(1)}, bf16[2,272,128]{2,1,0:T(8,128)(2,1)S(1)}, u32[]{:S(2)}, u32[]{:S(2)}) collective-permute-start(bf16[2,272,128]{2,1,0:T(8,128)(2,1)S(1)} %pack_metric.1.refs_0_), channel_id=1, source_target_pairs={{0,1},{1,0},{2,3},{3,2},{4,5},{5,4},{6,7},{7,6},{8,9},{9,8},{10,11... | collective-permute-start | bytes 417800 | tf_op jit(solution)/shard_map/ppermute | solution.py:305
  8.9 7.2 %collective-permute-start.6 = (bf16[2,272,128]{2,1,0:T(8,128)(2,1)S(1)}, bf16[2,272,128]{2,1,0:T(8,128)(2,1)S(1)}, u32[]{:S(2)}, u32[]{:S(2)}) collective-permute-start(bf16[2,272,128]{2,1,0:T(8,128)(2,1)S(1)} %collective-permute-done.5.refs_2_), channel_id=1, source_target_pairs={{0,1},{1,0},{2,3},{3,2},{4,5},{5,4},{6,7},{7,6},{8,9},{9,8},{10,11... | collective-permute-start | bytes 417800 | tf_op jit(solution)/shard_map/ppermute | solution.py:305
  8.9 7.2 %collective-permute-start.10 = (bf16[2,272,128]{2,1,0:T(8,128)(2,1)S(1)}, bf16[2,272,128]{2,1,0:T(8,128)(2,1)S(1)}, u32[]{:S(2)}, u32[]{:S(2)}) collective-permute-start(bf16[2,272,128]{2,1,0:T(8,128)(2,1)S(1)} %collective-permute-done.9.refs_6_), channel_id=1, source_target_pairs={{0,1},{1,0},{2,3},{3,2},{4,5},{5,4},{6,7},{7,6},{8,9},{9,8},{10,11... | collective-permute-start | bytes 417800 | tf_op jit(solution)/shard_map/ppermute | solution.py:305
  13.7 3.3 %collective-permute-start.8 = (bf16[2,272,128]{2,1,0:T(8,128)(2,1)S(1)}, bf16[2,272,128]{2,1,0:T(8,128)(2,1)S(1)}, u32[]{:S(2)}, u32[]{:S(2)}) collective-permute-start(bf16[2,272,128]{2,1,0:T(8,128)(2,1)S(1)} %collective-permute-done.7.refs_4_), channel_id=1, source_target_pairs={{0,1},{1,0},{2,3},{3,2},{4,5},{5,4},{6,7},{7,6},{8,9},{9,8},{10,11... | collective-permute-start | bytes 417800 | tf_op jit(solution)/shard_map/ppermute | solution.py:305
  17.0 0.7 %copy-start.5 = (s32[16,3]{0,1:T(4,128)S(1)}, s32[16,3]{0,1:T(4,128)}, u32[]{:S(2)}) copy-start(s32[16,3]{0,1:T(4,128)} %param.17) | copy-start | bytes 580
  18.5 12.8 %collective-permute-start.11 = (bf16[3,272,128]{2,1,0:T(8,128)(2,1)S(1)}, bf16[3,272,128]{2,1,0:T(8,128)(2,1)S(1)}, u32[]{:S(2)}, u32[]{:S(2)}) collective-permute-start(bf16[3,272,128]{2,1,0:T(8,128)(2,1)S(1)} %get-tuple-element.11.refs_0_), channel_id=1, source_target_pairs={{0,8},{1,9},{10,2},{11,3},{20,28},{21,29},{30,22},{31,23}} | collective-permute-start | bytes 626696 | tf_op jit(solution)/shard_map/ppermute | solution.py:326
  21.7 10.4 %collective-permute-start.12 = (bf16[3,272,128]{2,1,0:T(8,128)(2,1)S(1)}, bf16[3,272,128]{2,1,0:T(8,128)(2,1)S(1)}, u32[]{:S(2)}, u32[]{:S(2)}) collective-permute-start(bf16[3,272,128]{2,1,0:T(8,128)(2,1)S(1)} %get-tuple-element.12.refs_1_), channel_id=1, source_target_pairs={{0,16},{1,17},{10,26},{11,27},{20,4},{21,5},{30,14},{31,15}} | collective-permute-start | bytes 626696 | tf_op jit(solution)/shard_map/ppermute | solution.py:326
  23.0 4.4 %collective-permute-start = (bf16[4,2,4096]{2,1,0:T(2,128)(2,1)}, bf16[4,2,4096]{2,1,0:T(2,128)(2,1)S(1)}, u32[]{:S(2)}, u32[]{:S(2)}) collective-permute-start(bf16[4,2,4096]{2,1,0:T(2,128)(2,1)} %refs_0_.1), channel_id=1, source_target_pairs={{0,8},{16,24},{8,0},{24,16},{1,9},{17,25},{9,1},{25,17},{2,10},{18... | collective-permute-start | bytes 196616 | tf_op jit(solution)/shard_map/ppermute | solution.py:277
  23.1 9.7 %collective-permute-start.1 = (bf16[4,2,4096]{2,1,0:T(2,128)(2,1)}, bf16[4,2,4096]{2,1,0:T(2,128)(2,1)S(1)}, u32[]{:S(2)}, u32[]{:S(2)}) collective-permute-start(bf16[4,2,4096]{2,1,0:T(2,128)(2,1)} %refs_0_.1), channel_id=1, source_target_pairs={{8,16},{16,8},{9,17},{17,9},{10,18},{18,10},{11,19},{19,11},{12,20... | collective-permute-start | bytes 196616 | tf_op jit(solution)/shard_map/ppermute | solution.py:277
  25.0 35.2 %collective-permute-start.13 = (bf16[3,272,128]{2,1,0:T(8,128)(2,1)S(1)}, bf16[3,272,128]{2,1,0:T(8,128)(2,1)S(1)}, u32[]{:S(2)}, u32[]{:S(2)}) collective-permute-start(bf16[3,272,128]{2,1,0:T(8,128)(2,1)S(1)} %get-tuple-element.11.refs_0_), channel_id=1, source_target_pairs={{0,16},{1,17},{10,26},{11,27},{20,4},{21,5},{30,14},{31,15}} | collective-permute-start | bytes 626696 | tf_op jit(solution)/shard_map/ppermute | solution.py:326
  27.3 32.9 %collective-permute-start.15 = (bf16[3,272,128]{2,1,0:T(8,128)(2,1)S(1)}, bf16[3,272,128]{2,1,0:T(8,128)(2,1)S(1)}, u32[]{:S(2)}, u32[]{:S(2)}) collective-permute-start(bf16[3,272,128]{2,1,0:T(8,128)(2,1)S(1)} %get-tuple-element.12.refs_1_), channel_id=1, source_target_pairs={{0,8},{1,9},{10,2},{11,3},{20,28},{21,29},{30,22},{31,23}} | collective-permute-start | bytes 626696 | tf_op jit(solution)/shard_map/ppermute | solution.py:326
  31.4 28.9 %collective-permute-start.14 = (bf16[3,272,128]{2,1,0:T(8,128)(2,1)S(1)}, bf16[3,272,128]{2,1,0:T(8,128)(2,1)S(1)}, u32[]{:S(2)}, u32[]{:S(2)}) collective-permute-start(bf16[3,272,128]{2,1,0:T(8,128)(2,1)S(1)} %collective-permute-done.11.refs_2_), channel_id=1, source_target_pairs={{8,24},{9,25},{2,18},{3,19},{28,12},{29,13},{22,6},{23,7}} | collective-permute-start | bytes 626696 | tf_op jit(solution)/shard_map/ppermute | solution.py:326
  32.1 28.2 %collective-permute-start.16 = (bf16[3,272,128]{2,1,0:T(8,128)(2,1)S(1)}, bf16[3,272,128]{2,1,0:T(8,128)(2,1)S(1)}, u32[]{:S(2)}, u32[]{:S(2)}) collective-permute-start(bf16[3,272,128]{2,1,0:T(8,128)(2,1)S(1)} %collective-permute-done.12.refs_3_), channel_id=1, source_target_pairs={{16,24},{17,25},{26,18},{27,19},{4,12},{5,13},{14,6},{15,7}} | collective-permute-start | bytes 626696 | tf_op jit(solution)/shard_map/ppermute | solution.py:326
  32.7 3.4 %collective-permute-start.2 = (bf16[4,2,4096]{2,1,0:T(2,128)(2,1)}, bf16[4,2,4096]{2,1,0:T(2,128)(2,1)S(1)}, u32[]{:S(2)}, u32[]{:S(2)}) collective-permute-start(bf16[4,2,4096]{2,1,0:T(2,128)(2,1)} %refs_0_.1), channel_id=1, source_target_pairs={{0,1},{2,3},{4,5},{6,7},{1,0},{3,2},{5,4},{7,6},{8,9},{10,11},{12,... | collective-permute-start | bytes 196616 | tf_op jit(solution)/shard_map/ppermute | solution.py:277
  36.1 5.8 %collective-permute-start.3 = (bf16[4,2,4096]{2,1,0:T(2,128)(2,1)}, bf16[4,2,4096]{2,1,0:T(2,128)(2,1)S(1)}, u32[]{:S(2)}, u32[]{:S(2)}) collective-permute-start(bf16[4,2,4096]{2,1,0:T(2,128)(2,1)} %refs_0_.1), channel_id=1, source_target_pairs={{1,2},{3,4},{5,6},{2,1},{4,3},{6,5},{9,10},{11,12},{13,14},{10,9},... | collective-permute-start | bytes 196616 | tf_op jit(solution)/shard_map/ppermute | solution.py:277
  41.9 1.9 %copy-start = (bf16[4,2,6,256,128]{4,3,2,1,0:T(8,128)(2,1)S(1)}, bf16[4,2,6,256,128]{4,3,2,1,0:T(8,128)(2,1)}, u32[]{:S(2)}) copy-start(bf16[4,2,6,256,128]{4,3,2,1,0:T(8,128)(2,1)} %coef_ref.5) | copy-start | bytes 9437188
  43.8 1.0 %copy-start.2 = (bf16[4,2,8,4096]{3,2,1,0:T(8,128)(2,1)S(1)}, bf16[4,2,8,4096]{3,2,1,0:T(8,128)(2,1)}, u32[]{:S(2)}) copy-start(bf16[4,2,8,4096]{3,2,1,0:T(8,128)(2,1)} %inter_ref.1) | copy-start | bytes 1572868
  44.8 0.8 %copy-start.4 = (bf16[4,2,4096]{2,1,0:T(2,128)(2,1)S(1)}, bf16[4,2,4096]{2,1,0:T(2,128)(2,1)}, u32[]{:S(2)}) copy-start(bf16[4,2,4096]{2,1,0:T(2,128)(2,1)} %refs_0_.1) | copy-start | bytes 196612
  45.7 0.7 %copy-start.7 = (f32[4,2,64]{2,1,0:T(2,128)S(1)}, f32[4,2,64]{2,1,0:T(2,128)}, u32[]{:S(2)}) copy-start(f32[4,2,64]{2,1,0:T(2,128)} %virtual_ref.1) | copy-start | bytes 6148
  46.4 0.7 %copy-start.8 = (s32[16,4]{0,1:T(4,128)S(1)}, s32[16,4]{0,1:T(4,128)}, u32[]{:S(2)}) copy-start(s32[16,4]{0,1:T(4,128)} %param.18) | copy-start | bytes 772
  47.0 0.7 %copy-start.9 = (f32[16,4]{0,1:T(4,128)S(1)}, f32[16,4]{0,1:T(4,128)}, u32[]{:S(2)}) copy-start(f32[16,4]{0,1:T(4,128)} %param.19) | copy-start | bytes 772
  47.7 0.7 %copy-start.11 = (f32[16]{0:T(128)S(1)}, f32[16]{0:T(128)}, u32[]{:S(2)}) copy-start(f32[16]{0:T(128)} %occupied_ref.1) | copy-start | bytes 196
  48.4 8.0 %copy-start.1 = (bf16[4,2,6,256,128]{4,3,2,1,0:T(8,128)(2,1)S(1)}, bf16[4,2,6,256,128]{4,3,2,1,0:T(8,128)(2,1)}, u32[]{:S(2)}) copy-start(bf16[4,2,6,256,128]{4,3,2,1,0:T(8,128)(2,1)} %coef_ref.5) | copy-start | bytes 9437188
  56.4 3.9 %copy-start.10 = (s32[4,2]{0,1:T(2,128)S(1)}, s32[4,2]{0,1:T(2,128)}, u32[]{:S(2)}) copy-start(s32[4,2]{0,1:T(2,128)} %param.16) | copy-start | bytes 100

commit v2 on v1

v2 whole, which is shorter than its diff:
```python
import functools

import jax
import jax.numpy as jnp
from jax import lax
from jax.experimental import pallas as pl
from jax.experimental.pallas import tpu as pltpu
from jax.sharding import PartitionSpec as P

F32 = jnp.float32
BF16 = jnp.bfloat16
EXTRA = 16
VMEM = pl.BlockSpec(memory_space=pltpu.VMEM)
SMEM = pl.BlockSpec(memory_space=pltpu.SMEM)
HBM = pl.BlockSpec(memory_space=pltpu.HBM)
ANY = pl.BlockSpec(memory_space=pl.ANY)


def dot(a, b):
    return jnp.dot(a, b, preferred_element_type=F32)


def dot_nt(a, b):
    return lax.dot_general(a, b, (((1,), (1,)), ((), ())), preferred_element_type=F32)


def square_iota(n):
    return (
        lax.broadcasted_iota(jnp.int32, (n, n), 0),
        lax.broadcasted_iota(jnp.int32, (n, n), 1),
    )


def pack_kernel(
    atoms_ref, block_hbm, fit_ref, out_ref, table_ref, lines_ref,
    fits_ref, block_ref, flat_ref, sems, table_sem, block_sem,
):
    held = fit_ref.shape[0]
    half = fit_ref.shape[2] // 2
    row, col = square_iota(half)
    place = lax.broadcasted_iota(jnp.int32, (EXTRA, half), 0)
    fetches = [
        pltpu.make_async_copy(fit_ref.at[atom], fits_ref.at[atom], sems.at[atom])
        for atom in range(held)
    ]
    block = pltpu.make_async_copy(block_hbm, block_ref, block_sem)
    block.start()
    for fetch in fetches:
        fetch.start()
    table = pltpu.make_async_copy(atoms_ref, table_ref, table_sem)
    table.start()
    block.wait()
    row_count, column_count, chunks, lanes = lines_ref.shape
    for i in range(row_count):
        for q in range(chunks):
            flat_ref[i, q] = block_ref[i, :, q * lanes : (q + 1) * lanes].astype(F32)
    for i in range(row_count):
        for j in range(column_count):
            lines_ref[i, j] = flat_ref[i, :, j, :].astype(BF16)
    for atom in range(held):
        fetches[atom].wait()
        fit = fits_ref[atom]
        metric = lax.dot_general(fit, fit, (((0,), (0,)), ((), ())), preferred_element_type=F32)
        first, second = metric[:half, :half], metric[half:, half:]
        out_ref[atom, :half] = metric[:half, half:].astype(BF16)
        out_ref[atom, half : 2 * half] = jnp.where(row <= col, first, second).astype(BF16)
        lines = [jnp.sum(jnp.where(row == col, m, 0.0), axis=0, keepdims=True) for m in (first, second)]
        high = [line.astype(BF16).astype(F32) for line in lines]
        extra = jnp.where(
            place == 0,
            high[1],
            jnp.where(
                place == 1,
                lines[0] - high[0],
                jnp.where(place == 2, lines[1] - high[1], 0.0),
            ),
        )
        out_ref[atom, 2 * half :] = extra.astype(BF16)
    table.wait()


def unpack(packed, metric_ref):
    half = packed.shape[1]
    row, col = square_iota(half)
    corner = packed[:half]
    both = packed[half : 2 * half].astype(F32)
    extra = packed[2 * half :].astype(F32)
    turned = both.T
    metric_ref[:half, :half] = jnp.where(row <= col, both, turned).astype(BF16)
    metric_ref[:half, half:] = corner
    metric_ref[half:, :half] = corner.astype(F32).T.astype(BF16)
    metric_ref[half:, half:] = jnp.where(
        row > col, both, jnp.where(row == col, extra[0:1], turned)
    ).astype(BF16)
    return jnp.concatenate([extra[1:2], extra[2:3]], axis=1)


def ring_order(units):
    return [0] + list(range(1, units, 2)) + list(range(units - units % 2 - (0 if units % 2 else 2), 0, -2))


def ring_place(unit, units):
    return jnp.where(unit % 2 == 1, (unit + 1) // 2, (units - unit // 2) % units)


def pick_place(atom, row_place, col_place, cores, units, held):
    label = jnp.clip(atom - row_place * (units * cores * held), 0, units * cores * held - 1)
    owner, slot = label // held, label % held
    turn = (ring_place(col_place // cores, units) - ring_place(owner // cores, units) + units) % units
    side = (col_place % cores - owner % cores + cores) % cores
    return (turn * cores + side) * held + slot


def select_kernel(cores, units, pieces, atoms_ref, *refs):
    count = units * cores
    buffers, outs, all_ref = refs[:count], refs[count:-1], refs[-1]
    held = buffers[0].shape[0]
    row_place, col_place = lax.axis_index("row"), lax.axis_index("col")
    domain = atoms_ref.shape[0]
    columns = sum(pieces) // domain
    for index, buffer in enumerate(buffers):
        all_ref[index * held : (index + 1) * held] = buffer[...]
    targets = [(out, n) for out in outs for n in range(out.shape[0])]
    for index, (out, n) in enumerate(targets):
        atom = atoms_ref[index % domain, col_place * columns + index // domain]
        place = pick_place(atom, row_place, col_place, cores, units, held)
        out[n] = all_ref[place]


def pass_kernel(block_ref, *refs):
    refs[-1][...] = block_ref[...]


def neighbour_place(place, turn):
    return jnp.where(turn == 0, 0, jnp.where((place + turn) == jnp.bitwise_xor(place, 1), 1, 2))


def couple_kernel(partner_hbm, value_hbm, occupied_hbm, virtual_hbm, coef_hbm, inter_hbm, *refs):
    blocks = refs[:5]
    base_ref, row_turned_ref, turned_ref, coef_ref = refs[5:9]
    flat_ref, wide_ref, mats_ref, inters_ref, own_ref, inter_ref = refs[9:15]
    partner_ref, value_ref, occupied_ref, virtual_ref, sems, inter_sems, own_sems, coef_sems = refs[15:]
    row_count, column_count, terms, size = inter_ref.shape
    npno = base_ref.shape[2]
    lanes = 2 * npno
    chunks = size // lanes
    domain = coef_ref.shape[2]
    partners = terms // 2
    row_place, col_place = lax.axis_index("row"), lax.axis_index("col")
    first_row = row_place * row_count
    first_col = col_place * column_count
    fetches = [
        pltpu.make_async_copy(source, target, sems.at[n])
        for n, (source, target) in enumerate(
            [
                (partner_hbm, partner_ref),
                (value_hbm, value_ref),
                (occupied_hbm, occupied_ref),
                (virtual_hbm, virtual_ref),
            ]
        )
    ]

    def fetch_inter(i):
        return pltpu.make_async_copy(inter_hbm.at[i], inter_ref.at[i], inter_sems.at[i])

    def fetch_own(i):
        return pltpu.make_async_copy(
            coef_hbm.at[i, :, pl.ds(0, domain)], own_ref.at[i], own_sems.at[i]
        )

    def fetch_coef(i):
        return pltpu.make_async_copy(
            coef_hbm.at[i, :, pl.ds(domain, domain)], coef_ref.at[i], coef_sems.at[i]
        )

    for fetch in fetches:
        fetch.start()
    for i in range(row_count):
        fetch_inter(i).start()
    for i in range(row_count):
        fetch_own(i).start()
        fetch_coef(i).start()

    def square(lines):
        wide_ref[pl.ds(0, chunks, 2), :] = lines
        wide_ref[pl.ds(1, chunks, 2), :] = pltpu.roll(lines, npno, 1)
        return wide_ref[:, :npno]

    for index, block in enumerate(blocks):

        def one_block(i, carry, index=index, block=block):
            for j in range(column_count):
                mats_ref[index * row_count + i, j] = square(block[i, j].astype(F32)).astype(BF16)
            return carry

        lax.fori_loop(0, row_count, one_block, 0)
    for fetch in fetches:
        fetch.wait()

    def one_row(i, carry):
        fetch_inter(i).wait()
        fetch_own(i).wait()
        fetch_coef(i).wait()
        for j in range(column_count):
            for q in range(chunks):
                flat_ref[q] = inter_ref[i, j, :, q * lanes : (q + 1) * lanes].astype(F32)
            turned = []
            for n in range(terms):
                inter = square(flat_ref[:, n, :])
                inters_ref[n] = inter.astype(BF16)
                turned.append(inter.T.astype(BF16))
            total = jnp.zeros((npno, npno), F32)
            for n in range(terms):
                if n < partners:
                    away = partner_ref[n, first_row + i] - first_row + row_count
                    turn = away // row_count - 1
                    index = neighbour_place(row_place, turn) * row_count + away % row_count
                    weight = value_ref[n, first_row + i]
                    partner = mats_ref[index, j]
                else:
                    away = partner_ref[n - partners, first_col + j] - first_col + column_count
                    turn = away // column_count - 1
                    index = neighbour_place(col_place, turn)
                    index = jnp.where(index == 0, 0, index + 2) * row_count + i
                    weight = value_ref[n - partners, first_col + j]
                    partner = mats_ref[index, away % column_count]
                half = dot(inters_ref[n], partner).astype(BF16)
                total = total + weight * dot(half, turned[n])
            levels = jnp.broadcast_to(virtual_ref[i, pl.ds(j, 1)], (npno, npno))
            shift = levels + levels.T - occupied_ref[first_row + i] - occupied_ref[first_col + j]
            base_ref[i, j] = shift * mats_ref[i, j].astype(F32) - total
            for s in range(domain):
                row_turned_ref[i, s, j * npno : (j + 1) * npno] = own_ref[i, j, s].T[:npno]
                turned_ref[j, s, pl.ds(pl.multiple_of(i * npno, npno), npno)] = coef_ref[i, j, s].T[:npno]
        return carry

    lax.fori_loop(0, row_count, one_row, 0)


def row_kernel(cores, units, held, scale, atoms_ref, coef_hbm, turned_ref, base_ref, all_ref, *refs):
    out_ref, coef_ref, metric_ref, coef_sems = refs
    row_count, column_count, domain = coef_ref.shape[:3]
    npno = base_ref.shape[2]
    row_place, col_place = lax.axis_index("row"), lax.axis_index("col")

    def fetch(i):
        return pltpu.make_async_copy(
            coef_hbm.at[i, :, pl.ds(0, domain)], coef_ref.at[i], coef_sems.at[i]
        )

    for i in range(row_count):
        fetch(i).start()

    def one_row(i, carry):
        lows = []
        for s in range(domain):
            atom = atoms_ref[s, row_place * row_count + i]
            place = pick_place(atom, row_place, col_place, cores, units, held)
            lows.append(unpack(all_ref[place], metric_ref.at[s]))
        products = []
        for s in range(domain):
            left = turned_ref[i, s]
            product = dot(left, metric_ref[s]) + left.astype(F32) * lows[s]
            products.append(product.astype(BF16))
        fetch(i).wait()
        for j in range(column_count):
            total = dot(products[0][j * npno : (j + 1) * npno], coef_ref[i, j, 0])
            for s in range(1, domain):
                total = total + dot(products[s][j * npno : (j + 1) * npno], coef_ref[i, j, s])
            out_ref[i, j] = base_ref[i, j] + total[:, npno:] * scale
        return carry

    lax.fori_loop(0, row_count, one_row, 0)


def rows_away(column_count, row_count):
    source = lax.axis_index("col") * column_count // row_count
    return jnp.bitwise_xor(lax.axis_index("row"), source)


def merge_into(away, takers, kept, got, target):
    taken = functools.reduce(jnp.logical_or, [away == taker for taker in takers])

    @pl.when(taken)
    def _():
        target[...] = got[...]

    @pl.when(jnp.logical_not(taken))
    def _():
        target[...] = kept[...]


def merge_kernel(takers, column_count, row_count, *refs):
    count = len(takers)
    away = rows_away(column_count, row_count)
    for p in range(count):
        merge_into(away, takers[p], refs[p], refs[count + p], refs[2 * count + 1 + p])


def column_kernel(takers, scale, kept_hbm, coef_ref, turned_ref, base_ref, *refs):
    count = len(takers)
    out_ref, packed_ref, metric_ref, wide_ref, flat_ref, kept_ref, kept_sem = refs[2 * count :]
    row_count, column_count, domain = coef_ref.shape[:3]
    npno = base_ref.shape[2]
    lanes = 2 * npno
    kept_copy = pltpu.make_async_copy(kept_hbm, kept_ref, kept_sem)
    kept_copy.start()
    away = rows_away(column_count, row_count)
    start = 0
    for p in range(count):
        size = refs[p].shape[0]
        merge_into(away, takers[p], refs[p], refs[count + p], packed_ref.at[pl.ds(start, size)])
        start += size
    slots = column_count * domain
    lows = [unpack(packed_ref[index], metric_ref.at[index]) for index in range(slots)]
    products = []
    for index in range(slots):
        left = turned_ref[index // domain, index % domain]
        product = dot(left, metric_ref[index]) + left.astype(F32) * lows[index]
        products.append(product.astype(BF16))
    kept_copy.wait()
    row, col = square_iota(npno)
    lane = lax.broadcasted_iota(jnp.int32, (npno // 2, lanes), 1)
    for j in range(column_count):
        for i in range(row_count):
            total = None
            for s in range(domain):
                part = dot(products[j * domain + s][i * npno : (i + 1) * npno], coef_ref[i, j, s])
                total = part if total is None else total + part
            result = base_ref[i, j] + total[:, npno:] * scale
            kept = kept_ref[j, i]
            result = jnp.where((row < kept) & (col < kept), result, 0.0)
            wide_ref[i, j, :, :npno] = result
            even = wide_ref[i, j, pl.ds(0, npno // 2, 2), :]
            odd = wide_ref[i, j, pl.ds(1, npno // 2, 2), :]
            flat_ref[i, j] = jnp.where(lane < npno, even, pltpu.roll(odd, npno, 1))
    for i in range(row_count):
        for q in range(npno // 2):
            out_ref[i, :, q * lanes : (q + 1) * lanes] = flat_ref[i, :, q, :]


def call(kernel, out_shape, in_specs, out_specs, scratch, name, flops, moved):
    return pl.pallas_call(
        kernel,
        out_shape=out_shape,
        in_specs=in_specs,
        out_specs=out_specs,
        scratch_shapes=scratch,
        compiler_params=pltpu.CompilerParams(vmem_limit_bytes=48 * 2**20),
        cost_estimate=pl.CostEstimate(flops=flops, bytes_accessed=moved, transcendentals=0),
        name=name,
    )


def swapped(block, axis, first):
    size = lax.axis_size(axis)
    pairs = [(n, n + 1) for n in range(first, size - 1, 2)]
    return lax.ppermute(block, axis, pairs + [(b, a) for a, b in pairs])


def gather_metrics(packed, cores, units, first):
    order = ring_order(units)
    forward = [
        (order[n] * cores + k, order[(n + 1) % units] * cores + k)
        for n in range(units)
        for k in range(cores)
    ]
    backward = [(b, a) for a, b in forward]
    turns = [packed] + [None] * (units - 1)
    up = down = packed
    for step in range(1, units // 2 + 1):
        if step == 2:
            up = call(
                pass_kernel,
                jax.ShapeDtypeStruct(up.shape, up.dtype),
                [VMEM] + [ANY] * len(first),
                VMEM,
                [],
                "after_neighbours",
                0,
                0,
            )(up, *first)
        up = lax.ppermute(up, "col", forward)
        turns[step] = up
        if units - step > units // 2:
            down = lax.ppermute(down, "col", backward)
            turns[units - step] = down
    buffers = []
    for turn in turns:
        buffers.append(turn)
        for side in range(1, cores):
            swap = [
                (u * cores + k, u * cores + (k + side) % cores)
                for u in range(units)
                for k in range(cores)
            ]
            buffers.append(lax.ppermute(turn, "col", swap))
    return buffers


def spread(pieces, sources, column_count, row_count, first):
    rows, columns = lax.axis_size("row"), len(sources)
    bits = len(pieces)
    reached = [[0] for _ in pieces]
    for step in range(bits):
        got, takers = [], []
        for p in range(bits):
            bit = 1 << ((p + step) % bits)
            pairs = [
                ((sources[c] ^ away) * columns + c, (sources[c] ^ away ^ bit) * columns + c)
                for c in range(columns)
                for away in reached[p]
            ]
            got.append(lax.ppermute(pieces[p], ("row", "col"), pairs))
            takers.append([away ^ bit for away in reached[p]])
            reached[p] = reached[p] + takers[p]
        if step < bits - 1:
            pieces = call(
                functools.partial(merge_kernel, takers, column_count, row_count),
                tuple(jax.ShapeDtypeStruct(piece.shape, piece.dtype) for piece in pieces),
                [VMEM] * (2 * bits) + [ANY],
                (VMEM,) * bits,
                [],
                "merge",
                0,
                0,
            )(*pieces, *got, first)
    return list(pieces) + got, takers


def on_device(
    fitting,
    coefficients,
    amplitudes,
    intersections,
    virtual_energy,
    occupied_energy,
    kept_count,
    orbital_atoms,
    fock_partner,
    fock_value,
):
    row_count, column_count = amplitudes.shape[:2]
    held, aux, pao = fitting.shape
    domain = orbital_atoms.shape[1]
    npno = virtual_energy.shape[2]
    terms = intersections.shape[2]
    rows, columns = lax.axis_size("row"), lax.axis_size("col")
    cores = row_count // column_count
    units = columns // cores
    scale = (2 * domain * aux) ** (-0.5)
    depth = pao + EXTRA
    half = pao // 2

    chunks = npno // 2
    lanes = 2 * npno
    atoms_table, fit, own_block, partner, value, occupied, virtual, coefs, inter, kept = [
        pltpu.with_memory_space_constraint(array, pltpu.HBM)
        for array in (
            orbital_atoms.T,
            fitting,
            amplitudes,
            fock_partner.T,
            fock_value.T,
            occupied_energy,
            virtual_energy,
            coefficients,
            intersections,
            kept_count.T,
        )
    ]
    packed, table, lines = call(
        pack_kernel,
        (
            jax.ShapeDtypeStruct((held, depth, half), BF16),
            jax.ShapeDtypeStruct(atoms_table.shape, jnp.int32),
            jax.ShapeDtypeStruct((row_count, column_count, chunks, lanes), BF16),
        ),
        [HBM] * 3,
        (VMEM,) * 3,
        [
            pltpu.VMEM(fitting.shape, BF16),
            pltpu.VMEM(amplitudes.shape, BF16),
            pltpu.VMEM((row_count, chunks, column_count, lanes), F32),
            pltpu.SemaphoreType.DMA((held,)),
            pltpu.SemaphoreType.DMA(()),
            pltpu.SemaphoreType.DMA(()),
        ],
        "pack_metric",
        2 * held * aux * pao * pao,
        fitting.size * 2,
    )(atoms_table, own_block, fit)
    halos = [swapped(lines, axis, first) for axis in ("row", "col") for first in (0, 1)]
    buffers = gather_metrics(packed, cores, units, halos)
    blocks = [lines] + halos
    shape = (row_count, column_count, domain, pao, lanes)
    base, row_turned, turned, column_coefficients = call(
        couple_kernel,
        (
            jax.ShapeDtypeStruct((row_count, column_count, npno, npno), F32),
            jax.ShapeDtypeStruct((row_count, domain, column_count * npno, pao), BF16),
            jax.ShapeDtypeStruct((column_count, domain, row_count * npno, pao), BF16),
            jax.ShapeDtypeStruct(shape, BF16),
        ),
        [HBM] * 6 + [VMEM] * len(blocks),
        (VMEM,) * 4,
        [
            pltpu.VMEM((chunks, terms, lanes), F32),
            pltpu.VMEM((npno, lanes), F32),
            pltpu.VMEM((len(blocks) * row_count, column_count, npno, npno), BF16),
            pltpu.VMEM((terms, npno, npno), BF16),
            pltpu.VMEM(shape, BF16),
            pltpu.VMEM(intersections.shape, BF16),
            pltpu.SMEM(fock_partner.shape[::-1], jnp.int32),
            pltpu.SMEM(fock_value.shape[::-1], F32),
            pltpu.SMEM(occupied_energy.shape, F32),
            pltpu.VMEM(virtual_energy.shape, F32),
            pltpu.SemaphoreType.DMA((4,)),
            pltpu.SemaphoreType.DMA((row_count,)),
            pltpu.SemaphoreType.DMA((row_count,)),
            pltpu.SemaphoreType.DMA((row_count,)),
        ],
        "couple",
        4 * row_count * column_count * terms * npno**3,
        intersections.size * 4 + coefficients.size,
    )(partner, value, occupied, virtual, coefs, inter, *blocks)

    bits = rows.bit_length() - 1
    assert rows == 1 << bits
    wanted = column_count * domain
    sizes = [wanted * (p + 1) // bits - wanted * p // bits for p in range(bits)]
    atoms = len(buffers) * held
    *pieces, metrics = call(
        functools.partial(select_kernel, cores, units, sizes),
        tuple(jax.ShapeDtypeStruct((n, depth, half), BF16) for n in sizes + [atoms]),
        [SMEM] + [VMEM] * len(buffers),
        (VMEM,) * (bits + 1),
        [],
        "select_column_atoms",
        0,
        (wanted + 2 * atoms) * depth * half * 4,
    )(table, *buffers)
    sources = [c * column_count // row_count for c in range(columns)]
    pieces, takers = spread(pieces, sources, column_count, row_count, base)

    base = call(
        functools.partial(row_kernel, cores, units, held, scale),
        jax.ShapeDtypeStruct(base.shape, F32),
        [SMEM, HBM] + [VMEM] * 3,
        VMEM,
        [
            pltpu.VMEM(shape, BF16),
            pltpu.VMEM((domain, pao, pao), BF16),
            pltpu.SemaphoreType.DMA((row_count,)),
        ],
        "row_exchange",
        2 * row_count * column_count * domain * pao * npno * (pao + npno),
        coefficients.size,
    )(table, coefs, row_turned, base, metrics)

    return call(
        functools.partial(column_kernel, takers, scale),
        jax.ShapeDtypeStruct(amplitudes.shape, F32),
        [HBM] + [VMEM] * (3 + len(pieces)),
        VMEM,
        [
            pltpu.VMEM((wanted, depth, half), BF16),
            pltpu.VMEM((wanted, pao, pao), BF16),
            pltpu.VMEM((row_count, column_count, npno, lanes), F32),
            pltpu.VMEM((row_count, column_count, chunks, lanes), F32),
            pltpu.SMEM(kept_count.shape[::-1], jnp.int32),
            pltpu.SemaphoreType.DMA(()),
        ],
        "column_exchange",
        2 * row_count * column_count * domain * pao * npno * (pao + npno),
        coefficients.size,
    )(kept, column_coefficients, turned, base, *pieces)


def solution(mesh):
    placed = (
        P(("row", "col"), None, None),
        P("row", "col", None, None, None),
        P("row", "col", None),
        P("row", "col", None, None),
        P("row", "col", None),
        P(),
        P("row", "col"),
        P(),
        P(),
        P(),
    )
    return jax.shard_map(
        on_device, mesh=mesh, in_specs=placed, out_specs=P("row", "col", None), check_vma=False
    )
```

time: 63.5 us -> 46.9 us (0.74)
  the two profiles are of different devices: /device:TPU:21 before, /device:TPU:0 now
where the time goes in v2:
time: 46.9 us; the launch traced here: 46.7 us
  starting transfers between devices  23.6 us (50%)
  Pallas kernels  13.7 us (29%)
  waiting for transfers between devices  9.19 us (20%)
    ppermute x4, starting transfers between devices, swapped(): return lax.ppermute(block, axis, pairs + [(b, a) for a, b in pairs])  9.61 us
    ppermute x4, starting transfers between devices, spread(): got.append(lax.ppermute(pieces[p], ('row', 'col'), pairs))  9.42 us
    pallas_call x1, Pallas kernels, on_device(): call(couple_kernel, (jax.ShapeDtypeStruct((row_count, column_count, npno,...  5.1 us
    ppermute x2, waiting for transfers between devices, gather_metrics(): up = lax.ppermute(up, 'col', forward)  4.28 us
    pallas_call x1, Pallas kernels, on_device(): call(functools.partial(row_kernel, cores, units, held, scale), jax.ShapeD...  4.05 us
    ppermute x2, starting transfers between devices, gather_metrics(): up = lax.ppermute(up, 'col', forward)  3.51 us
    ppermute x4, waiting for transfers between devices, swapped(): return lax.ppermute(block, axis, pairs + [(b, a) for a, b in pairs])  2.78 us
    pallas_call x1, Pallas kernels, on_device(): call(functools.partial(column_kernel, takers, scale), jax.ShapeDtypeStruc...  1.92 us
  transfers between devices with their start and end apart: 15, of which 4 were waited for; matrix products, arithmetic and copies ran while one was open for 0% of the time, Pallas kernels for 20%

profile of v2, /device:TPU:0, one launch (start us, length us, event | category | flops | bytes accessed | tf_op | source)
XLA Modules:
  0.0 46.7 jit_solution(8437706003521853232)
XLA Ops:
  0.0 1.8 %pack_metric.1 = (bf16[2,272,128]{2,1,0:T(8,128)(2,1)S(1)}, s32[3,16]{1,0:T(4,128)S(1)}, bf16[4,2,32,128]{3,2,1,0:T(8,128)(2,1)S(1)}) custom-call(s32[3,16]{1,0:T(4,128)} %bitcast.4, bf16[4,2,4096]{2,1,0:T(2,128)(2,1)} %block_hbm.1, bf16[2,512,256]{2,1,0:T(8,128)(2,1)} %fit_ref.1), custom_call_target="tpu_custom_call" | custom-call | flops 134217728 | bytes 524288 | tf_op jit(solution)/shard_map/pack_metric/pallas_call | solution.py:473
  1.8 3.1 %collective-permute-start.5 = (bf16[2,272,128]{2,1,0:T(8,128)(2,1)S(1)}, bf16[2,272,128]{2,1,0:T(8,128)(2,1)S(1)}, u32[]{:S(2)}, u32[]{:S(2)}) collective-permute-start(bf16[2,272,128]{2,1,0:T(8,128)(2,1)S(1)} %get-tuple-element.23.refs_0_), channel_id=1, source_target_pairs={{0,2},{1,3},{2,6},{3,7},{6,4},{7,5},{4,0},{5,1},{8,10},{9,11},{10,... | collective-permute-start | bytes 417800 | tf_op jit(solution)/shard_map/ppermute | solution.py:384
  4.9 0.7 %collective-permute-start.3 = (bf16[4,2,32,128]{3,2,1,0:T(8,128)(2,1)S(1)}, bf16[4,2,32,128]{3,2,1,0:T(8,128)(2,1)S(1)}, u32[]{:S(2)}, u32[]{:S(2)}) collective-permute-start(bf16[4,2,32,128]{3,2,1,0:T(8,128)(2,1)S(1)} %get-tuple-element.17.refs_0_), channel_id=1, source_target_pairs={{1,2},{3,4},{5,6},{2,1},{4,3},{6,5},{9,10},{11,12},{13,14},{10,9},... | collective-permute-start | bytes 196616 | tf_op jit(solution)/shard_map/ppermute | solution.py:359
  5.5 4.0 %collective-permute-start.2 = (bf16[4,2,32,128]{3,2,1,0:T(8,128)(2,1)S(1)}, bf16[4,2,32,128]{3,2,1,0:T(8,128)(2,1)S(1)}, u32[]{:S(2)}, u32[]{:S(2)}) collective-permute-start(bf16[4,2,32,128]{3,2,1,0:T(8,128)(2,1)S(1)} %get-tuple-element.17.refs_0_), channel_id=1, source_target_pairs={{0,1},{2,3},{4,5},{6,7},{1,0},{3,2},{5,4},{7,6},{8,9},{10,11},{12,... | collective-permute-start | bytes 196616 | tf_op jit(solution)/shard_map/ppermute | solution.py:359
  9.5 0.7 %collective-permute-start.1 = (bf16[4,2,32,128]{3,2,1,0:T(8,128)(2,1)S(1)}, bf16[4,2,32,128]{3,2,1,0:T(8,128)(2,1)S(1)}, u32[]{:S(2)}, u32[]{:S(2)}) collective-permute-start(bf16[4,2,32,128]{3,2,1,0:T(8,128)(2,1)S(1)} %get-tuple-element.17.refs_0_), channel_id=1, source_target_pairs={{8,16},{16,8},{9,17},{17,9},{10,18},{18,10},{11,19},{19,11},{12,20... | collective-permute-start | bytes 196616 | tf_op jit(solution)/shard_map/ppermute | solution.py:359
  10.2 4.3 %collective-permute-start = (bf16[4,2,32,128]{3,2,1,0:T(8,128)(2,1)S(1)}, bf16[4,2,32,128]{3,2,1,0:T(8,128)(2,1)S(1)}, u32[]{:S(2)}, u32[]{:S(2)}) collective-permute-start(bf16[4,2,32,128]{3,2,1,0:T(8,128)(2,1)S(1)} %get-tuple-element.17.refs_0_), channel_id=1, source_target_pairs={{0,8},{16,24},{8,0},{24,16},{1,9},{17,25},{9,1},{25,17},{2,10},{18... | collective-permute-start | bytes 196616 | tf_op jit(solution)/shard_map/ppermute | solution.py:359
  14.5 0.0 collective-permute-done.3.refs_4_.refs_3_
  14.5 0.5 %collective-permute-start.9 = (bf16[2,272,128]{2,1,0:T(8,128)(2,1)S(1)}, bf16[2,272,128]{2,1,0:T(8,128)(2,1)S(1)}, u32[]{:S(2)}, u32[]{:S(2)}) collective-permute-start(bf16[2,272,128]{2,1,0:T(8,128)(2,1)S(1)} %get-tuple-element.23.refs_0_), channel_id=1, source_target_pairs={{2,0},{3,1},{6,2},{7,3},{4,6},{5,7},{0,4},{1,5},{10,8},{11,9},{14,... | collective-permute-start | bytes 417800 | tf_op jit(solution)/shard_map/ppermute | solution.py:387
  15.0 0.0 collective-permute-done.2.refs_3_.refs_2_
  15.0 0.0 collective-permute-done.1.refs_2_.refs_1_
  15.0 2.8 %collective-permute-done.refs_1_.refs_0_ = bf16[4,2,32,128]{3,2,1,0:T(8,128)(2,1)S(1)} collective-permute-done((bf16[4,2,32,128]{3,2,1,0:T(8,128)(2,1)S(1)}, bf16[4,2,32,128]{3,2,1,0:T(8,128)(2,1)S(1)}, u32[]{:S(2)}, u32[]{:S(2)}) %collective-permute-start) | collective-permute-done | bytes 65568 | tf_op jit(solution)/shard_map/ppermute | solution.py:359
  17.8 0.0 collective-permute-done.5.block_ref.refs_2_
  17.8 0.4 collective-permute-start.7
  18.3 0.0 collective-permute-start.4
  18.3 0.5 %collective-permute-start.6 = (bf16[2,272,128]{2,1,0:T(8,128)(2,1)S(1)}, bf16[2,272,128]{2,1,0:T(8,128)(2,1)S(1)}, u32[]{:S(2)}, u32[]{:S(2)}) collective-permute-start(bf16[2,272,128]{2,1,0:T(8,128)(2,1)S(1)} %collective-permute-done.5.block_ref.refs_2_), channel_id=1, source_target_pairs={{0,1},{1,0},{2,3},{3,2},{4,5},{5,4},{6,7},{7,6},{8,9},{9,8},{10,11... | collective-permute-start | bytes 417800 | tf_op jit(solution)/shard_map/ppermute | solution.py:398
  18.8 0.8 %collective-permute-done.9.refs_6_ = bf16[2,272,128]{2,1,0:T(8,128)(2,1)S(1)} collective-permute-done((bf16[2,272,128]{2,1,0:T(8,128)(2,1)S(1)}, bf16[2,272,128]{2,1,0:T(8,128)(2,1)S(1)}, u32[]{:S(2)}, u32[]{:S(2)}) %collective-permute-start.9) | collective-permute-done | bytes 139296 | tf_op jit(solution)/shard_map/ppermute | solution.py:387
  19.5 0.0 collective-permute-start.10
  19.5 4.3 %collective-permute-done.7.refs_4_ = bf16[2,272,128]{2,1,0:T(8,128)(2,1)S(1)} collective-permute-done((bf16[2,272,128]{2,1,0:T(8,128)(2,1)S(1)}, bf16[2,272,128]{2,1,0:T(8,128)(2,1)S(1)}, u32[]{:S(2)}, u32[]{:S(2)}) %collective-permute-start.7) | collective-permute-done | bytes 139296 | tf_op jit(solution)/shard_map/ppermute | solution.py:384
  23.8 0.0 collective-permute-start.8
  23.8 0.0 collective-permute-done.4.refs_1_
  23.8 0.0 collective-permute-done.10.refs_7_
  23.8 0.0 collective-permute-done.6.refs_3_
  23.8 1.3 %collective-permute-done.8.refs_5_ = bf16[2,272,128]{2,1,0:T(8,128)(2,1)S(1)} collective-permute-done((bf16[2,272,128]{2,1,0:T(8,128)(2,1)S(1)}, bf16[2,272,128]{2,1,0:T(8,128)(2,1)S(1)}, u32[]{:S(2)}, u32[]{:S(2)}) %collective-permute-start.8) | collective-permute-done | bytes 139296 | tf_op jit(solution)/shard_map/ppermute | solution.py:398
  25.2 0.8 %select_column_atoms.1 = (bf16[3,272,128]{2,1,0:T(8,128)(2,1)S(1)}, bf16[3,272,128]{2,1,0:T(8,128)(2,1)S(1)}, bf16[16,272,128]{2,1,0:T(8,128)(2,1)S(1)}) custom-call(s32[3,16]{1,0:T(4,128)S(1)} %get-tuple-element.20.atoms_ref, bf16[2,272,128]{2,1,0:T(8,128)(2,1)S(1)} %get-tuple-element.23.refs_0_, bf16[2,272,128]{2,1,0:T(8,128)(2,1)S(1)} %collective-permute-done.4.refs_1_, ...), custom_call_target="tpu_custom_call" | custom-call | bytes 5292032 | tf_op jit(solution)/shard_map/select_column_atoms/pallas_call | solution.py:534
  26.0 2.9 %collective-permute-start.11 = (bf16[3,272,128]{2,1,0:T(8,128)(2,1)S(1)}, bf16[3,272,128]{2,1,0:T(8,128)(2,1)S(1)}, u32[]{:S(2)}, u32[]{:S(2)}) collective-permute-start(bf16[3,272,128]{2,1,0:T(8,128)(2,1)S(1)} %get-tuple-element.25.refs_0_), channel_id=1, source_target_pairs={{0,8},{1,9},{10,2},{11,3},{20,28},{21,29},{30,22},{31,23}} | collective-permute-start | bytes 626696 | tf_op jit(solution)/shard_map/ppermute | solution.py:415
  28.9 1.3 %collective-permute-start.12 = (bf16[3,272,128]{2,1,0:T(8,128)(2,1)S(1)}, bf16[3,272,128]{2,1,0:T(8,128)(2,1)S(1)}, u32[]{:S(2)}, u32[]{:S(2)}) collective-permute-start(bf16[3,272,128]{2,1,0:T(8,128)(2,1)S(1)} %get-tuple-element.26.refs_1_), channel_id=1, source_target_pairs={{0,16},{1,17},{10,26},{11,27},{20,4},{21,5},{30,14},{31,15}} | collective-permute-start | bytes 626696 | tf_op jit(solution)/shard_map/ppermute | solution.py:415
  30.2 5.1 %couple.1 = (f32[4,2,64,64]{3,2,1,0:T(8,128)S(1)}, bf16[4,3,128,256]{3,2,1,0:T(8,128)(2,1)S(1)}, bf16[2,3,256,256]{3,2,1,0:T(8,128)(2,1)S(1)}, bf16[4,2,3,256,128]{4,3,2,1,0:T(8,128)(2,1)S(1)}) custom-call(s32[4,16]{1,0:T(4,128)} %bitcast.5, f32[4,16]{1,0:T(4,128)} %bitcast.6, f32[16]{0:T(128)} %occupied_hbm.1, f32[4,2,64]{2,1,0:T(2,128)} %virtual_hbm.1, ...), custom_call_target="tpu_custom_call" | custom-call | flops 67108864 | bytes 2621440 | tf_op jit(solution)/shard_map/couple/pallas_call | solution.py:498
  35.3 0.0 collective-permute-done.11.refs_2_
  35.3 0.0 collective-permute-done.12.refs_3_
  35.3 0.1 merge.1
  35.4 3.9 %collective-permute-start.13 = (bf16[3,272,128]{2,1,0:T(8,128)(2,1)S(1)}, bf16[3,272,128]{2,1,0:T(8,128)(2,1)S(1)}, u32[]{:S(2)}, u32[]{:S(2)}) collective-permute-start(bf16[3,272,128]{2,1,0:T(8,128)(2,1)S(1)} %get-tuple-element.27.refs_0_), channel_id=1, source_target_pairs={{0,16},{8,24},{1,17},{9,25},{10,26},{2,18},{11,27},{3,19},{20,4},{... | collective-permute-start | bytes 626696 | tf_op jit(solution)/shard_map/ppermute | solution.py:415
  39.3 1.3 %collective-permute-start.14 = (bf16[3,272,128]{2,1,0:T(8,128)(2,1)S(1)}, bf16[3,272,128]{2,1,0:T(8,128)(2,1)S(1)}, u32[]{:S(2)}, u32[]{:S(2)}) collective-permute-start(bf16[3,272,128]{2,1,0:T(8,128)(2,1)S(1)} %get-tuple-element.28.refs_1_), channel_id=1, source_target_pairs={{0,8},{16,24},{1,9},{17,25},{10,2},{26,18},{11,3},{27,19},{20,28},... | collective-permute-start | bytes 626696 | tf_op jit(solution)/shard_map/ppermute | solution.py:415
  40.6 4.1 %row_exchange.1.base_ref = f32[4,2,64,64]{3,2,1,0:T(8,128)S(1)} custom-call(s32[3,16]{1,0:T(4,128)S(1)} %get-tuple-element.20.atoms_ref, bf16[4,2,6,256,128]{4,3,2,1,0:T(8,128)(2,1)} %coef_hbm.3, bf16[4,3,128,256]{3,2,1,0:T(8,128)(2,1)S(1)} %get-tuple-element.21.turned_ref, f32[4,2,64,64]{3,2,1,0:T(8,128)S(1)} %get-tuple-element.22.base_ref.refs_4_, ...), custom_call_target="tpu_custom_call" | custom-call | flops 251658240 | bytes 1572864 | tf_op jit(solution)/shard_map/row_exchange/pallas_call | solution.py:547
  44.7 0.0 collective-permute-done.13.refs_2_
  44.7 0.0 collective-permute-done.14.refs_3_
  44.7 1.9 %column_exchange.1 = f32[4,2,4096]{2,1,0:T(2,128)} custom-call(s32[2,4]{1,0:T(2,128)} %bitcast.7, bf16[4,2,3,256,128]{4,3,2,1,0:T(8,128)(2,1)S(1)} %get-tuple-element.18.coef_ref, bf16[2,3,256,256]{3,2,1,0:T(8,128)(2,1)S(1)} %get-tuple-element.19.turned_ref, f32[4,2,64,64]{3,2,1,0:T(8,128)S(1)} %row_exchange.1.base_ref, ...), custom_call_target="tpu_custom_call" | custom-call | flops 251658240 | bytes 1572864 | tf_op jit(solution)/shard_map/column_exchange/pallas_call | solution.py:562
  (1 shorter events, 0.0 us)
Async XLA Ops:
  1.8 16.0 %collective-permute-start.5 = (bf16[2,272,128]{2,1,0:T(8,128)(2,1)S(1)}, bf16[2,272,128]{2,1,0:T(8,128)(2,1)S(1)}, u32[]{:S(2)}, u32[]{:S(2)}) collective-permute-start(bf16[2,272,128]{2,1,0:T(8,128)(2,1)S(1)} %get-tuple-element.23.refs_0_), channel_id=1, source_target_pairs={{0,2},{1,3},{2,6},{3,7},{6,4},{7,5},{4,0},{5,1},{8,10},{9,11},{10,... | collective-permute-start | bytes 417800 | tf_op jit(solution)/shard_map/ppermute | solution.py:384
  4.9 9.6 %collective-permute-start.3 = (bf16[4,2,32,128]{3,2,1,0:T(8,128)(2,1)S(1)}, bf16[4,2,32,128]{3,2,1,0:T(8,128)(2,1)S(1)}, u32[]{:S(2)}, u32[]{:S(2)}) collective-permute-start(bf16[4,2,32,128]{3,2,1,0:T(8,128)(2,1)S(1)} %get-tuple-element.17.refs_0_), channel_id=1, source_target_pairs={{1,2},{3,4},{5,6},{2,1},{4,3},{6,5},{9,10},{11,12},{13,14},{10,9},... | collective-permute-start | bytes 196616 | tf_op jit(solution)/shard_map/ppermute | solution.py:359
  5.5 9.5 %collective-permute-start.2 = (bf16[4,2,32,128]{3,2,1,0:T(8,128)(2,1)S(1)}, bf16[4,2,32,128]{3,2,1,0:T(8,128)(2,1)S(1)}, u32[]{:S(2)}, u32[]{:S(2)}) collective-permute-start(bf16[4,2,32,128]{3,2,1,0:T(8,128)(2,1)S(1)} %get-tuple-element.17.refs_0_), channel_id=1, source_target_pairs={{0,1},{2,3},{4,5},{6,7},{1,0},{3,2},{5,4},{7,6},{8,9},{10,11},{12,... | collective-permute-start | bytes 196616 | tf_op jit(solution)/shard_map/ppermute | solution.py:359
  9.5 5.5 %collective-permute-start.1 = (bf16[4,2,32,128]{3,2,1,0:T(8,128)(2,1)S(1)}, bf16[4,2,32,128]{3,2,1,0:T(8,128)(2,1)S(1)}, u32[]{:S(2)}, u32[]{:S(2)}) collective-permute-start(bf16[4,2,32,128]{3,2,1,0:T(8,128)(2,1)S(1)} %get-tuple-element.17.refs_0_), channel_id=1, source_target_pairs={{8,16},{16,8},{9,17},{17,9},{10,18},{18,10},{11,19},{19,11},{12,20... | collective-permute-start | bytes 196616 | tf_op jit(solution)/shard_map/ppermute | solution.py:359
  10.2 7.6 %collective-permute-start = (bf16[4,2,32,128]{3,2,1,0:T(8,128)(2,1)S(1)}, bf16[4,2,32,128]{3,2,1,0:T(8,128)(2,1)S(1)}, u32[]{:S(2)}, u32[]{:S(2)}) collective-permute-start(bf16[4,2,32,128]{3,2,1,0:T(8,128)(2,1)S(1)} %get-tuple-element.17.refs_0_), channel_id=1, source_target_pairs={{0,8},{16,24},{8,0},{24,16},{1,9},{17,25},{9,1},{25,17},{2,10},{18... | collective-permute-start | bytes 196616 | tf_op jit(solution)/shard_map/ppermute | solution.py:359
  14.5 5.1 %collective-permute-start.9 = (bf16[2,272,128]{2,1,0:T(8,128)(2,1)S(1)}, bf16[2,272,128]{2,1,0:T(8,128)(2,1)S(1)}, u32[]{:S(2)}, u32[]{:S(2)}) collective-permute-start(bf16[2,272,128]{2,1,0:T(8,128)(2,1)S(1)} %get-tuple-element.23.refs_0_), channel_id=1, source_target_pairs={{2,0},{3,1},{6,2},{7,3},{4,6},{5,7},{0,4},{1,5},{10,8},{11,9},{14,... | collective-permute-start | bytes 417800 | tf_op jit(solution)/shard_map/ppermute | solution.py:387
  17.8 6.0 %collective-permute-start.7 = (bf16[2,272,128]{2,1,0:T(8,128)(2,1)S(1)}, bf16[2,272,128]{2,1,0:T(8,128)(2,1)S(1)}, u32[]{:S(2)}, u32[]{:S(2)}) collective-permute-start(bf16[2,272,128]{2,1,0:T(8,128)(2,1)S(1)} %after_neighbours.1), channel_id=1, source_target_pairs={{0,2},{1,3},{2,6},{3,7},{6,4},{7,5},{4,0},{5,1},{8,10},{9,11},{10,... | collective-permute-start | bytes 417800 | tf_op jit(solution)/shard_map/ppermute | solution.py:384
  18.3 5.6 %collective-permute-start.4 = (bf16[2,272,128]{2,1,0:T(8,128)(2,1)S(1)}, bf16[2,272,128]{2,1,0:T(8,128)(2,1)S(1)}, u32[]{:S(2)}, u32[]{:S(2)}) collective-permute-start(bf16[2,272,128]{2,1,0:T(8,128)(2,1)S(1)} %get-tuple-element.23.refs_0_), channel_id=1, source_target_pairs={{0,1},{1,0},{2,3},{3,2},{4,5},{5,4},{6,7},{7,6},{8,9},{9,8},{10,11... | collective-permute-start | bytes 417800 | tf_op jit(solution)/shard_map/ppermute | solution.py:398
  18.3 5.6 %collective-permute-start.6 = (bf16[2,272,128]{2,1,0:T(8,128)(2,1)S(1)}, bf16[2,272,128]{2,1,0:T(8,128)(2,1)S(1)}, u32[]{:S(2)}, u32[]{:S(2)}) collective-permute-start(bf16[2,272,128]{2,1,0:T(8,128)(2,1)S(1)} %collective-permute-done.5.block_ref.refs_2_), channel_id=1, source_target_pairs={{0,1},{1,0},{2,3},{3,2},{4,5},{5,4},{6,7},{7,6},{8,9},{9,8},{10,11... | collective-permute-start | bytes 417800 | tf_op jit(solution)/shard_map/ppermute | solution.py:398
  19.5 4.3 %collective-permute-start.10 = (bf16[2,272,128]{2,1,0:T(8,128)(2,1)S(1)}, bf16[2,272,128]{2,1,0:T(8,128)(2,1)S(1)}, u32[]{:S(2)}, u32[]{:S(2)}) collective-permute-start(bf16[2,272,128]{2,1,0:T(8,128)(2,1)S(1)} %collective-permute-done.9.refs_6_), channel_id=1, source_target_pairs={{0,1},{1,0},{2,3},{3,2},{4,5},{5,4},{6,7},{7,6},{8,9},{9,8},{10,11... | collective-permute-start | bytes 417800 | tf_op jit(solution)/shard_map/ppermute | solution.py:398
  23.8 1.4 %collective-permute-start.8 = (bf16[2,272,128]{2,1,0:T(8,128)(2,1)S(1)}, bf16[2,272,128]{2,1,0:T(8,128)(2,1)S(1)}, u32[]{:S(2)}, u32[]{:S(2)}) collective-permute-start(bf16[2,272,128]{2,1,0:T(8,128)(2,1)S(1)} %collective-permute-done.7.refs_4_), channel_id=1, source_target_pairs={{0,1},{1,0},{2,3},{3,2},{4,5},{5,4},{6,7},{7,6},{8,9},{9,8},{10,11... | collective-permute-start | bytes 417800 | tf_op jit(solution)/shard_map/ppermute | solution.py:398
  26.0 9.3 %collective-permute-start.11 = (bf16[3,272,128]{2,1,0:T(8,128)(2,1)S(1)}, bf16[3,272,128]{2,1,0:T(8,128)(2,1)S(1)}, u32[]{:S(2)}, u32[]{:S(2)}) collective-permute-start(bf16[3,272,128]{2,1,0:T(8,128)(2,1)S(1)} %get-tuple-element.25.refs_0_), channel_id=1, source_target_pairs={{0,8},{1,9},{10,2},{11,3},{20,28},{21,29},{30,22},{31,23}} | collective-permute-start | bytes 626696 | tf_op jit(solution)/shard_map/ppermute | solution.py:415
  28.9 6.4 %collective-permute-start.12 = (bf16[3,272,128]{2,1,0:T(8,128)(2,1)S(1)}, bf16[3,272,128]{2,1,0:T(8,128)(2,1)S(1)}, u32[]{:S(2)}, u32[]{:S(2)}) collective-permute-start(bf16[3,272,128]{2,1,0:T(8,128)(2,1)S(1)} %get-tuple-element.26.refs_1_), channel_id=1, source_target_pairs={{0,16},{1,17},{10,26},{11,27},{20,4},{21,5},{30,14},{31,15}} | collective-permute-start | bytes 626696 | tf_op jit(solution)/shard_map/ppermute | solution.py:415
  35.4 9.3 %collective-permute-start.13 = (bf16[3,272,128]{2,1,0:T(8,128)(2,1)S(1)}, bf16[3,272,128]{2,1,0:T(8,128)(2,1)S(1)}, u32[]{:S(2)}, u32[]{:S(2)}) collective-permute-start(bf16[3,272,128]{2,1,0:T(8,128)(2,1)S(1)} %get-tuple-element.27.refs_0_), channel_id=1, source_target_pairs={{0,16},{8,24},{1,17},{9,25},{10,26},{2,18},{11,27},{3,19},{20,4},{... | collective-permute-start | bytes 626696 | tf_op jit(solution)/shard_map/ppermute | solution.py:415
  39.3 5.4 %collective-permute-start.14 = (bf16[3,272,128]{2,1,0:T(8,128)(2,1)S(1)}, bf16[3,272,128]{2,1,0:T(8,128)(2,1)S(1)}, u32[]{:S(2)}, u32[]{:S(2)}) collective-permute-start(bf16[3,272,128]{2,1,0:T(8,128)(2,1)S(1)} %get-tuple-element.28.refs_1_), channel_id=1, source_target_pairs={{0,8},{16,24},{1,9},{17,25},{10,2},{26,18},{11,3},{27,19},{20,28},... | collective-permute-start | bytes 626696 | tf_op jit(solution)/shard_map/ppermute | solution.py:415

commit v3 on v2

--- a/solution.py
+++ b/solution.py
@@ -111,20 +111,19 @@
     return (turn * cores + side) * held + slot
 
 
-def select_kernel(cores, units, pieces, atoms_ref, *refs):
+def select_kernel(cores, units, atoms_ref, *refs):
     count = units * cores
-    buffers, outs, all_ref = refs[:count], refs[count:-1], refs[-1]
+    buffers, (piece_ref, all_ref) = refs[:count], refs[-2:]
     held = buffers[0].shape[0]
     row_place, col_place = lax.axis_index("row"), lax.axis_index("col")
     domain = atoms_ref.shape[0]
-    columns = sum(pieces) // domain
+    wanted = piece_ref.shape[0]
     for index, buffer in enumerate(buffers):
         all_ref[index * held : (index + 1) * held] = buffer[...]
-    targets = [(out, n) for out in outs for n in range(out.shape[0])]
-    for index, (out, n) in enumerate(targets):
-        atom = atoms_ref[index % domain, col_place * columns + index // domain]
+    for index in range(wanted):
+        atom = atoms_ref[index % domain, col_place * (wanted // domain) + index // domain]
         place = pick_place(atom, row_place, col_place, cores, units, held)
-        out[n] = all_ref[place]
+        piece_ref[index] = all_ref[place]
 
 
 def pass_kernel(block_ref, *refs):
@@ -274,13 +273,14 @@
     lax.fori_loop(0, row_count, one_row, 0)
 
 
-def rows_away(column_count, row_count):
-    source = lax.axis_index("col") * column_count // row_count
-    return jnp.bitwise_xor(lax.axis_index("row"), source)
-
-
-def merge_into(away, takers, kept, got, target):
-    taken = functools.reduce(jnp.logical_or, [away == taker for taker in takers])
+def merge_into(takers, column_count, row_count, kept, got, target):
+    col_place = lax.axis_index("col")
+    away = jnp.bitwise_xor(lax.axis_index("row"), col_place * column_count // row_count)
+    turn = col_place % len(takers)
+    taken = functools.reduce(
+        jnp.logical_or,
+        [(turn == n) & (away == taker) for n, these in enumerate(takers) for taker in these],
+    )
 
     @pl.when(taken)
     def _():
@@ -291,27 +291,20 @@
         target[...] = kept[...]
 
 
-def merge_kernel(takers, column_count, row_count, *refs):
-    count = len(takers)
-    away = rows_away(column_count, row_count)
-    for p in range(count):
-        merge_into(away, takers[p], refs[p], refs[count + p], refs[2 * count + 1 + p])
-
-
-def column_kernel(takers, scale, kept_hbm, coef_ref, turned_ref, base_ref, *refs):
-    count = len(takers)
-    out_ref, packed_ref, metric_ref, wide_ref, flat_ref, kept_ref, kept_sem = refs[2 * count :]
+def merge_kernel(takers, column_count, row_count, kept_ref, got_ref, _, out_ref):
+    merge_into(takers, column_count, row_count, kept_ref, got_ref, out_ref)
+
+
+def column_kernel(
+    takers, scale, kept_hbm, coef_ref, turned_ref, base_ref, held_ref, got_ref,
+    out_ref, packed_ref, metric_ref, wide_ref, flat_ref, kept_ref, kept_sem,
+):
     row_count, column_count, domain = coef_ref.shape[:3]
     npno = base_ref.shape[2]
     lanes = 2 * npno
     kept_copy = pltpu.make_async_copy(kept_hbm, kept_ref, kept_sem)
     kept_copy.start()
-    away = rows_away(column_count, row_count)
-    start = 0
-    for p in range(count):
-        size = refs[p].shape[0]
-        merge_into(away, takers[p], refs[p], refs[count + p], packed_ref.at[pl.ds(start, size)])
-        start += size
+    merge_into(takers, column_count, row_count, held_ref, got_ref, packed_ref)
     slots = column_count * domain
     lows = [unpack(packed_ref[index], metric_ref.at[index]) for index in range(slots)]
     products = []
@@ -359,7 +352,20 @@
     return lax.ppermute(block, axis, pairs + [(b, a) for a, b in pairs])
 
 
-def gather_metrics(packed, cores, units, first):
+def after(block, others):
+    return call(
+        pass_kernel,
+        jax.ShapeDtypeStruct(block.shape, block.dtype),
+        [VMEM] + [ANY] * len(others),
+        VMEM,
+        [],
+        "after_others",
+        0,
+        0,
+    )(block, *others)
+
+
+def gather_metrics(packed, cores, units, first, second):
     order = ring_order(units)
     forward = [
         (order[n] * cores + k, order[(n + 1) % units] * cores + k)
@@ -371,17 +377,10 @@
     up = down = packed
     for step in range(1, units // 2 + 1):
         if step == 2:
-            up = call(
-                pass_kernel,
-                jax.ShapeDtypeStruct(up.shape, up.dtype),
-                [VMEM] + [ANY] * len(first),
-                VMEM,
-                [],
-                "after_neighbours",
-                0,
-                0,
-            )(up, *first)
+            up = after(up, first)
         up = lax.ppermute(up, "col", forward)
+        if step == 2:
+            up = after(up, second)
         turns[step] = up
         if units - step > units // 2:
             down = lax.ppermute(down, "col", backward)
@@ -399,34 +398,35 @@
     return buffers
 
 
-def spread(pieces, sources, column_count, row_count, first):
+def spread(piece, sources, column_count, row_count, first):
     rows, columns = lax.axis_size("row"), len(sources)
-    bits = len(pieces)
-    reached = [[0] for _ in pieces]
+    bits = rows.bit_length() - 1
+    assert rows == 1 << bits
+    reached = [[0] for _ in range(bits)]
     for step in range(bits):
-        got, takers = [], []
-        for p in range(bits):
-            bit = 1 << ((p + step) % bits)
-            pairs = [
+        pairs, takers = [], []
+        for turn in range(bits):
+            bit = 1 << ((turn + step) % bits)
+            pairs += [
                 ((sources[c] ^ away) * columns + c, (sources[c] ^ away ^ bit) * columns + c)
-                for c in range(columns)
-                for away in reached[p]
+                for c in range(turn, columns, bits)
+                for away in reached[turn]
             ]
-            got.append(lax.ppermute(pieces[p], ("row", "col"), pairs))
-            takers.append([away ^ bit for away in reached[p]])
-            reached[p] = reached[p] + takers[p]
+            takers.append([away ^ bit for away in reached[turn]])
+            reached[turn] = reached[turn] + takers[turn]
+        got = lax.ppermute(piece, ("row", "col"), pairs)
         if step < bits - 1:
-            pieces = call(
+            piece = call(
                 functools.partial(merge_kernel, takers, column_count, row_count),
-                tuple(jax.ShapeDtypeStruct(piece.shape, piece.dtype) for piece in pieces),
-                [VMEM] * (2 * bits) + [ANY],
-                (VMEM,) * bits,
+                jax.ShapeDtypeStruct(piece.shape, piece.dtype),
+                [VMEM, VMEM, ANY],
+                VMEM,
                 [],
                 "merge",
                 0,
                 0,
-            )(*pieces, *got, first)
-    return list(pieces) + got, takers
+            )(piece, got, first)
+    return piece, got, takers
 
 
 def on_device(
@@ -446,7 +446,7 @@
     domain = orbital_atoms.shape[1]
     npno = virtual_energy.shape[2]
     terms = intersections.shape[2]
-    rows, columns = lax.axis_size("row"), lax.axis_size("col")
+    columns = lax.axis_size("col")
     cores = row_count // column_count
     units = columns // cores
     scale = (2 * domain * aux) ** (-0.5)
@@ -492,7 +492,7 @@
         fitting.size * 2,
     )(atoms_table, own_block, fit)
     halos = [swapped(lines, axis, first) for axis in ("row", "col") for first in (0, 1)]
-    buffers = gather_metrics(packed, cores, units, halos)
+    buffers = gather_metrics(packed, cores, units, halos[2:], halos[:2])
     blocks = [lines] + halos
     shape = (row_count, column_count, domain, pao, lanes)
     base, row_turned, turned, column_coefficients = call(
@@ -526,23 +526,20 @@
         intersections.size * 4 + coefficients.size,
     )(partner, value, occupied, virtual, coefs, inter, *blocks)
 
-    bits = rows.bit_length() - 1
-    assert rows == 1 << bits
     wanted = column_count * domain
-    sizes = [wanted * (p + 1) // bits - wanted * p // bits for p in range(bits)]
     atoms = len(buffers) * held
-    *pieces, metrics = call(
-        functools.partial(select_kernel, cores, units, sizes),
-        tuple(jax.ShapeDtypeStruct((n, depth, half), BF16) for n in sizes + [atoms]),
+    piece, metrics = call(
+        functools.partial(select_kernel, cores, units),
+        tuple(jax.ShapeDtypeStruct((n, depth, half), BF16) for n in (wanted, atoms)),
         [SMEM] + [VMEM] * len(buffers),
-        (VMEM,) * (bits + 1),
+        (VMEM,) * 2,
         [],
         "select_column_atoms",
         0,
         (wanted + 2 * atoms) * depth * half * 4,
     )(table, *buffers)
     sources = [c * column_count // row_count for c in range(columns)]
-    pieces, takers = spread(pieces, sources, column_count, row_count, base)
+    piece, got, takers = spread(piece, sources, column_count, row_count, base)
 
     base = call(
         functools.partial(row_kernel, cores, units, held, scale),
@@ -562,7 +559,7 @@
     return call(
         functools.partial(column_kernel, takers, scale),
         jax.ShapeDtypeStruct(amplitudes.shape, F32),
-        [HBM] + [VMEM] * (3 + len(pieces)),
+        [HBM] + [VMEM] * 5,
         VMEM,
         [
             pltpu.VMEM((wanted, depth, half), BF16),
@@ -575,7 +572,7 @@
         "column_exchange",
         2 * row_count * column_count * domain * pao * npno * (pao + npno),
         coefficients.size,
-    )(kept, column_coefficients, turned, base, *pieces)
+    )(kept, column_coefficients, turned, base, piece, got)
 
 
 def solution(mesh):

time: 46.9 us -> 41.8 us (0.89)
  the two profiles are of different devices: /device:TPU:0 before, /device:TPU:12 now
where the time goes in v3:
time: 41.8 us; the launch traced here: 41.6 us
  starting transfers between devices  14.6 us (35%)
  Pallas kernels  13.8 us (33%)
  waiting for transfers between devices  13.1 us (31%)
    ppermute x2, waiting for transfers between devices, spread(): got = lax.ppermute(piece, ('row', 'col'), pairs)  6.67 us
    ppermute x4, starting transfers between devices, swapped(): return lax.ppermute(block, axis, pairs + [(b, a) for a, b in pairs])  5.38 us
    ppermute x4, waiting for transfers between devices, swapped(): return lax.ppermute(block, axis, pairs + [(b, a) for a, b in pairs])  5.12 us
    pallas_call x1, Pallas kernels, on_device(): call(couple_kernel, (jax.ShapeDtypeStruct((row_count, column_count, npno,...  5.11 us
    ppermute x2, starting transfers between devices, gather_metrics(): up = lax.ppermute(up, 'col', forward)  4.46 us
    pallas_call x1, Pallas kernels, on_device(): call(functools.partial(row_kernel, cores, units, held, scale), jax.ShapeD...  4.05 us
    ppermute x1, starting transfers between devices, gather_metrics(): down = lax.ppermute(down, 'col', backward)  2.12 us
    ppermute x2, starting transfers between devices, spread(): got = lax.ppermute(piece, ('row', 'col'), pairs)  1.98 us
  transfers between devices with their start and end apart: 13, of which 6 were waited for; matrix products, arithmetic and copies ran while one was open for 0% of the time, Pallas kernels for 22%

profile of v3, /device:TPU:12, one launch (start us, length us, event | category | flops | bytes accessed | tf_op | source)
XLA Modules:
  0.0 41.6 jit_solution(2765741839510325867)
XLA Ops:
  0.0 1.8 %pack_metric.1 = (bf16[2,272,128]{2,1,0:T(8,128)(2,1)S(1)}, s32[3,16]{1,0:T(4,128)S(1)}, bf16[4,2,32,128]{3,2,1,0:T(8,128)(2,1)S(1)}) custom-call(s32[3,16]{1,0:T(4,128)} %bitcast.4, bf16[4,2,4096]{2,1,0:T(2,128)(2,1)} %block_hbm.1, bf16[2,512,256]{2,1,0:T(8,128)(2,1)} %fit_ref.1), custom_call_target="tpu_custom_call" | custom-call | flops 134217728 | bytes 524288 | tf_op jit(solution)/shard_map/pack_metric/pallas_call | solution.py:473
  1.8 2.6 %collective-permute-start.5 = (bf16[2,272,128]{2,1,0:T(8,128)(2,1)S(1)}, bf16[2,272,128]{2,1,0:T(8,128)(2,1)S(1)}, u32[]{:S(2)}, u32[]{:S(2)}) collective-permute-start(bf16[2,272,128]{2,1,0:T(8,128)(2,1)S(1)} %get-tuple-element.20.refs_0_), channel_id=1, source_target_pairs={{0,2},{1,3},{2,6},{3,7},{6,4},{7,5},{4,0},{5,1},{8,10},{9,11},{10,... | collective-permute-start | bytes 417800 | tf_op jit(solution)/shard_map/ppermute | solution.py:381
  4.4 1.9 %collective-permute-start.3 = (bf16[4,2,32,128]{3,2,1,0:T(8,128)(2,1)S(1)}, bf16[4,2,32,128]{3,2,1,0:T(8,128)(2,1)S(1)}, u32[]{:S(2)}, u32[]{:S(2)}) collective-permute-start(bf16[4,2,32,128]{3,2,1,0:T(8,128)(2,1)S(1)} %get-tuple-element.14.refs_0_), channel_id=1, source_target_pairs={{1,2},{3,4},{5,6},{2,1},{4,3},{6,5},{9,10},{11,12},{13,14},{10,9},... | collective-permute-start | bytes 196616 | tf_op jit(solution)/shard_map/ppermute | solution.py:352
  6.3 0.1 collective-permute-start.2
  6.4 2.1 %collective-permute-start.9 = (bf16[2,272,128]{2,1,0:T(8,128)(2,1)S(1)}, bf16[2,272,128]{2,1,0:T(8,128)(2,1)S(1)}, u32[]{:S(2)}, u32[]{:S(2)}) collective-permute-start(bf16[2,272,128]{2,1,0:T(8,128)(2,1)S(1)} %get-tuple-element.20.refs_0_), channel_id=1, source_target_pairs={{2,0},{3,1},{6,2},{7,3},{4,6},{5,7},{0,4},{1,5},{10,8},{11,9},{14,... | collective-permute-start | bytes 417800 | tf_op jit(solution)/shard_map/ppermute | solution.py:386
  8.5 1.5 %collective-permute-done.3.refs_4_.refs_1_ = bf16[4,2,32,128]{3,2,1,0:T(8,128)(2,1)S(1)} collective-permute-done((bf16[4,2,32,128]{3,2,1,0:T(8,128)(2,1)S(1)}, bf16[4,2,32,128]{3,2,1,0:T(8,128)(2,1)S(1)}, u32[]{:S(2)}, u32[]{:S(2)}) %collective-permute-start.3) | collective-permute-done | bytes 65568 | tf_op jit(solution)/shard_map/ppermute | solution.py:352
  10.0 0.0 collective-permute-done.2.refs_3_.refs_0_
  10.0 0.0 collective-permute-done.5.block_ref.refs_2_
  10.0 1.8 %collective-permute-start.7 = (bf16[2,272,128]{2,1,0:T(8,128)(2,1)S(1)}, bf16[2,272,128]{2,1,0:T(8,128)(2,1)S(1)}, u32[]{:S(2)}, u32[]{:S(2)}) collective-permute-start(bf16[2,272,128]{2,1,0:T(8,128)(2,1)S(1)} %after_others.2), channel_id=1, source_target_pairs={{0,2},{1,3},{2,6},{3,7},{6,4},{7,5},{4,0},{5,1},{8,10},{9,11},{10,... | collective-permute-start | bytes 417800 | tf_op jit(solution)/shard_map/ppermute | solution.py:381
  11.8 3.3 %collective-permute-start.1 = (bf16[4,2,32,128]{3,2,1,0:T(8,128)(2,1)S(1)}, bf16[4,2,32,128]{3,2,1,0:T(8,128)(2,1)S(1)}, u32[]{:S(2)}, u32[]{:S(2)}) collective-permute-start(bf16[4,2,32,128]{3,2,1,0:T(8,128)(2,1)S(1)} %get-tuple-element.14.refs_0_), channel_id=1, source_target_pairs={{8,16},{16,8},{9,17},{17,9},{10,18},{18,10},{11,19},{19,11},{12,20... | collective-permute-start | bytes 196616 | tf_op jit(solution)/shard_map/ppermute | solution.py:352
  15.2 0.1 collective-permute-start
  15.3 0.1 collective-permute-start.4
  15.3 3.5 %collective-permute-done.1.refs_2_.refs_1_ = bf16[4,2,32,128]{3,2,1,0:T(8,128)(2,1)S(1)} collective-permute-done((bf16[4,2,32,128]{3,2,1,0:T(8,128)(2,1)S(1)}, bf16[4,2,32,128]{3,2,1,0:T(8,128)(2,1)S(1)}, u32[]{:S(2)}, u32[]{:S(2)}) %collective-permute-start.1) | collective-permute-done | bytes 65568 | tf_op jit(solution)/shard_map/ppermute | solution.py:352
  18.9 0.0 collective-permute-start.6
  18.9 0.0 collective-permute-done.9.refs_6_
  18.9 0.5 %collective-permute-start.10 = (bf16[2,272,128]{2,1,0:T(8,128)(2,1)S(1)}, bf16[2,272,128]{2,1,0:T(8,128)(2,1)S(1)}, u32[]{:S(2)}, u32[]{:S(2)}) collective-permute-start(bf16[2,272,128]{2,1,0:T(8,128)(2,1)S(1)} %collective-permute-done.9.refs_6_), channel_id=1, source_target_pairs={{0,1},{1,0},{2,3},{3,2},{4,5},{5,4},{6,7},{7,6},{8,9},{9,8},{10,11... | collective-permute-start | bytes 417800 | tf_op jit(solution)/shard_map/ppermute | solution.py:397
  19.4 0.1 collective-permute-done.refs_1_.refs_0_
  19.5 0.0 collective-permute-done.7.block_ref
  19.5 0.1 collective-permute-start.8
  19.6 0.0 collective-permute-done.4.refs_1_
  19.6 0.8 %collective-permute-done.10.refs_7_ = bf16[2,272,128]{2,1,0:T(8,128)(2,1)S(1)} collective-permute-done((bf16[2,272,128]{2,1,0:T(8,128)(2,1)S(1)}, bf16[2,272,128]{2,1,0:T(8,128)(2,1)S(1)}, u32[]{:S(2)}, u32[]{:S(2)}) %collective-permute-start.10) | collective-permute-done | bytes 139296 | tf_op jit(solution)/shard_map/ppermute | solution.py:397
  20.5 0.0 collective-permute-done.6.refs_3_
  20.5 0.5 %collective-permute-done.8.refs_5_ = bf16[2,272,128]{2,1,0:T(8,128)(2,1)S(1)} collective-permute-done((bf16[2,272,128]{2,1,0:T(8,128)(2,1)S(1)}, bf16[2,272,128]{2,1,0:T(8,128)(2,1)S(1)}, u32[]{:S(2)}, u32[]{:S(2)}) %collective-permute-start.8) | collective-permute-done | bytes 139296 | tf_op jit(solution)/shard_map/ppermute | solution.py:397
  21.0 0.8 %select_column_atoms.1 = (bf16[6,272,128]{2,1,0:T(8,128)(2,1)S(1)}, bf16[16,272,128]{2,1,0:T(8,128)(2,1)S(1)}) custom-call(s32[3,16]{1,0:T(4,128)S(1)} %get-tuple-element.17.atoms_ref, bf16[2,272,128]{2,1,0:T(8,128)(2,1)S(1)} %get-tuple-element.20.refs_0_, bf16[2,272,128]{2,1,0:T(8,128)(2,1)S(1)} %collective-permute-done.4.refs_1_, ...), custom_call_target="tpu_custom_call" | custom-call | bytes 5292032 | tf_op jit(solution)/shard_map/select_column_atoms/pallas_call | solution.py:531
  21.8 0.7 %collective-permute-start.11 = (bf16[6,272,128]{2,1,0:T(8,128)(2,1)S(1)}, bf16[6,272,128]{2,1,0:T(8,128)(2,1)S(1)}, u32[]{:S(2)}, u32[]{:S(2)}) collective-permute-start(bf16[6,272,128]{2,1,0:T(8,128)(2,1)S(1)} %get-tuple-element.22.kept_ref), channel_id=1, source_target_pairs={{0,8},{10,2},{20,28},{30,22},{1,17},{11,27},{21,5},{31,15}} | collective-permute-start | bytes 1253384 | tf_op jit(solution)/shard_map/ppermute | solution.py:417
  22.5 5.1 %couple.1 = (f32[4,2,64,64]{3,2,1,0:T(8,128)S(1)}, bf16[4,3,128,256]{3,2,1,0:T(8,128)(2,1)S(1)}, bf16[2,3,256,256]{3,2,1,0:T(8,128)(2,1)S(1)}, bf16[4,2,3,256,128]{4,3,2,1,0:T(8,128)(2,1)S(1)}) custom-call(s32[4,16]{1,0:T(4,128)} %bitcast.5, f32[4,16]{1,0:T(4,128)} %bitcast.6, f32[16]{0:T(128)} %occupied_hbm.1, f32[4,2,64]{2,1,0:T(2,128)} %virtual_hbm.1, ...), custom_call_target="tpu_custom_call" | custom-call | flops 67108864 | bytes 2621440 | tf_op jit(solution)/shard_map/couple/pallas_call | solution.py:498
  27.6 0.0 collective-permute-done.11.got_ref
  27.6 0.1 merge.1.held_ref
  27.7 1.3 %collective-permute-start.12 = (bf16[6,272,128]{2,1,0:T(8,128)(2,1)S(1)}, bf16[6,272,128]{2,1,0:T(8,128)(2,1)S(1)}, u32[]{:S(2)}, u32[]{:S(2)}) collective-permute-start(bf16[6,272,128]{2,1,0:T(8,128)(2,1)S(1)} %merge.1.held_ref), channel_id=1, source_target_pairs={{0,16},{8,24},{10,26},{2,18},{20,4},{28,12},{30,14},{22,6},{1,9},{... | collective-permute-start | bytes 1253384 | tf_op jit(solution)/shard_map/ppermute | solution.py:417
  29.0 4.1 %row_exchange.1.base_ref = f32[4,2,64,64]{3,2,1,0:T(8,128)S(1)} custom-call(s32[3,16]{1,0:T(4,128)S(1)} %get-tuple-element.17.atoms_ref, bf16[4,2,6,256,128]{4,3,2,1,0:T(8,128)(2,1)} %coef_hbm.3, bf16[4,3,128,256]{3,2,1,0:T(8,128)(2,1)S(1)} %get-tuple-element.18.turned_ref, f32[4,2,64,64]{3,2,1,0:T(8,128)S(1)} %get-tuple-element.19.base_ref._, ...), custom_call_target="tpu_custom_call" | custom-call | flops 251658240 | bytes 1572864 | tf_op jit(solution)/shard_map/row_exchange/pallas_call | solution.py:544
  33.0 6.7 %collective-permute-done.12.got_ref = bf16[6,272,128]{2,1,0:T(8,128)(2,1)S(1)} collective-permute-done((bf16[6,272,128]{2,1,0:T(8,128)(2,1)S(1)}, bf16[6,272,128]{2,1,0:T(8,128)(2,1)S(1)}, u32[]{:S(2)}, u32[]{:S(2)}) %collective-permute-start.12) | collective-permute-done | bytes 417824 | tf_op jit(solution)/shard_map/ppermute | solution.py:417
  39.7 1.9 %column_exchange.1 = f32[4,2,4096]{2,1,0:T(2,128)} custom-call(s32[2,4]{1,0:T(2,128)} %bitcast.7, bf16[4,2,3,256,128]{4,3,2,1,0:T(8,128)(2,1)S(1)} %get-tuple-element.15.coef_ref, bf16[2,3,256,256]{3,2,1,0:T(8,128)(2,1)S(1)} %get-tuple-element.16.turned_ref, f32[4,2,64,64]{3,2,1,0:T(8,128)S(1)} %row_exchange.1.base_ref, ...), custom_call_target="tpu_custom_call" | custom-call | flops 251658240 | bytes 1572864 | tf_op jit(solution)/shard_map/column_exchange/pallas_call | solution.py:559
  (2 shorter events, 0.0 us)
Async XLA Ops:
  1.8 8.2 %collective-permute-start.5 = (bf16[2,272,128]{2,1,0:T(8,128)(2,1)S(1)}, bf16[2,272,128]{2,1,0:T(8,128)(2,1)S(1)}, u32[]{:S(2)}, u32[]{:S(2)}) collective-permute-start(bf16[2,272,128]{2,1,0:T(8,128)(2,1)S(1)} %get-tuple-element.20.refs_0_), channel_id=1, source_target_pairs={{0,2},{1,3},{2,6},{3,7},{6,4},{7,5},{4,0},{5,1},{8,10},{9,11},{10,... | collective-permute-start | bytes 417800 | tf_op jit(solution)/shard_map/ppermute | solution.py:381
  4.4 5.6 %collective-permute-start.3 = (bf16[4,2,32,128]{3,2,1,0:T(8,128)(2,1)S(1)}, bf16[4,2,32,128]{3,2,1,0:T(8,128)(2,1)S(1)}, u32[]{:S(2)}, u32[]{:S(2)}) collective-permute-start(bf16[4,2,32,128]{3,2,1,0:T(8,128)(2,1)S(1)} %get-tuple-element.14.refs_0_), channel_id=1, source_target_pairs={{1,2},{3,4},{5,6},{2,1},{4,3},{6,5},{9,10},{11,12},{13,14},{10,9},... | collective-permute-start | bytes 196616 | tf_op jit(solution)/shard_map/ppermute | solution.py:352
  6.3 3.7 %collective-permute-start.2 = (bf16[4,2,32,128]{3,2,1,0:T(8,128)(2,1)S(1)}, bf16[4,2,32,128]{3,2,1,0:T(8,128)(2,1)S(1)}, u32[]{:S(2)}, u32[]{:S(2)}) collective-permute-start(bf16[4,2,32,128]{3,2,1,0:T(8,128)(2,1)S(1)} %get-tuple-element.14.refs_0_), channel_id=1, source_target_pairs={{0,1},{2,3},{4,5},{6,7},{1,0},{3,2},{5,4},{7,6},{8,9},{10,11},{12,... | collective-permute-start | bytes 196616 | tf_op jit(solution)/shard_map/ppermute | solution.py:352
  6.4 12.5 %collective-permute-start.9 = (bf16[2,272,128]{2,1,0:T(8,128)(2,1)S(1)}, bf16[2,272,128]{2,1,0:T(8,128)(2,1)S(1)}, u32[]{:S(2)}, u32[]{:S(2)}) collective-permute-start(bf16[2,272,128]{2,1,0:T(8,128)(2,1)S(1)} %get-tuple-element.20.refs_0_), channel_id=1, source_target_pairs={{2,0},{3,1},{6,2},{7,3},{4,6},{5,7},{0,4},{1,5},{10,8},{11,9},{14,... | collective-permute-start | bytes 417800 | tf_op jit(solution)/shard_map/ppermute | solution.py:386
  10.0 9.5 %collective-permute-start.7 = (bf16[2,272,128]{2,1,0:T(8,128)(2,1)S(1)}, bf16[2,272,128]{2,1,0:T(8,128)(2,1)S(1)}, u32[]{:S(2)}, u32[]{:S(2)}) collective-permute-start(bf16[2,272,128]{2,1,0:T(8,128)(2,1)S(1)} %after_others.2), channel_id=1, source_target_pairs={{0,2},{1,3},{2,6},{3,7},{6,4},{7,5},{4,0},{5,1},{8,10},{9,11},{10,... | collective-permute-start | bytes 417800 | tf_op jit(solution)/shard_map/ppermute | solution.py:381
  11.8 7.0 %collective-permute-start.1 = (bf16[4,2,32,128]{3,2,1,0:T(8,128)(2,1)S(1)}, bf16[4,2,32,128]{3,2,1,0:T(8,128)(2,1)S(1)}, u32[]{:S(2)}, u32[]{:S(2)}) collective-permute-start(bf16[4,2,32,128]{3,2,1,0:T(8,128)(2,1)S(1)} %get-tuple-element.14.refs_0_), channel_id=1, source_target_pairs={{8,16},{16,8},{9,17},{17,9},{10,18},{18,10},{11,19},{19,11},{12,20... | collective-permute-start | bytes 196616 | tf_op jit(solution)/shard_map/ppermute | solution.py:352
  15.2 4.3 %collective-permute-start = (bf16[4,2,32,128]{3,2,1,0:T(8,128)(2,1)S(1)}, bf16[4,2,32,128]{3,2,1,0:T(8,128)(2,1)S(1)}, u32[]{:S(2)}, u32[]{:S(2)}) collective-permute-start(bf16[4,2,32,128]{3,2,1,0:T(8,128)(2,1)S(1)} %get-tuple-element.14.refs_0_), channel_id=1, source_target_pairs={{0,8},{16,24},{8,0},{24,16},{1,9},{17,25},{9,1},{25,17},{2,10},{18... | collective-permute-start | bytes 196616 | tf_op jit(solution)/shard_map/ppermute | solution.py:352
  15.3 4.4 %collective-permute-start.4 = (bf16[2,272,128]{2,1,0:T(8,128)(2,1)S(1)}, bf16[2,272,128]{2,1,0:T(8,128)(2,1)S(1)}, u32[]{:S(2)}, u32[]{:S(2)}) collective-permute-start(bf16[2,272,128]{2,1,0:T(8,128)(2,1)S(1)} %get-tuple-element.20.refs_0_), channel_id=1, source_target_pairs={{0,1},{1,0},{2,3},{3,2},{4,5},{5,4},{6,7},{7,6},{8,9},{9,8},{10,11... | collective-permute-start | bytes 417800 | tf_op jit(solution)/shard_map/ppermute | solution.py:397
  18.9 1.6 %collective-permute-start.6 = (bf16[2,272,128]{2,1,0:T(8,128)(2,1)S(1)}, bf16[2,272,128]{2,1,0:T(8,128)(2,1)S(1)}, u32[]{:S(2)}, u32[]{:S(2)}) collective-permute-start(bf16[2,272,128]{2,1,0:T(8,128)(2,1)S(1)} %collective-permute-done.5.block_ref.refs_2_), channel_id=1, source_target_pairs={{0,1},{1,0},{2,3},{3,2},{4,5},{5,4},{6,7},{7,6},{8,9},{9,8},{10,11... | collective-permute-start | bytes 417800 | tf_op jit(solution)/shard_map/ppermute | solution.py:397
  18.9 1.6 %collective-permute-start.10 = (bf16[2,272,128]{2,1,0:T(8,128)(2,1)S(1)}, bf16[2,272,128]{2,1,0:T(8,128)(2,1)S(1)}, u32[]{:S(2)}, u32[]{:S(2)}) collective-permute-start(bf16[2,272,128]{2,1,0:T(8,128)(2,1)S(1)} %collective-permute-done.9.refs_6_), channel_id=1, source_target_pairs={{0,1},{1,0},{2,3},{3,2},{4,5},{5,4},{6,7},{7,6},{8,9},{9,8},{10,11... | collective-permute-start | bytes 417800 | tf_op jit(solution)/shard_map/ppermute | solution.py:397
  19.5 1.4 %collective-permute-start.8 = (bf16[2,272,128]{2,1,0:T(8,128)(2,1)S(1)}, bf16[2,272,128]{2,1,0:T(8,128)(2,1)S(1)}, u32[]{:S(2)}, u32[]{:S(2)}) collective-permute-start(bf16[2,272,128]{2,1,0:T(8,128)(2,1)S(1)} %after_others.3.refs_4_), channel_id=1, source_target_pairs={{0,1},{1,0},{2,3},{3,2},{4,5},{5,4},{6,7},{7,6},{8,9},{9,8},{10,11... | collective-permute-start | bytes 417800 | tf_op jit(solution)/shard_map/ppermute | solution.py:397
  21.8 5.8 %collective-permute-start.11 = (bf16[6,272,128]{2,1,0:T(8,128)(2,1)S(1)}, bf16[6,272,128]{2,1,0:T(8,128)(2,1)S(1)}, u32[]{:S(2)}, u32[]{:S(2)}) collective-permute-start(bf16[6,272,128]{2,1,0:T(8,128)(2,1)S(1)} %get-tuple-element.22.kept_ref), channel_id=1, source_target_pairs={{0,8},{10,2},{20,28},{30,22},{1,17},{11,27},{21,5},{31,15}} | collective-permute-start | bytes 1253384 | tf_op jit(solution)/shard_map/ppermute | solution.py:417
  27.7 12.0 %collective-permute-start.12 = (bf16[6,272,128]{2,1,0:T(8,128)(2,1)S(1)}, bf16[6,272,128]{2,1,0:T(8,128)(2,1)S(1)}, u32[]{:S(2)}, u32[]{:S(2)}) collective-permute-start(bf16[6,272,128]{2,1,0:T(8,128)(2,1)S(1)} %merge.1.held_ref), channel_id=1, source_target_pairs={{0,16},{8,24},{10,26},{2,18},{20,4},{28,12},{30,14},{22,6},{1,9},{... | collective-permute-start | bytes 1253384 | tf_op jit(solution)/shard_map/ppermute | solution.py:417

commit v4 on v3

--- a/solution.py
+++ b/solution.py
@@ -134,16 +134,14 @@
     return jnp.where(turn == 0, 0, jnp.where((place + turn) == jnp.bitwise_xor(place, 1), 1, 2))
 
 
-def couple_kernel(partner_hbm, value_hbm, occupied_hbm, virtual_hbm, coef_hbm, inter_hbm, *refs):
-    blocks = refs[:5]
-    base_ref, row_turned_ref, turned_ref, coef_ref = refs[5:9]
-    flat_ref, wide_ref, mats_ref, inters_ref, own_ref, inter_ref = refs[9:15]
-    partner_ref, value_ref, occupied_ref, virtual_ref, sems, inter_sems, own_sems, coef_sems = refs[15:]
+def couple_kernel(partner_hbm, value_hbm, occupied_hbm, virtual_hbm, inter_hbm, *refs):
+    exchange_ref, blocks = refs[0], refs[1:6]
+    base_ref, flat_ref, wide_ref, mats_ref, inters_ref, inter_ref = refs[6:12]
+    partner_ref, value_ref, occupied_ref, virtual_ref, sems, inter_sems = refs[12:]
     row_count, column_count, terms, size = inter_ref.shape
     npno = base_ref.shape[2]
     lanes = 2 * npno
     chunks = size // lanes
-    domain = coef_ref.shape[2]
     partners = terms // 2
     row_place, col_place = lax.axis_index("row"), lax.axis_index("col")
     first_row = row_place * row_count
@@ -163,24 +161,10 @@
     def fetch_inter(i):
         return pltpu.make_async_copy(inter_hbm.at[i], inter_ref.at[i], inter_sems.at[i])
 
-    def fetch_own(i):
-        return pltpu.make_async_copy(
-            coef_hbm.at[i, :, pl.ds(0, domain)], own_ref.at[i], own_sems.at[i]
-        )
-
-    def fetch_coef(i):
-        return pltpu.make_async_copy(
-            coef_hbm.at[i, :, pl.ds(domain, domain)], coef_ref.at[i], coef_sems.at[i]
-        )
-
     for fetch in fetches:
         fetch.start()
     for i in range(row_count):
         fetch_inter(i).start()
-    for i in range(row_count):
-        fetch_own(i).start()
-        fetch_coef(i).start()
-
     def square(lines):
         wide_ref[pl.ds(0, chunks, 2), :] = lines
         wide_ref[pl.ds(1, chunks, 2), :] = pltpu.roll(lines, npno, 1)
@@ -199,8 +183,6 @@
 
     def one_row(i, carry):
         fetch_inter(i).wait()
-        fetch_own(i).wait()
-        fetch_coef(i).wait()
         for j in range(column_count):
             for q in range(chunks):
                 flat_ref[q] = inter_ref[i, j, :, q * lanes : (q + 1) * lanes].astype(F32)
@@ -228,28 +210,39 @@
                 total = total + weight * dot(half, turned[n])
             levels = jnp.broadcast_to(virtual_ref[i, pl.ds(j, 1)], (npno, npno))
             shift = levels + levels.T - occupied_ref[first_row + i] - occupied_ref[first_col + j]
-            base_ref[i, j] = shift * mats_ref[i, j].astype(F32) - total
+            base_ref[i, j] = exchange_ref[i, j] + shift * mats_ref[i, j].astype(F32) - total
+        return carry
+
+    lax.fori_loop(0, row_count, one_row, 0)
+
+
+def prepare_kernel(coef_hbm, own_ref, coef_ref, own_turned_ref, turned_ref, own_sems, coef_sems):
+    row_count, column_count, domain, _, lanes = own_ref.shape
+    npno = lanes // 2
+
+    def fetch(i, first, target_ref, sems):
+        return pltpu.make_async_copy(
+            coef_hbm.at[i, :, pl.ds(first, domain)], target_ref.at[i], sems.at[i]
+        )
+
+    for i in range(row_count):
+        fetch(i, 0, own_ref, own_sems).start()
+        fetch(i, domain, coef_ref, coef_sems).start()
+    for i in range(row_count):
+        fetch(i, 0, own_ref, own_sems).wait()
+        for j in range(column_count):
             for s in range(domain):
-                row_turned_ref[i, s, j * npno : (j + 1) * npno] = own_ref[i, j, s].T[:npno]
-                turned_ref[j, s, pl.ds(pl.multiple_of(i * npno, npno), npno)] = coef_ref[i, j, s].T[:npno]
-        return carry
-
-    lax.fori_loop(0, row_count, one_row, 0)
-
-
-def row_kernel(cores, units, held, scale, atoms_ref, coef_hbm, turned_ref, base_ref, all_ref, *refs):
-    out_ref, coef_ref, metric_ref, coef_sems = refs
+                own_turned_ref[i, s, j * npno : (j + 1) * npno] = own_ref[i, j, s].T[:npno]
+        fetch(i, domain, coef_ref, coef_sems).wait()
+        for j in range(column_count):
+            for s in range(domain):
+                turned_ref[j, s, i * npno : (i + 1) * npno] = coef_ref[i, j, s].T[:npno]
+
+
+def row_kernel(cores, units, held, scale, atoms_ref, coef_ref, turned_ref, all_ref, out_ref, metric_ref):
     row_count, column_count, domain = coef_ref.shape[:3]
-    npno = base_ref.shape[2]
+    npno = out_ref.shape[2]
     row_place, col_place = lax.axis_index("row"), lax.axis_index("col")
-
-    def fetch(i):
-        return pltpu.make_async_copy(
-            coef_hbm.at[i, :, pl.ds(0, domain)], coef_ref.at[i], coef_sems.at[i]
-        )
-
-    for i in range(row_count):
-        fetch(i).start()
 
     def one_row(i, carry):
         lows = []
@@ -262,12 +255,11 @@
             left = turned_ref[i, s]
             product = dot(left, metric_ref[s]) + left.astype(F32) * lows[s]
             products.append(product.astype(BF16))
-        fetch(i).wait()
         for j in range(column_count):
             total = dot(products[0][j * npno : (j + 1) * npno], coef_ref[i, j, 0])
             for s in range(1, domain):
                 total = total + dot(products[s][j * npno : (j + 1) * npno], coef_ref[i, j, s])
-            out_ref[i, j] = base_ref[i, j] + total[:, npno:] * scale
+            out_ref[i, j] = total[:, npno:] * scale
         return carry
 
     lax.fori_loop(0, row_count, one_row, 0)
@@ -291,8 +283,8 @@
         target[...] = kept[...]
 
 
-def merge_kernel(takers, column_count, row_count, kept_ref, got_ref, _, out_ref):
-    merge_into(takers, column_count, row_count, kept_ref, got_ref, out_ref)
+def merge_kernel(takers, column_count, row_count, kept_ref, got_ref, *refs):
+    merge_into(takers, column_count, row_count, kept_ref, got_ref, refs[-1])
 
 
 def column_kernel(
@@ -346,10 +338,21 @@
     )
 
 
-def swapped(block, axis, first):
+def partners_of(size, first):
+    pairs = [(n, n + 1) for n in range(first, size - 1, 2)]
+    alone = [(n, n) for n in range(size) if n < first or n >= first + 2 * len(pairs)]
+    return pairs, pairs + [(b, a) for a, b in pairs] + alone
+
+
+def neighbours(block, axis):
     size = lax.axis_size(axis)
-    pairs = [(n, n + 1) for n in range(first, size - 1, 2)]
-    return lax.ppermute(block, axis, pairs + [(b, a) for a, b in pairs])
+    even = lax.ppermute(block, axis, partners_of(size, 0)[1])
+    pairs, route = partners_of(size, 1)
+    if size % 4 == 0 and axis == "row" and all(a ^ b == 3 for a, b in pairs):
+        odd = lax.ppermute(even, axis, [(n, n ^ 2) for n in range(size)])
+    else:
+        odd = lax.ppermute(block, axis, route)
+    return [even, odd]
 
 
 def after(block, others):
@@ -376,10 +379,10 @@
     turns = [packed] + [None] * (units - 1)
     up = down = packed
     for step in range(1, units // 2 + 1):
-        if step == 2:
+        if step == 2 and first:
             up = after(up, first)
         up = lax.ppermute(up, "col", forward)
-        if step == 2:
+        if step == 2 and second:
             up = after(up, second)
         turns[step] = up
         if units - step > units // 2:
@@ -408,9 +411,9 @@
         for turn in range(bits):
             bit = 1 << ((turn + step) % bits)
             pairs += [
-                ((sources[c] ^ away) * columns + c, (sources[c] ^ away ^ bit) * columns + c)
+                (row * columns + c, (row ^ bit) * columns + c)
                 for c in range(turn, columns, bits)
-                for away in reached[turn]
+                for row in range(rows)
             ]
             takers.append([away ^ bit for away in reached[turn]])
             reached[turn] = reached[turn] + takers[turn]
@@ -419,13 +422,13 @@
             piece = call(
                 functools.partial(merge_kernel, takers, column_count, row_count),
                 jax.ShapeDtypeStruct(piece.shape, piece.dtype),
-                [VMEM, VMEM, ANY],
+                [VMEM, VMEM] + [ANY] * len(first),
                 VMEM,
                 [],
                 "merge",
                 0,
                 0,
-            )(piece, got, first)
+            )(piece, got, *first)
     return piece, got, takers
 
 
@@ -491,41 +494,26 @@
         2 * held * aux * pao * pao,
         fitting.size * 2,
     )(atoms_table, own_block, fit)
-    halos = [swapped(lines, axis, first) for axis in ("row", "col") for first in (0, 1)]
-    buffers = gather_metrics(packed, cores, units, halos[2:], halos[:2])
-    blocks = [lines] + halos
+    row_halos = neighbours(lines, "row")
+    col_halos = neighbours(lines, "col")
     shape = (row_count, column_count, domain, pao, lanes)
-    base, row_turned, turned, column_coefficients = call(
-        couple_kernel,
+    own_coefficients, column_coefficients, own_turned, turned = call(
+        prepare_kernel,
         (
-            jax.ShapeDtypeStruct((row_count, column_count, npno, npno), F32),
+            jax.ShapeDtypeStruct(shape, BF16),
+            jax.ShapeDtypeStruct(shape, BF16),
             jax.ShapeDtypeStruct((row_count, domain, column_count * npno, pao), BF16),
             jax.ShapeDtypeStruct((column_count, domain, row_count * npno, pao), BF16),
-            jax.ShapeDtypeStruct(shape, BF16),
         ),
-        [HBM] * 6 + [VMEM] * len(blocks),
+        [HBM],
         (VMEM,) * 4,
-        [
-            pltpu.VMEM((chunks, terms, lanes), F32),
-            pltpu.VMEM((npno, lanes), F32),
-            pltpu.VMEM((len(blocks) * row_count, column_count, npno, npno), BF16),
-            pltpu.VMEM((terms, npno, npno), BF16),
-            pltpu.VMEM(shape, BF16),
-            pltpu.VMEM(intersections.shape, BF16),
-            pltpu.SMEM(fock_partner.shape[::-1], jnp.int32),
-            pltpu.SMEM(fock_value.shape[::-1], F32),
-            pltpu.SMEM(occupied_energy.shape, F32),
-            pltpu.VMEM(virtual_energy.shape, F32),
-            pltpu.SemaphoreType.DMA((4,)),
-            pltpu.SemaphoreType.DMA((row_count,)),
-            pltpu.SemaphoreType.DMA((row_count,)),
-            pltpu.SemaphoreType.DMA((row_count,)),
-        ],
-        "couple",
-        4 * row_count * column_count * terms * npno**3,
-        intersections.size * 4 + coefficients.size,
-    )(partner, value, occupied, virtual, coefs, inter, *blocks)
-
+        [pltpu.SemaphoreType.DMA((row_count,)), pltpu.SemaphoreType.DMA((row_count,))],
+        "prepare",
+        0,
+        coefficients.size * 4,
+    )(coefs)
+    buffers = gather_metrics(packed, cores, units, row_halos[:1], [own_turned] + row_halos[1:])
+    blocks = [lines] + row_halos + col_halos
     wanted = column_count * domain
     atoms = len(buffers) * held
     piece, metrics = call(
@@ -538,23 +526,42 @@
         0,
         (wanted + 2 * atoms) * depth * half * 4,
     )(table, *buffers)
-    sources = [c * column_count // row_count for c in range(columns)]
-    piece, got, takers = spread(piece, sources, column_count, row_count, base)
-
-    base = call(
+    exchange = call(
         functools.partial(row_kernel, cores, units, held, scale),
-        jax.ShapeDtypeStruct(base.shape, F32),
-        [SMEM, HBM] + [VMEM] * 3,
+        jax.ShapeDtypeStruct((row_count, column_count, npno, npno), F32),
+        [SMEM] + [VMEM] * 3,
         VMEM,
-        [
-            pltpu.VMEM(shape, BF16),
-            pltpu.VMEM((domain, pao, pao), BF16),
-            pltpu.SemaphoreType.DMA((row_count,)),
-        ],
+        [pltpu.VMEM((domain, pao, pao), BF16)],
         "row_exchange",
         2 * row_count * column_count * domain * pao * npno * (pao + npno),
         coefficients.size,
-    )(table, coefs, row_turned, base, metrics)
+    )(table, own_coefficients, own_turned, metrics)
+
+    sources = [c * column_count // row_count for c in range(columns)]
+    piece, got, takers = spread(piece, sources, column_count, row_count, [exchange] + col_halos)
+
+    base = call(
+        couple_kernel,
+        jax.ShapeDtypeStruct((row_count, column_count, npno, npno), F32),
+        [HBM] * 5 + [VMEM] * (1 + len(blocks)),
+        VMEM,
+        [
+            pltpu.VMEM((chunks, terms, lanes), F32),
+            pltpu.VMEM((npno, lanes), F32),
+            pltpu.VMEM((len(blocks) * row_count, column_count, npno, npno), BF16),
+            pltpu.VMEM((terms, npno, npno), BF16),
+            pltpu.VMEM(intersections.shape, BF16),
+            pltpu.SMEM(fock_partner.shape[::-1], jnp.int32),
+            pltpu.SMEM(fock_value.shape[::-1], F32),
+            pltpu.SMEM(occupied_energy.shape, F32),
+            pltpu.VMEM(virtual_energy.shape, F32),
+            pltpu.SemaphoreType.DMA((4,)),
+            pltpu.SemaphoreType.DMA((row_count,)),
+        ],
+        "couple",
+        4 * row_count * column_count * terms * npno**3,
+        intersections.size * 4,
+    )(partner, value, occupied, virtual, inter, exchange, *blocks)
 
     return call(
         functools.partial(column_kernel, takers, scale),

time: 41.8 us -> 38.9 us (0.931)
  the two profiles are of different devices: /device:TPU:12 before, /device:TPU:0 now
where the time goes in v4:
time: 38.9 us; the launch traced here: 38.4 us
  starting transfers between devices  16 us (41%)
  Pallas kernels  14.2 us (37%)
  waiting for transfers between devices  8.06 us (21%)
    ppermute x2, starting transfers between devices, gather_metrics(): up = lax.ppermute(up, 'col', forward)  6.9 us
    ppermute x2, waiting for transfers between devices, spread(): got = lax.ppermute(piece, ('row', 'col'), pairs)  5.16 us
    pallas_call x1, Pallas kernels, on_device(): call(couple_kernel, jax.ShapeDtypeStruct((row_count, column_count, npno,...  4.34 us
    pallas_call x1, Pallas kernels, on_device(): call(functools.partial(row_kernel, cores, units, held, scale), jax.ShapeD...  3.11 us
    ppermute x2, starting transfers between devices, spread(): got = lax.ppermute(piece, ('row', 'col'), pairs)  2.9 us
    pallas_call x1, Pallas kernels, on_device(): call(prepare_kernel, (jax.ShapeDtypeStruct(shape, BF16), jax.ShapeDtypeSt...  2.25 us
    pallas_call x1, Pallas kernels, on_device(): call(functools.partial(column_kernel, takers, scale), jax.ShapeDtypeStruc...  1.92 us
    pallas_call x1, Pallas kernels, on_device(): call(pack_kernel, (jax.ShapeDtypeStruct((held, depth, half), BF16), jax.S...  1.78 us
  transfers between devices with their start and end apart: 13, of which 7 were waited for; matrix products, arithmetic and copies ran while one was open for 0% of the time, Pallas kernels for 25%

profile of v4, /device:TPU:0, one launch (start us, length us, event | category | flops | bytes accessed | tf_op | source)
XLA Modules:
  0.0 38.4 jit_solution(8085514743773795721)
XLA Ops:
  0.0 1.8 %pack_metric.1 = (bf16[2,272,128]{2,1,0:T(8,128)(2,1)S(1)}, s32[3,16]{1,0:T(4,128)S(1)}, bf16[4,2,32,128]{3,2,1,0:T(8,128)(2,1)S(1)}) custom-call(s32[3,16]{1,0:T(4,128)} %bitcast.4, bf16[4,2,4096]{2,1,0:T(2,128)(2,1)} %block_hbm.1, bf16[2,512,256]{2,1,0:T(8,128)(2,1)} %fit_ref.1), custom_call_target="tpu_custom_call" | custom-call | flops 134217728 | bytes 524288 | tf_op jit(solution)/shard_map/pack_metric/pallas_call | solution.py:476
  1.8 3.1 %collective-permute-start.1 = (bf16[2,272,128]{2,1,0:T(8,128)(2,1)S(1)}, bf16[2,272,128]{2,1,0:T(8,128)(2,1)S(1)}, u32[]{:S(2)}, u32[]{:S(2)}) collective-permute-start(bf16[2,272,128]{2,1,0:T(8,128)(2,1)S(1)} %get-tuple-element.19.refs_0_), channel_id=1, source_target_pairs={{0,2},{1,3},{2,6},{3,7},{6,4},{7,5},{4,0},{5,1},{8,10},{9,11},{10,... | collective-permute-start | bytes 417800 | tf_op jit(solution)/shard_map/ppermute | solution.py:384
  4.9 1.5 %collective-permute-start.3 = (bf16[4,2,32,128]{3,2,1,0:T(8,128)(2,1)S(1)}, bf16[4,2,32,128]{3,2,1,0:T(8,128)(2,1)S(1)}, u32[]{:S(2)}, u32[]{:S(2)}) collective-permute-start(bf16[4,2,32,128]{3,2,1,0:T(8,128)(2,1)S(1)} %get-tuple-element.20.refs_1_), channel_id=1, source_target_pairs={{0,8},{16,24},{8,0},{24,16},{1,9},{17,25},{9,1},{25,17},{2,10},{18... | collective-permute-start | bytes 196616 | tf_op jit(solution)/shard_map/ppermute | solution.py:349
  6.4 1.3 %collective-permute-start.7 = (bf16[2,272,128]{2,1,0:T(8,128)(2,1)S(1)}, bf16[2,272,128]{2,1,0:T(8,128)(2,1)S(1)}, u32[]{:S(2)}, u32[]{:S(2)}) collective-permute-start(bf16[2,272,128]{2,1,0:T(8,128)(2,1)S(1)} %get-tuple-element.19.refs_0_), channel_id=1, source_target_pairs={{2,0},{3,1},{6,2},{7,3},{4,6},{5,7},{0,4},{1,5},{10,8},{11,9},{14,... | collective-permute-start | bytes 417800 | tf_op jit(solution)/shard_map/ppermute | solution.py:389
  7.7 1.4 %collective-permute-done.3.refs_0_.refs_2_ = bf16[4,2,32,128]{3,2,1,0:T(8,128)(2,1)S(1)} collective-permute-done((bf16[4,2,32,128]{3,2,1,0:T(8,128)(2,1)S(1)}, bf16[4,2,32,128]{3,2,1,0:T(8,128)(2,1)S(1)}, u32[]{:S(2)}, u32[]{:S(2)}) %collective-permute-start.3) | collective-permute-done | bytes 65568 | tf_op jit(solution)/shard_map/ppermute | solution.py:349
  9.1 0.5 %collective-permute-done.1.block_ref.refs_2_ = bf16[2,272,128]{2,1,0:T(8,128)(2,1)S(1)} collective-permute-done((bf16[2,272,128]{2,1,0:T(8,128)(2,1)S(1)}, bf16[2,272,128]{2,1,0:T(8,128)(2,1)S(1)}, u32[]{:S(2)}, u32[]{:S(2)}) %collective-permute-start.1) | collective-permute-done | bytes 139296 | tf_op jit(solution)/shard_map/ppermute | solution.py:384
  9.6 3.8 %collective-permute-start.4 = (bf16[2,272,128]{2,1,0:T(8,128)(2,1)S(1)}, bf16[2,272,128]{2,1,0:T(8,128)(2,1)S(1)}, u32[]{:S(2)}, u32[]{:S(2)}) collective-permute-start(bf16[2,272,128]{2,1,0:T(8,128)(2,1)S(1)} %after_others.2), channel_id=1, source_target_pairs={{0,2},{1,3},{2,6},{3,7},{6,4},{7,5},{4,0},{5,1},{8,10},{9,11},{10,... | collective-permute-start | bytes 417800 | tf_op jit(solution)/shard_map/ppermute | solution.py:384
  13.4 1.5 %collective-permute-start.5 = (bf16[4,2,32,128]{3,2,1,0:T(8,128)(2,1)S(1)}, bf16[4,2,32,128]{3,2,1,0:T(8,128)(2,1)S(1)}, u32[]{:S(2)}, u32[]{:S(2)}) collective-permute-start(bf16[4,2,32,128]{3,2,1,0:T(8,128)(2,1)S(1)} %collective-permute-done.3.refs_0_.refs_2_), channel_id=1, source_target_pairs={{0,16},{8,24},{16,0},{24,8},{1,17},{9,25},{17,1},{25,9},{2,18},{10... | collective-permute-start | bytes 196616 | tf_op jit(solution)/shard_map/ppermute | solution.py:352
  15.0 0.0 collective-permute-start
  15.0 2.2 %prepare.1 = (bf16[4,2,3,256,128]{4,3,2,1,0:T(8,128)(2,1)S(1)}, bf16[4,2,3,256,128]{4,3,2,1,0:T(8,128)(2,1)S(1)}, bf16[4,3,128,256]{3,2,1,0:T(8,128)(2,1)S(1)}, bf16[2,3,256,256]{3,2,1,0:T(8,128)(2,1)S(1)}) custom-call(bf16[4,2,6,256,128]{4,3,2,1,0:T(8,128)(2,1)} %coef_hbm.1), custom_call_target="tpu_custom_call" | custom-call | bytes 6291456 | tf_op jit(solution)/shard_map/prepare/pallas_call | solution.py:500
  17.2 0.6 %collective-permute-start.2 = (bf16[2,272,128]{2,1,0:T(8,128)(2,1)S(1)}, bf16[2,272,128]{2,1,0:T(8,128)(2,1)S(1)}, u32[]{:S(2)}, u32[]{:S(2)}) collective-permute-start(bf16[2,272,128]{2,1,0:T(8,128)(2,1)S(1)} %collective-permute-done.1.block_ref.refs_2_), channel_id=1, source_target_pairs={{0,1},{1,0},{2,3},{3,2},{4,5},{5,4},{6,7},{7,6},{8,9},{9,8},{10,11... | collective-permute-start | bytes 417800 | tf_op jit(solution)/shard_map/ppermute | solution.py:400
  17.8 0.0 collective-permute-done.7.refs_6_
  17.8 0.1 collective-permute-start.8
  17.9 0.0 collective-permute-done.5.refs_1_.refs_3_
  17.9 0.0 collective-permute-done.4.block_ref
  17.9 0.5 %collective-permute-start.6 = (bf16[2,272,128]{2,1,0:T(8,128)(2,1)S(1)}, bf16[2,272,128]{2,1,0:T(8,128)(2,1)S(1)}, u32[]{:S(2)}, u32[]{:S(2)}) collective-permute-start(bf16[2,272,128]{2,1,0:T(8,128)(2,1)S(1)} %after_others.3.refs_4_), channel_id=1, source_target_pairs={{0,1},{1,0},{2,3},{3,2},{4,5},{5,4},{6,7},{7,6},{8,9},{9,8},{10,11... | collective-permute-start | bytes 417800 | tf_op jit(solution)/shard_map/ppermute | solution.py:400
  18.4 0.0 collective-permute-done.refs_1_
  18.4 0.4 %collective-permute-done.2.refs_3_ = bf16[2,272,128]{2,1,0:T(8,128)(2,1)S(1)} collective-permute-done((bf16[2,272,128]{2,1,0:T(8,128)(2,1)S(1)}, bf16[2,272,128]{2,1,0:T(8,128)(2,1)S(1)}, u32[]{:S(2)}, u32[]{:S(2)}) %collective-permute-start.2) | collective-permute-done | bytes 139296 | tf_op jit(solution)/shard_map/ppermute | solution.py:400
  18.8 0.4 collective-permute-done.8.refs_7_
  19.1 0.2 collective-permute-done.6.refs_5_
  19.4 0.8 %select_column_atoms.1 = (bf16[6,272,128]{2,1,0:T(8,128)(2,1)S(1)}, bf16[16,272,128]{2,1,0:T(8,128)(2,1)S(1)}) custom-call(s32[3,16]{1,0:T(4,128)S(1)} %get-tuple-element.16.atoms_ref, bf16[2,272,128]{2,1,0:T(8,128)(2,1)S(1)} %get-tuple-element.19.refs_0_, bf16[2,272,128]{2,1,0:T(8,128)(2,1)S(1)} %collective-permute-done.refs_1_, ...), custom_call_target="tpu_custom_call" | custom-call | bytes 5292032 | tf_op jit(solution)/shard_map/select_column_atoms/pallas_call | solution.py:519
  20.2 1.6 %collective-permute-start.11 = (bf16[6,272,128]{2,1,0:T(8,128)(2,1)S(1)}, bf16[6,272,128]{2,1,0:T(8,128)(2,1)S(1)}, u32[]{:S(2)}, u32[]{:S(2)}) collective-permute-start(bf16[6,272,128]{2,1,0:T(8,128)(2,1)S(1)} %get-tuple-element.22.kept_ref), channel_id=1, source_target_pairs={{0,8},{8,0},{16,24},{24,16},{2,10},{10,2},{18,26},{26,18},{4,12},{... | collective-permute-start | bytes 1253384 | tf_op jit(solution)/shard_map/ppermute | solution.py:420
  21.8 0.0 collective-permute-start.9
  21.8 0.7 %collective-permute-start.10 = (bf16[4,2,32,128]{3,2,1,0:T(8,128)(2,1)S(1)}, bf16[4,2,32,128]{3,2,1,0:T(8,128)(2,1)S(1)}, u32[]{:S(2)}, u32[]{:S(2)}) collective-permute-start(bf16[4,2,32,128]{3,2,1,0:T(8,128)(2,1)S(1)} %get-tuple-element.20.refs_1_), channel_id=1, source_target_pairs={{1,2},{3,4},{5,6},{2,1},{4,3},{6,5},{0,0},{7,7},{9,10},{11,12},{13... | collective-permute-start | bytes 196616 | tf_op jit(solution)/shard_map/ppermute | solution.py:354
  22.4 3.1 %row_exchange.1.refs_0_ = f32[4,2,64,64]{3,2,1,0:T(8,128)S(1)} custom-call(s32[3,16]{1,0:T(4,128)S(1)} %get-tuple-element.16.atoms_ref, bf16[4,2,3,256,128]{4,3,2,1,0:T(8,128)(2,1)S(1)} %get-tuple-element.17.coef_ref, bf16[4,3,128,256]{3,2,1,0:T(8,128)(2,1)S(1)} %get-tuple-element.18.refs_0_.turned_ref, bf16[16,272,128]{2,1,0:T(8,128)(2,1)S(1)} %get-tuple-element.21.all_ref), custom_call_target="tpu_custom_call" | custom-call | flops 251658240 | bytes 1572864 | tf_op jit(solution)/shard_map/row_exchange/pallas_call | solution.py:529
  25.5 0.0 collective-permute-done.9.refs_4_.refs_1_
  25.5 0.0 collective-permute-done.10.refs_5_.refs_2_
  25.5 2.8 %collective-permute-done.11.got_ref = bf16[6,272,128]{2,1,0:T(8,128)(2,1)S(1)} collective-permute-done((bf16[6,272,128]{2,1,0:T(8,128)(2,1)S(1)}, bf16[6,272,128]{2,1,0:T(8,128)(2,1)S(1)}, u32[]{:S(2)}, u32[]{:S(2)}) %collective-permute-start.11) | collective-permute-done | bytes 417824 | tf_op jit(solution)/shard_map/ppermute | solution.py:420
  28.3 1.3 %collective-permute-start.12 = (bf16[6,272,128]{2,1,0:T(8,128)(2,1)S(1)}, bf16[6,272,128]{2,1,0:T(8,128)(2,1)S(1)}, u32[]{:S(2)}, u32[]{:S(2)}) collective-permute-start(bf16[6,272,128]{2,1,0:T(8,128)(2,1)S(1)} %merge.1.held_ref), channel_id=1, source_target_pairs={{0,16},{8,24},{16,0},{24,8},{2,18},{10,26},{18,2},{26,10},{4,20},{... | collective-permute-start | bytes 1253384 | tf_op jit(solution)/shard_map/ppermute | solution.py:420
  29.7 4.3 %couple.1.base_ref = f32[4,2,64,64]{3,2,1,0:T(8,128)S(1)} custom-call(s32[4,16]{1,0:T(4,128)} %bitcast.5, f32[4,16]{1,0:T(4,128)} %bitcast.6, f32[16]{0:T(128)} %occupied_hbm.1, f32[4,2,64]{2,1,0:T(2,128)} %virtual_hbm.1, bf16[4,2,8,4096]{3,2,1,0:T(8,128)(2,1)} %inter_hbm.1, f32[4,2,64,64]{3,2,1,0:T(8,128)S(1)} %row_exchange.1.refs_0_, ...), custom_call_target="tpu_custom_call" | custom-call | flops 67108864 | bytes 1048576 | tf_op jit(solution)/shard_map/couple/pallas_call | solution.py:543
  34.0 2.4 %collective-permute-done.12.got_ref = bf16[6,272,128]{2,1,0:T(8,128)(2,1)S(1)} collective-permute-done((bf16[6,272,128]{2,1,0:T(8,128)(2,1)S(1)}, bf16[6,272,128]{2,1,0:T(8,128)(2,1)S(1)}, u32[]{:S(2)}, u32[]{:S(2)}) %collective-permute-start.12) | collective-permute-done | bytes 417824 | tf_op jit(solution)/shard_map/ppermute | solution.py:420
  36.4 1.9 %column_exchange.1 = f32[4,2,4096]{2,1,0:T(2,128)} custom-call(s32[2,4]{1,0:T(2,128)} %bitcast.7, bf16[4,2,3,256,128]{4,3,2,1,0:T(8,128)(2,1)S(1)} %get-tuple-element.14.coef_ref, bf16[2,3,256,256]{3,2,1,0:T(8,128)(2,1)S(1)} %get-tuple-element.15.turned_ref, f32[4,2,64,64]{3,2,1,0:T(8,128)S(1)} %couple.1.base_ref, bf16[6,272,128]{2,1,0:T(8,128)(2,1)S(1)} %merge.1.held_ref, ...), custom_call_target="tpu_custom_call" | custom-call | flops 251658240 | bytes 1572864 | tf_op jit(solution)/shard_map/column_exchange/pallas_call | solution.py:566
  (3 shorter events, 0.0 us)
Async XLA Ops:
  1.8 7.8 %collective-permute-start.1 = (bf16[2,272,128]{2,1,0:T(8,128)(2,1)S(1)}, bf16[2,272,128]{2,1,0:T(8,128)(2,1)S(1)}, u32[]{:S(2)}, u32[]{:S(2)}) collective-permute-start(bf16[2,272,128]{2,1,0:T(8,128)(2,1)S(1)} %get-tuple-element.19.refs_0_), channel_id=1, source_target_pairs={{0,2},{1,3},{2,6},{3,7},{6,4},{7,5},{4,0},{5,1},{8,10},{9,11},{10,... | collective-permute-start | bytes 417800 | tf_op jit(solution)/shard_map/ppermute | solution.py:384
  4.9 4.3 %collective-permute-start.3 = (bf16[4,2,32,128]{3,2,1,0:T(8,128)(2,1)S(1)}, bf16[4,2,32,128]{3,2,1,0:T(8,128)(2,1)S(1)}, u32[]{:S(2)}, u32[]{:S(2)}) collective-permute-start(bf16[4,2,32,128]{3,2,1,0:T(8,128)(2,1)S(1)} %get-tuple-element.20.refs_1_), channel_id=1, source_target_pairs={{0,8},{16,24},{8,0},{24,16},{1,9},{17,25},{9,1},{25,17},{2,10},{18... | collective-permute-start | bytes 196616 | tf_op jit(solution)/shard_map/ppermute | solution.py:349
  6.4 11.4 %collective-permute-start.7 = (bf16[2,272,128]{2,1,0:T(8,128)(2,1)S(1)}, bf16[2,272,128]{2,1,0:T(8,128)(2,1)S(1)}, u32[]{:S(2)}, u32[]{:S(2)}) collective-permute-start(bf16[2,272,128]{2,1,0:T(8,128)(2,1)S(1)} %get-tuple-element.19.refs_0_), channel_id=1, source_target_pairs={{2,0},{3,1},{6,2},{7,3},{4,6},{5,7},{0,4},{1,5},{10,8},{11,9},{14,... | collective-permute-start | bytes 417800 | tf_op jit(solution)/shard_map/ppermute | solution.py:389
  9.6 8.3 %collective-permute-start.4 = (bf16[2,272,128]{2,1,0:T(8,128)(2,1)S(1)}, bf16[2,272,128]{2,1,0:T(8,128)(2,1)S(1)}, u32[]{:S(2)}, u32[]{:S(2)}) collective-permute-start(bf16[2,272,128]{2,1,0:T(8,128)(2,1)S(1)} %after_others.2), channel_id=1, source_target_pairs={{0,2},{1,3},{2,6},{3,7},{6,4},{7,5},{4,0},{5,1},{8,10},{9,11},{10,... | collective-permute-start | bytes 417800 | tf_op jit(solution)/shard_map/ppermute | solution.py:384
  13.4 4.4 %collective-permute-start.5 = (bf16[4,2,32,128]{3,2,1,0:T(8,128)(2,1)S(1)}, bf16[4,2,32,128]{3,2,1,0:T(8,128)(2,1)S(1)}, u32[]{:S(2)}, u32[]{:S(2)}) collective-permute-start(bf16[4,2,32,128]{3,2,1,0:T(8,128)(2,1)S(1)} %collective-permute-done.3.refs_0_.refs_2_), channel_id=1, source_target_pairs={{0,16},{8,24},{16,0},{24,8},{1,17},{9,25},{17,1},{25,9},{2,18},{10... | collective-permute-start | bytes 196616 | tf_op jit(solution)/shard_map/ppermute | solution.py:352
  15.0 3.4 %collective-permute-start = (bf16[2,272,128]{2,1,0:T(8,128)(2,1)S(1)}, bf16[2,272,128]{2,1,0:T(8,128)(2,1)S(1)}, u32[]{:S(2)}, u32[]{:S(2)}) collective-permute-start(bf16[2,272,128]{2,1,0:T(8,128)(2,1)S(1)} %get-tuple-element.19.refs_0_), channel_id=1, source_target_pairs={{0,1},{1,0},{2,3},{3,2},{4,5},{5,4},{6,7},{7,6},{8,9},{9,8},{10,11... | collective-permute-start | bytes 417800 | tf_op jit(solution)/shard_map/ppermute | solution.py:400
  17.2 1.6 %collective-permute-start.2 = (bf16[2,272,128]{2,1,0:T(8,128)(2,1)S(1)}, bf16[2,272,128]{2,1,0:T(8,128)(2,1)S(1)}, u32[]{:S(2)}, u32[]{:S(2)}) collective-permute-start(bf16[2,272,128]{2,1,0:T(8,128)(2,1)S(1)} %collective-permute-done.1.block_ref.refs_2_), channel_id=1, source_target_pairs={{0,1},{1,0},{2,3},{3,2},{4,5},{5,4},{6,7},{7,6},{8,9},{9,8},{10,11... | collective-permute-start | bytes 417800 | tf_op jit(solution)/shard_map/ppermute | solution.py:400
  17.8 1.4 %collective-permute-start.8 = (bf16[2,272,128]{2,1,0:T(8,128)(2,1)S(1)}, bf16[2,272,128]{2,1,0:T(8,128)(2,1)S(1)}, u32[]{:S(2)}, u32[]{:S(2)}) collective-permute-start(bf16[2,272,128]{2,1,0:T(8,128)(2,1)S(1)} %collective-permute-done.7.refs_6_), channel_id=1, source_target_pairs={{0,1},{1,0},{2,3},{3,2},{4,5},{5,4},{6,7},{7,6},{8,9},{9,8},{10,11... | collective-permute-start | bytes 417800 | tf_op jit(solution)/shard_map/ppermute | solution.py:400
  17.9 1.5 %collective-permute-start.6 = (bf16[2,272,128]{2,1,0:T(8,128)(2,1)S(1)}, bf16[2,272,128]{2,1,0:T(8,128)(2,1)S(1)}, u32[]{:S(2)}, u32[]{:S(2)}) collective-permute-start(bf16[2,272,128]{2,1,0:T(8,128)(2,1)S(1)} %after_others.3.refs_4_), channel_id=1, source_target_pairs={{0,1},{1,0},{2,3},{3,2},{4,5},{5,4},{6,7},{7,6},{8,9},{9,8},{10,11... | collective-permute-start | bytes 417800 | tf_op jit(solution)/shard_map/ppermute | solution.py:400
  20.2 8.1 %collective-permute-start.11 = (bf16[6,272,128]{2,1,0:T(8,128)(2,1)S(1)}, bf16[6,272,128]{2,1,0:T(8,128)(2,1)S(1)}, u32[]{:S(2)}, u32[]{:S(2)}) collective-permute-start(bf16[6,272,128]{2,1,0:T(8,128)(2,1)S(1)} %get-tuple-element.22.kept_ref), channel_id=1, source_target_pairs={{0,8},{8,0},{16,24},{24,16},{2,10},{10,2},{18,26},{26,18},{4,12},{... | collective-permute-start | bytes 1253384 | tf_op jit(solution)/shard_map/ppermute | solution.py:420
  21.8 3.8 %collective-permute-start.9 = (bf16[4,2,32,128]{3,2,1,0:T(8,128)(2,1)S(1)}, bf16[4,2,32,128]{3,2,1,0:T(8,128)(2,1)S(1)}, u32[]{:S(2)}, u32[]{:S(2)}) collective-permute-start(bf16[4,2,32,128]{3,2,1,0:T(8,128)(2,1)S(1)} %get-tuple-element.20.refs_1_), channel_id=1, source_target_pairs={{0,1},{2,3},{4,5},{6,7},{1,0},{3,2},{5,4},{7,6},{8,9},{10,11},{12,... | collective-permute-start | bytes 196616 | tf_op jit(solution)/shard_map/ppermute | solution.py:349
  21.8 3.8 %collective-permute-start.10 = (bf16[4,2,32,128]{3,2,1,0:T(8,128)(2,1)S(1)}, bf16[4,2,32,128]{3,2,1,0:T(8,128)(2,1)S(1)}, u32[]{:S(2)}, u32[]{:S(2)}) collective-permute-start(bf16[4,2,32,128]{3,2,1,0:T(8,128)(2,1)S(1)} %get-tuple-element.20.refs_1_), channel_id=1, source_target_pairs={{1,2},{3,4},{5,6},{2,1},{4,3},{6,5},{0,0},{7,7},{9,10},{11,12},{13... | collective-permute-start | bytes 196616 | tf_op jit(solution)/shard_map/ppermute | solution.py:354
  28.3 8.1 %collective-permute-start.12 = (bf16[6,272,128]{2,1,0:T(8,128)(2,1)S(1)}, bf16[6,272,128]{2,1,0:T(8,128)(2,1)S(1)}, u32[]{:S(2)}, u32[]{:S(2)}) collective-permute-start(bf16[6,272,128]{2,1,0:T(8,128)(2,1)S(1)} %merge.1.held_ref), channel_id=1, source_target_pairs={{0,16},{8,24},{16,0},{24,8},{2,18},{10,26},{18,2},{26,10},{4,20},{... | collective-permute-start | bytes 1253384 | tf_op jit(solution)/shard_map/ppermute | solution.py:420

commit v5 on v4

--- a/solution.py
+++ b/solution.py
@@ -57,8 +57,9 @@
     for i in range(row_count):
         for j in range(column_count):
             lines_ref[i, j] = flat_ref[i, :, j, :].astype(BF16)
+    for fetch in fetches:
+        fetch.wait()
     for atom in range(held):
-        fetches[atom].wait()
         fit = fits_ref[atom]
         metric = lax.dot_general(fit, fit, (((0,), (0,)), ((), ())), preferred_element_type=F32)
         first, second = metric[:half, :half], metric[half:, half:]
@@ -134,14 +135,13 @@
     return jnp.where(turn == 0, 0, jnp.where((place + turn) == jnp.bitwise_xor(place, 1), 1, 2))
 
 
-def couple_kernel(partner_hbm, value_hbm, occupied_hbm, virtual_hbm, inter_hbm, *refs):
+def couple_kernel(scale, partner_hbm, value_hbm, occupied_hbm, virtual_hbm, kept_hbm, inter_hbm, *refs):
     exchange_ref, blocks = refs[0], refs[1:6]
-    base_ref, flat_ref, wide_ref, mats_ref, inters_ref, inter_ref = refs[6:12]
-    partner_ref, value_ref, occupied_ref, virtual_ref, sems, inter_sems = refs[12:]
+    base_ref, factor_ref, flat_ref, wide_ref, mats_ref, inters_ref, inter_ref = refs[6:13]
+    partner_ref, value_ref, occupied_ref, virtual_ref, kept_ref, sems, inter_sems = refs[13:]
     row_count, column_count, terms, size = inter_ref.shape
-    npno = base_ref.shape[2]
-    lanes = 2 * npno
-    chunks = size // lanes
+    chunks, lanes = base_ref.shape[2:]
+    npno = lanes // 2
     partners = terms // 2
     row_place, col_place = lax.axis_index("row"), lax.axis_index("col")
     first_row = row_place * row_count
@@ -154,6 +154,7 @@
                 (value_hbm, value_ref),
                 (occupied_hbm, occupied_ref),
                 (virtual_hbm, virtual_ref),
+                (kept_hbm, kept_ref),
             ]
         )
     ]
@@ -180,6 +181,11 @@
         lax.fori_loop(0, row_count, one_block, 0)
     for fetch in fetches:
         fetch.wait()
+
+    place = lax.broadcasted_iota(jnp.int32, (chunks, lanes), 0)
+    lane = lax.broadcasted_iota(jnp.int32, (chunks, lanes), 1)
+    first = 2 * place + jnp.where(lane < npno, 0, 1)
+    second = jnp.where(lane < npno, lane, lane - npno)
 
     def one_row(i, carry):
         fetch_inter(i).wait()
@@ -210,7 +216,13 @@
                 total = total + weight * dot(half, turned[n])
             levels = jnp.broadcast_to(virtual_ref[i, pl.ds(j, 1)], (npno, npno))
             shift = levels + levels.T - occupied_ref[first_row + i] - occupied_ref[first_col + j]
-            base_ref[i, j] = exchange_ref[i, j] + shift * mats_ref[i, j].astype(F32) - total
+            result = exchange_ref[i, j] + shift * mats_ref[i, j].astype(F32) - total
+            wide_ref[:, :npno] = result
+            even = wide_ref[pl.ds(0, chunks, 2), :]
+            odd = pltpu.roll(wide_ref[pl.ds(1, chunks, 2), :], npno, 1)
+            keep = (first < kept_ref[j, i]) & (second < kept_ref[j, i])
+            base_ref[i, j] = jnp.where(keep, jnp.where(lane < npno, even, odd), 0.0)
+            factor_ref[i, j] = jnp.where(keep, scale, 0.0)
         return carry
 
     lax.fori_loop(0, row_count, one_row, 0)
@@ -288,41 +300,38 @@
 
 
 def column_kernel(
-    takers, scale, kept_hbm, coef_ref, turned_ref, base_ref, held_ref, got_ref,
-    out_ref, packed_ref, metric_ref, wide_ref, flat_ref, kept_ref, kept_sem,
+    takers, coef_ref, turned_ref, base_ref, factor_ref, held_ref, got_ref,
+    out_hbm, packed_ref, metric_ref, wide_ref, flat_ref, out_ref, sems,
 ):
-    row_count, column_count, domain = coef_ref.shape[:3]
-    npno = base_ref.shape[2]
-    lanes = 2 * npno
-    kept_copy = pltpu.make_async_copy(kept_hbm, kept_ref, kept_sem)
-    kept_copy.start()
+    row_count, column_count, domain, pao, lanes = coef_ref.shape
+    npno = lanes // 2
+    chunks = npno // 2
     merge_into(takers, column_count, row_count, held_ref, got_ref, packed_ref)
     slots = column_count * domain
     lows = [unpack(packed_ref[index], metric_ref.at[index]) for index in range(slots)]
     products = []
-    for index in range(slots):
-        left = turned_ref[index // domain, index % domain]
-        product = dot(left, metric_ref[index]) + left.astype(F32) * lows[index]
-        products.append(product.astype(BF16))
-    kept_copy.wait()
-    row, col = square_iota(npno)
-    lane = lax.broadcasted_iota(jnp.int32, (npno // 2, lanes), 1)
     for j in range(column_count):
-        for i in range(row_count):
-            total = None
-            for s in range(domain):
-                part = dot(products[j * domain + s][i * npno : (i + 1) * npno], coef_ref[i, j, s])
-                total = part if total is None else total + part
-            result = base_ref[i, j] + total[:, npno:] * scale
-            kept = kept_ref[j, i]
-            result = jnp.where((row < kept) & (col < kept), result, 0.0)
-            wide_ref[i, j, :, :npno] = result
-            even = wide_ref[i, j, pl.ds(0, npno // 2, 2), :]
-            odd = wide_ref[i, j, pl.ds(1, npno // 2, 2), :]
-            flat_ref[i, j] = jnp.where(lane < npno, even, pltpu.roll(odd, npno, 1))
+        parts = []
+        for s in range(domain):
+            left = turned_ref[j, s]
+            part = dot(left, metric_ref[j * domain + s]) + left.astype(F32) * lows[j * domain + s]
+            parts.append(part.astype(BF16))
+        products.append(jnp.concatenate(parts, axis=1))
+    lane = lax.broadcasted_iota(jnp.int32, (chunks, lanes), 1)
     for i in range(row_count):
-        for q in range(npno // 2):
+        for j in range(column_count):
+            wide_ref[i, j] = dot(
+                products[j][i * npno : (i + 1) * npno], coef_ref[i, j].reshape(domain * pao, lanes)
+            )
+            even = wide_ref[i, j, pl.ds(0, chunks, 2), :]
+            odd = wide_ref[i, j, pl.ds(1, chunks, 2), :]
+            total = jnp.where(lane < npno, pltpu.roll(even, npno, 1), odd)
+            flat_ref[i, j] = base_ref[i, j] + factor_ref[i, j] * total
+        for q in range(chunks):
             out_ref[i, :, q * lanes : (q + 1) * lanes] = flat_ref[i, :, q, :]
+        pltpu.make_async_copy(out_ref.at[i], out_hbm.at[i], sems.at[i]).start()
+    for i in range(row_count):
+        pltpu.make_async_copy(out_ref.at[i], out_hbm.at[i], sems.at[i]).wait()
 
 
 def call(kernel, out_shape, in_specs, out_specs, scratch, name, flops, moved):
@@ -349,7 +358,7 @@
     even = lax.ppermute(block, axis, partners_of(size, 0)[1])
     pairs, route = partners_of(size, 1)
     if size % 4 == 0 and axis == "row" and all(a ^ b == 3 for a, b in pairs):
-        odd = lax.ppermute(even, axis, [(n, n ^ 2) for n in range(size)])
+        odd = lax.ppermute(block, axis, [(n, n ^ 3) for n in range(size)])
     else:
         odd = lax.ppermute(block, axis, route)
     return [even, odd]
@@ -512,7 +521,7 @@
         0,
         coefficients.size * 4,
     )(coefs)
-    buffers = gather_metrics(packed, cores, units, row_halos[:1], [own_turned] + row_halos[1:])
+    buffers = gather_metrics(packed, cores, units, row_halos, [own_turned])
     blocks = [lines] + row_halos + col_halos
     wanted = column_count * domain
     atoms = len(buffers) * held
@@ -540,11 +549,11 @@
     sources = [c * column_count // row_count for c in range(columns)]
     piece, got, takers = spread(piece, sources, column_count, row_count, [exchange] + col_halos)
 
-    base = call(
-        couple_kernel,
-        jax.ShapeDtypeStruct((row_count, column_count, npno, npno), F32),
-        [HBM] * 5 + [VMEM] * (1 + len(blocks)),
-        VMEM,
+    base, factor = call(
+        functools.partial(couple_kernel, scale),
+        (jax.ShapeDtypeStruct((row_count, column_count, chunks, lanes), F32),) * 2,
+        [HBM] * 6 + [VMEM] * (1 + len(blocks)),
+        (VMEM,) * 2,
         [
             pltpu.VMEM((chunks, terms, lanes), F32),
             pltpu.VMEM((npno, lanes), F32),
@@ -555,31 +564,32 @@
             pltpu.SMEM(fock_value.shape[::-1], F32),
             pltpu.SMEM(occupied_energy.shape, F32),
             pltpu.VMEM(virtual_energy.shape, F32),
-            pltpu.SemaphoreType.DMA((4,)),
+            pltpu.SMEM(kept_count.shape[::-1], jnp.int32),
+            pltpu.SemaphoreType.DMA((5,)),
             pltpu.SemaphoreType.DMA((row_count,)),
         ],
         "couple",
         4 * row_count * column_count * terms * npno**3,
         intersections.size * 4,
-    )(partner, value, occupied, virtual, inter, exchange, *blocks)
+    )(partner, value, occupied, virtual, kept, inter, exchange, *blocks)
 
     return call(
-        functools.partial(column_kernel, takers, scale),
+        functools.partial(column_kernel, takers),
         jax.ShapeDtypeStruct(amplitudes.shape, F32),
-        [HBM] + [VMEM] * 5,
-        VMEM,
+        [VMEM] * 6,
+        HBM,
         [
             pltpu.VMEM((wanted, depth, half), BF16),
             pltpu.VMEM((wanted, pao, pao), BF16),
             pltpu.VMEM((row_count, column_count, npno, lanes), F32),
             pltpu.VMEM((row_count, column_count, chunks, lanes), F32),
-            pltpu.SMEM(kept_count.shape[::-1], jnp.int32),
-            pltpu.SemaphoreType.DMA(()),
+            pltpu.VMEM(amplitudes.shape, F32),
+            pltpu.SemaphoreType.DMA((row_count,)),
         ],
         "column_exchange",
         2 * row_count * column_count * domain * pao * npno * (pao + npno),
         coefficients.size,
-    )(kept, column_coefficients, turned, base, piece, got)
+    )(column_coefficients, turned, base, factor, piece, got)
 
 
 def solution(mesh):

time: 38.9 us -> 38.3 us (0.985); the launches traced: 38.4 us -> 38.2 us
  starting transfers between devices: 16 us -> 14 us
  waiting for transfers between devices: 8.06 us -> 9.2 us
  Pallas kernels: 14.2 us -> 14.8 us
    ppermute x1, waiting for transfers between devices: 0.01 us -> 2.32 us  [neighbours(): odd = lax.ppermute(block, axis, [(n, n ^ 3) for n in range(size)])]
    ppermute x2, waiting for transfers between devices: 1.43 us -> 0.01 us  [neighbours(): even = lax.ppermute(block, axis, partners_of(size, 0)[1])]
    ppermute x2, starting transfers between devices: 6.9 us -> 5.72 us  [gather_metrics(): up = lax.ppermute(up, 'col', forward)]
    pallas_call x2, Pallas kernels: 6.26 us -> 7.14 us  [the longest x1 5.53 us: on_device(): call(functools.partial(couple_kernel, scale), (jax.ShapeDtypeStruct((row_...]
    ppermute x2, waiting for transfers between devices: 5.16 us -> 4.32 us  [spread(): got = lax.ppermute(piece, ('row', 'col'), pairs)]
    ppermute x2, waiting for transfers between devices: 0.47 us -> 1.23 us  [gather_metrics(): up = lax.ppermute(up, 'col', forward)]
    ppermute x4, starting transfers between devices: 1.15 us -> 0.73 us  [gather_metrics(): buffers.append(lax.ppermute(turn, 'col', swap))]
  transfers between devices with their start and end apart: 13 -> 13, of which waited for: 7 -> 5; matrix products, arithmetic and copies ran while one was open for 0% -> 0% of each run, Pallas kernels for 25% -> 29%
where the time goes in v5:
time: 38.3 us; the launch traced here: 38.2 us
  Pallas kernels  14.8 us (39%)
  starting transfers between devices  14 us (37%)
  waiting for transfers between devices  9.2 us (24%)
    ppermute x2, starting transfers between devices, gather_metrics(): up = lax.ppermute(up, 'col', forward)  5.72 us
    pallas_call x1, Pallas kernels, on_device(): call(functools.partial(couple_kernel, scale), (jax.ShapeDtypeStruct((row_...  5.53 us
    ppermute x2, waiting for transfers between devices, spread(): got = lax.ppermute(piece, ('row', 'col'), pairs)  4.32 us
    pallas_call x1, Pallas kernels, on_device(): call(functools.partial(row_kernel, cores, units, held, scale), jax.ShapeD...  3.1 us
    ppermute x2, starting transfers between devices, spread(): got = lax.ppermute(piece, ('row', 'col'), pairs)  2.57 us
    ppermute x1, waiting for transfers between devices, neighbours(): odd = lax.ppermute(block, axis, [(n, n ^ 3) for n in range(size)])  2.32 us
    pallas_call x1, Pallas kernels, on_device(): call(prepare_kernel, (jax.ShapeDtypeStruct(shape, BF16), jax.ShapeDtypeSt...  2.25 us
    pallas_call x1, Pallas kernels, on_device(): call(functools.partial(column_kernel, takers), jax.ShapeDtypeStruct(ampli...  1.6 us
  transfers between devices with their start and end apart: 13, of which 5 were waited for; matrix products, arithmetic and copies ran while one was open for 0% of the time, Pallas kernels for 29%

profile of v5, /device:TPU:0, one launch (start us, length us, event | category | flops | bytes accessed | tf_op | source)
XLA Modules:
  0.0 38.2 jit_solution(2555462348825550911)
XLA Ops:
  0.0 1.5 %pack_metric.1 = (bf16[2,272,128]{2,1,0:T(8,128)(2,1)S(1)}, s32[3,16]{1,0:T(4,128)S(1)}, bf16[4,2,32,128]{3,2,1,0:T(8,128)(2,1)S(1)}) custom-call(s32[3,16]{1,0:T(4,128)} %bitcast.4, bf16[4,2,4096]{2,1,0:T(2,128)(2,1)} %block_hbm.1, bf16[2,512,256]{2,1,0:T(8,128)(2,1)} %fit_ref.1), custom_call_target="tpu_custom_call" | custom-call | flops 134217728 | bytes 524288 | tf_op jit(solution)/shard_map/pack_metric/pallas_call | solution.py:485
  1.5 3.1 %collective-permute-start.1 = (bf16[2,272,128]{2,1,0:T(8,128)(2,1)S(1)}, bf16[2,272,128]{2,1,0:T(8,128)(2,1)S(1)}, u32[]{:S(2)}, u32[]{:S(2)}) collective-permute-start(bf16[2,272,128]{2,1,0:T(8,128)(2,1)S(1)} %get-tuple-element.21.refs_0_), channel_id=1, source_target_pairs={{0,2},{1,3},{2,6},{3,7},{6,4},{7,5},{4,0},{5,1},{8,10},{9,11},{10,... | collective-permute-start | bytes 417800 | tf_op jit(solution)/shard_map/ppermute | solution.py:393
  4.6 1.5 %collective-permute-start.3 = (bf16[4,2,32,128]{3,2,1,0:T(8,128)(2,1)S(1)}, bf16[4,2,32,128]{3,2,1,0:T(8,128)(2,1)S(1)}, u32[]{:S(2)}, u32[]{:S(2)}) collective-permute-start(bf16[4,2,32,128]{3,2,1,0:T(8,128)(2,1)S(1)} %get-tuple-element.22.refs_1_), channel_id=1, source_target_pairs={{0,8},{16,24},{8,0},{24,16},{1,9},{17,25},{9,1},{25,17},{2,10},{18... | collective-permute-start | bytes 196616 | tf_op jit(solution)/shard_map/ppermute | solution.py:358
  6.1 1.5 %collective-permute-start.4 = (bf16[4,2,32,128]{3,2,1,0:T(8,128)(2,1)S(1)}, bf16[4,2,32,128]{3,2,1,0:T(8,128)(2,1)S(1)}, u32[]{:S(2)}, u32[]{:S(2)}) collective-permute-start(bf16[4,2,32,128]{3,2,1,0:T(8,128)(2,1)S(1)} %get-tuple-element.22.refs_1_), channel_id=1, source_target_pairs={{0,24},{8,16},{16,8},{24,0},{1,25},{9,17},{17,9},{25,1},{2,26},{10... | collective-permute-start | bytes 196616 | tf_op jit(solution)/shard_map/ppermute | solution.py:361
  7.6 1.3 %collective-permute-start.7 = (bf16[2,272,128]{2,1,0:T(8,128)(2,1)S(1)}, bf16[2,272,128]{2,1,0:T(8,128)(2,1)S(1)}, u32[]{:S(2)}, u32[]{:S(2)}) collective-permute-start(bf16[2,272,128]{2,1,0:T(8,128)(2,1)S(1)} %get-tuple-element.21.refs_0_), channel_id=1, source_target_pairs={{2,0},{3,1},{6,2},{7,3},{4,6},{5,7},{0,4},{1,5},{10,8},{11,9},{14,... | collective-permute-start | bytes 417800 | tf_op jit(solution)/shard_map/ppermute | solution.py:398
  8.9 0.0 collective-permute-done.3.refs_0_.refs_2_
  8.9 2.3 %collective-permute-done.4.refs_1_.refs_3_ = bf16[4,2,32,128]{3,2,1,0:T(8,128)(2,1)S(1)} collective-permute-done((bf16[4,2,32,128]{3,2,1,0:T(8,128)(2,1)S(1)}, bf16[4,2,32,128]{3,2,1,0:T(8,128)(2,1)S(1)}, u32[]{:S(2)}, u32[]{:S(2)}) %collective-permute-start.4) | collective-permute-done | bytes 65568 | tf_op jit(solution)/shard_map/ppermute | solution.py:361
  11.2 0.0 collective-permute-done.1.block_ref.refs_2_
  11.3 2.6 %collective-permute-start.5 = (bf16[2,272,128]{2,1,0:T(8,128)(2,1)S(1)}, bf16[2,272,128]{2,1,0:T(8,128)(2,1)S(1)}, u32[]{:S(2)}, u32[]{:S(2)}) collective-permute-start(bf16[2,272,128]{2,1,0:T(8,128)(2,1)S(1)} %after_others.2), channel_id=1, source_target_pairs={{0,2},{1,3},{2,6},{3,7},{6,4},{7,5},{4,0},{5,1},{8,10},{9,11},{10,... | collective-permute-start | bytes 417800 | tf_op jit(solution)/shard_map/ppermute | solution.py:393
  13.9 0.0 collective-permute-start
  13.9 2.2 %prepare.1 = (bf16[4,2,3,256,128]{4,3,2,1,0:T(8,128)(2,1)S(1)}, bf16[4,2,3,256,128]{4,3,2,1,0:T(8,128)(2,1)S(1)}, bf16[4,3,128,256]{3,2,1,0:T(8,128)(2,1)S(1)}, bf16[2,3,256,256]{3,2,1,0:T(8,128)(2,1)S(1)}) custom-call(bf16[4,2,6,256,128]{4,3,2,1,0:T(8,128)(2,1)} %coef_hbm.1), custom_call_target="tpu_custom_call" | custom-call | bytes 6291456 | tf_op jit(solution)/shard_map/prepare/pallas_call | solution.py:509
  16.2 0.6 %collective-permute-start.2 = (bf16[2,272,128]{2,1,0:T(8,128)(2,1)S(1)}, bf16[2,272,128]{2,1,0:T(8,128)(2,1)S(1)}, u32[]{:S(2)}, u32[]{:S(2)}) collective-permute-start(bf16[2,272,128]{2,1,0:T(8,128)(2,1)S(1)} %collective-permute-done.1.block_ref.refs_2_), channel_id=1, source_target_pairs={{0,1},{1,0},{2,3},{3,2},{4,5},{5,4},{6,7},{7,6},{8,9},{9,8},{10,11... | collective-permute-start | bytes 417800 | tf_op jit(solution)/shard_map/ppermute | solution.py:409
  16.7 0.0 collective-permute-done.7.refs_6_
  16.7 0.1 collective-permute-start.8
  16.8 1.2 %collective-permute-done.5.block_ref = bf16[2,272,128]{2,1,0:T(8,128)(2,1)S(1)} collective-permute-done((bf16[2,272,128]{2,1,0:T(8,128)(2,1)S(1)}, bf16[2,272,128]{2,1,0:T(8,128)(2,1)S(1)}, u32[]{:S(2)}, u32[]{:S(2)}) %collective-permute-start.5) | collective-permute-done | bytes 139296 | tf_op jit(solution)/shard_map/ppermute | solution.py:393
  18.1 0.1 collective-permute-start.6
  18.1 0.0 collective-permute-done.refs_1_
  18.2 0.0 collective-permute-done.2.refs_3_
  18.2 0.0 collective-permute-done.8.refs_7_
  18.2 1.3 %collective-permute-done.6.refs_5_ = bf16[2,272,128]{2,1,0:T(8,128)(2,1)S(1)} collective-permute-done((bf16[2,272,128]{2,1,0:T(8,128)(2,1)S(1)}, bf16[2,272,128]{2,1,0:T(8,128)(2,1)S(1)}, u32[]{:S(2)}, u32[]{:S(2)}) %collective-permute-start.6) | collective-permute-done | bytes 139296 | tf_op jit(solution)/shard_map/ppermute | solution.py:409
  19.5 0.8 %select_column_atoms.1 = (bf16[6,272,128]{2,1,0:T(8,128)(2,1)S(1)}, bf16[16,272,128]{2,1,0:T(8,128)(2,1)S(1)}) custom-call(s32[3,16]{1,0:T(4,128)S(1)} %get-tuple-element.18.atoms_ref, bf16[2,272,128]{2,1,0:T(8,128)(2,1)S(1)} %get-tuple-element.21.refs_0_, bf16[2,272,128]{2,1,0:T(8,128)(2,1)S(1)} %collective-permute-done.refs_1_, ...), custom_call_target="tpu_custom_call" | custom-call | bytes 5292032 | tf_op jit(solution)/shard_map/select_column_atoms/pallas_call | solution.py:528
  20.3 1.6 %collective-permute-start.11 = (bf16[6,272,128]{2,1,0:T(8,128)(2,1)S(1)}, bf16[6,272,128]{2,1,0:T(8,128)(2,1)S(1)}, u32[]{:S(2)}, u32[]{:S(2)}) collective-permute-start(bf16[6,272,128]{2,1,0:T(8,128)(2,1)S(1)} %get-tuple-element.26.kept_ref), channel_id=1, source_target_pairs={{0,8},{8,0},{16,24},{24,16},{2,10},{10,2},{18,26},{26,18},{4,12},{... | collective-permute-start | bytes 1253384 | tf_op jit(solution)/shard_map/ppermute | solution.py:429
  21.9 0.0 collective-permute-start.9
  21.9 0.7 %collective-permute-start.10 = (bf16[4,2,32,128]{3,2,1,0:T(8,128)(2,1)S(1)}, bf16[4,2,32,128]{3,2,1,0:T(8,128)(2,1)S(1)}, u32[]{:S(2)}, u32[]{:S(2)}) collective-permute-start(bf16[4,2,32,128]{3,2,1,0:T(8,128)(2,1)S(1)} %get-tuple-element.22.refs_1_), channel_id=1, source_target_pairs={{1,2},{3,4},{5,6},{2,1},{4,3},{6,5},{0,0},{7,7},{9,10},{11,12},{13... | collective-permute-start | bytes 196616 | tf_op jit(solution)/shard_map/ppermute | solution.py:363
  22.5 3.1 %row_exchange.1.refs_0_ = f32[4,2,64,64]{3,2,1,0:T(8,128)S(1)} custom-call(s32[3,16]{1,0:T(4,128)S(1)} %get-tuple-element.18.atoms_ref, bf16[4,2,3,256,128]{4,3,2,1,0:T(8,128)(2,1)S(1)} %get-tuple-element.19.coef_ref, bf16[4,3,128,256]{3,2,1,0:T(8,128)(2,1)S(1)} %get-tuple-element.20.refs_0_.turned_ref, bf16[16,272,128]{2,1,0:T(8,128)(2,1)S(1)} %get-tuple-element.23.all_ref), custom_call_target="tpu_custom_call" | custom-call | flops 251658240 | bytes 1572864 | tf_op jit(solution)/shard_map/row_exchange/pallas_call | solution.py:538
  25.6 0.0 collective-permute-done.9.refs_4_.refs_1_
  25.6 0.0 collective-permute-done.10.refs_5_.refs_2_
  25.6 2.8 %collective-permute-done.11.got_ref = bf16[6,272,128]{2,1,0:T(8,128)(2,1)S(1)} collective-permute-done((bf16[6,272,128]{2,1,0:T(8,128)(2,1)S(1)}, bf16[6,272,128]{2,1,0:T(8,128)(2,1)S(1)}, u32[]{:S(2)}, u32[]{:S(2)}) %collective-permute-start.11) | collective-permute-done | bytes 417824 | tf_op jit(solution)/shard_map/ppermute | solution.py:429
  28.4 1.0 %collective-permute-start.12 = (bf16[6,272,128]{2,1,0:T(8,128)(2,1)S(1)}, bf16[6,272,128]{2,1,0:T(8,128)(2,1)S(1)}, u32[]{:S(2)}, u32[]{:S(2)}) collective-permute-start(bf16[6,272,128]{2,1,0:T(8,128)(2,1)S(1)} %merge.1.held_ref), channel_id=1, source_target_pairs={{0,16},{8,24},{16,0},{24,8},{2,18},{10,26},{18,2},{26,10},{4,20},{... | collective-permute-start | bytes 1253384 | tf_op jit(solution)/shard_map/ppermute | solution.py:429
  29.5 5.5 %couple.1 = (f32[4,2,32,128]{3,2,1,0:T(8,128)S(1)}, f32[4,2,32,128]{3,2,1,0:T(8,128)S(1)}) custom-call(s32[4,16]{1,0:T(4,128)} %bitcast.5, f32[4,16]{1,0:T(4,128)} %bitcast.6, f32[16]{0:T(128)} %occupied_hbm.1, f32[4,2,64]{2,1,0:T(2,128)} %virtual_hbm.1, s32[2,4]{1,0:T(2,128)} %bitcast.7, bf16[4,2,8,4096]{3,2,1,0:T(8,128)(2,1)} %inter_hbm.1, ...), custom_call_target="tpu_custom_call" | custom-call | flops 67108864 | bytes 1048576 | tf_op jit(solution)/shard_map/couple/pallas_call | solution.py:552
  35.0 1.6 %collective-permute-done.12.got_ref = bf16[6,272,128]{2,1,0:T(8,128)(2,1)S(1)} collective-permute-done((bf16[6,272,128]{2,1,0:T(8,128)(2,1)S(1)}, bf16[6,272,128]{2,1,0:T(8,128)(2,1)S(1)}, u32[]{:S(2)}, u32[]{:S(2)}) %collective-permute-start.12) | collective-permute-done | bytes 417824 | tf_op jit(solution)/shard_map/ppermute | solution.py:429
  36.5 1.6 %column_exchange.1 = f32[4,2,4096]{2,1,0:T(2,128)} custom-call(bf16[4,2,3,256,128]{4,3,2,1,0:T(8,128)(2,1)S(1)} %get-tuple-element.16.coef_ref, bf16[2,3,256,256]{3,2,1,0:T(8,128)(2,1)S(1)} %get-tuple-element.17.turned_ref, f32[4,2,32,128]{3,2,1,0:T(8,128)S(1)} %get-tuple-element.24.base_ref, f32[4,2,32,128]{3,2,1,0:T(8,128)S(1)} %get-tuple-element.25.factor_ref, ...), custom_call_target="tpu_custom_call" | custom-call | flops 251658240 | bytes 1572864 | tf_op jit(solution)/shard_map/column_exchange/pallas_call | solution.py:576
  (3 shorter events, 0.0 us)
Async XLA Ops:
  1.5 9.7 %collective-permute-start.1 = (bf16[2,272,128]{2,1,0:T(8,128)(2,1)S(1)}, bf16[2,272,128]{2,1,0:T(8,128)(2,1)S(1)}, u32[]{:S(2)}, u32[]{:S(2)}) collective-permute-start(bf16[2,272,128]{2,1,0:T(8,128)(2,1)S(1)} %get-tuple-element.21.refs_0_), channel_id=1, source_target_pairs={{0,2},{1,3},{2,6},{3,7},{6,4},{7,5},{4,0},{5,1},{8,10},{9,11},{10,... | collective-permute-start | bytes 417800 | tf_op jit(solution)/shard_map/ppermute | solution.py:393
  4.6 4.3 %collective-permute-start.3 = (bf16[4,2,32,128]{3,2,1,0:T(8,128)(2,1)S(1)}, bf16[4,2,32,128]{3,2,1,0:T(8,128)(2,1)S(1)}, u32[]{:S(2)}, u32[]{:S(2)}) collective-permute-start(bf16[4,2,32,128]{3,2,1,0:T(8,128)(2,1)S(1)} %get-tuple-element.22.refs_1_), channel_id=1, source_target_pairs={{0,8},{16,24},{8,0},{24,16},{1,9},{17,25},{9,1},{25,17},{2,10},{18... | collective-permute-start | bytes 196616 | tf_op jit(solution)/shard_map/ppermute | solution.py:358
  6.1 5.2 %collective-permute-start.4 = (bf16[4,2,32,128]{3,2,1,0:T(8,128)(2,1)S(1)}, bf16[4,2,32,128]{3,2,1,0:T(8,128)(2,1)S(1)}, u32[]{:S(2)}, u32[]{:S(2)}) collective-permute-start(bf16[4,2,32,128]{3,2,1,0:T(8,128)(2,1)S(1)} %get-tuple-element.22.refs_1_), channel_id=1, source_target_pairs={{0,24},{8,16},{16,8},{24,0},{1,25},{9,17},{17,9},{25,1},{2,26},{10... | collective-permute-start | bytes 196616 | tf_op jit(solution)/shard_map/ppermute | solution.py:361
  7.6 9.2 %collective-permute-start.7 = (bf16[2,272,128]{2,1,0:T(8,128)(2,1)S(1)}, bf16[2,272,128]{2,1,0:T(8,128)(2,1)S(1)}, u32[]{:S(2)}, u32[]{:S(2)}) collective-permute-start(bf16[2,272,128]{2,1,0:T(8,128)(2,1)S(1)} %get-tuple-element.21.refs_0_), channel_id=1, source_target_pairs={{2,0},{3,1},{6,2},{7,3},{4,6},{5,7},{0,4},{1,5},{10,8},{11,9},{14,... | collective-permute-start | bytes 417800 | tf_op jit(solution)/shard_map/ppermute | solution.py:398
  11.3 6.8 %collective-permute-start.5 = (bf16[2,272,128]{2,1,0:T(8,128)(2,1)S(1)}, bf16[2,272,128]{2,1,0:T(8,128)(2,1)S(1)}, u32[]{:S(2)}, u32[]{:S(2)}) collective-permute-start(bf16[2,272,128]{2,1,0:T(8,128)(2,1)S(1)} %after_others.2), channel_id=1, source_target_pairs={{0,2},{1,3},{2,6},{3,7},{6,4},{7,5},{4,0},{5,1},{8,10},{9,11},{10,... | collective-permute-start | bytes 417800 | tf_op jit(solution)/shard_map/ppermute | solution.py:393
  13.9 4.2 %collective-permute-start = (bf16[2,272,128]{2,1,0:T(8,128)(2,1)S(1)}, bf16[2,272,128]{2,1,0:T(8,128)(2,1)S(1)}, u32[]{:S(2)}, u32[]{:S(2)}) collective-permute-start(bf16[2,272,128]{2,1,0:T(8,128)(2,1)S(1)} %get-tuple-element.21.refs_0_), channel_id=1, source_target_pairs={{0,1},{1,0},{2,3},{3,2},{4,5},{5,4},{6,7},{7,6},{8,9},{9,8},{10,11... | collective-permute-start | bytes 417800 | tf_op jit(solution)/shard_map/ppermute | solution.py:409
  16.2 2.0 %collective-permute-start.2 = (bf16[2,272,128]{2,1,0:T(8,128)(2,1)S(1)}, bf16[2,272,128]{2,1,0:T(8,128)(2,1)S(1)}, u32[]{:S(2)}, u32[]{:S(2)}) collective-permute-start(bf16[2,272,128]{2,1,0:T(8,128)(2,1)S(1)} %collective-permute-done.1.block_ref.refs_2_), channel_id=1, source_target_pairs={{0,1},{1,0},{2,3},{3,2},{4,5},{5,4},{6,7},{7,6},{8,9},{9,8},{10,11... | collective-permute-start | bytes 417800 | tf_op jit(solution)/shard_map/ppermute | solution.py:409
  16.7 1.4 %collective-permute-start.8 = (bf16[2,272,128]{2,1,0:T(8,128)(2,1)S(1)}, bf16[2,272,128]{2,1,0:T(8,128)(2,1)S(1)}, u32[]{:S(2)}, u32[]{:S(2)}) collective-permute-start(bf16[2,272,128]{2,1,0:T(8,128)(2,1)S(1)} %collective-permute-done.7.refs_6_), channel_id=1, source_target_pairs={{0,1},{1,0},{2,3},{3,2},{4,5},{5,4},{6,7},{7,6},{8,9},{9,8},{10,11... | collective-permute-start | bytes 417800 | tf_op jit(solution)/shard_map/ppermute | solution.py:409
  18.1 1.4 %collective-permute-start.6 = (bf16[2,272,128]{2,1,0:T(8,128)(2,1)S(1)}, bf16[2,272,128]{2,1,0:T(8,128)(2,1)S(1)}, u32[]{:S(2)}, u32[]{:S(2)}) collective-permute-start(bf16[2,272,128]{2,1,0:T(8,128)(2,1)S(1)} %after_others.3.refs_4_), channel_id=1, source_target_pairs={{0,1},{1,0},{2,3},{3,2},{4,5},{5,4},{6,7},{7,6},{8,9},{9,8},{10,11... | collective-permute-start | bytes 417800 | tf_op jit(solution)/shard_map/ppermute | solution.py:409
  20.3 8.1 %collective-permute-start.11 = (bf16[6,272,128]{2,1,0:T(8,128)(2,1)S(1)}, bf16[6,272,128]{2,1,0:T(8,128)(2,1)S(1)}, u32[]{:S(2)}, u32[]{:S(2)}) collective-permute-start(bf16[6,272,128]{2,1,0:T(8,128)(2,1)S(1)} %get-tuple-element.26.kept_ref), channel_id=1, source_target_pairs={{0,8},{8,0},{16,24},{24,16},{2,10},{10,2},{18,26},{26,18},{4,12},{... | collective-permute-start | bytes 1253384 | tf_op jit(solution)/shard_map/ppermute | solution.py:429
  21.9 3.8 %collective-permute-start.9 = (bf16[4,2,32,128]{3,2,1,0:T(8,128)(2,1)S(1)}, bf16[4,2,32,128]{3,2,1,0:T(8,128)(2,1)S(1)}, u32[]{:S(2)}, u32[]{:S(2)}) collective-permute-start(bf16[4,2,32,128]{3,2,1,0:T(8,128)(2,1)S(1)} %get-tuple-element.22.refs_1_), channel_id=1, source_target_pairs={{0,1},{2,3},{4,5},{6,7},{1,0},{3,2},{5,4},{7,6},{8,9},{10,11},{12,... | collective-permute-start | bytes 196616 | tf_op jit(solution)/shard_map/ppermute | solution.py:358
  21.9 3.8 %collective-permute-start.10 = (bf16[4,2,32,128]{3,2,1,0:T(8,128)(2,1)S(1)}, bf16[4,2,32,128]{3,2,1,0:T(8,128)(2,1)S(1)}, u32[]{:S(2)}, u32[]{:S(2)}) collective-permute-start(bf16[4,2,32,128]{3,2,1,0:T(8,128)(2,1)S(1)} %get-tuple-element.22.refs_1_), channel_id=1, source_target_pairs={{1,2},{3,4},{5,6},{2,1},{4,3},{6,5},{0,0},{7,7},{9,10},{11,12},{13... | collective-permute-start | bytes 196616 | tf_op jit(solution)/shard_map/ppermute | solution.py:363
  28.4 8.1 %collective-permute-start.12 = (bf16[6,272,128]{2,1,0:T(8,128)(2,1)S(1)}, bf16[6,272,128]{2,1,0:T(8,128)(2,1)S(1)}, u32[]{:S(2)}, u32[]{:S(2)}) collective-permute-start(bf16[6,272,128]{2,1,0:T(8,128)(2,1)S(1)} %merge.1.held_ref), channel_id=1, source_target_pairs={{0,16},{8,24},{16,0},{24,8},{2,18},{10,26},{18,2},{26,10},{4,20},{... | collective-permute-start | bytes 1253384 | tf_op jit(solution)/shard_map/ppermute | solution.py:429

commit v6 on v5

--- a/solution.py
+++ b/solution.py
@@ -114,17 +114,16 @@
 
 def select_kernel(cores, units, atoms_ref, *refs):
     count = units * cores
-    buffers, (piece_ref, all_ref) = refs[:count], refs[-2:]
+    buffers, pieces, all_ref = refs[:count], refs[count:-1], refs[-1]
     held = buffers[0].shape[0]
     row_place, col_place = lax.axis_index("row"), lax.axis_index("col")
-    domain = atoms_ref.shape[0]
-    wanted = piece_ref.shape[0]
     for index, buffer in enumerate(buffers):
         all_ref[index * held : (index + 1) * held] = buffer[...]
-    for index in range(wanted):
-        atom = atoms_ref[index % domain, col_place * (wanted // domain) + index // domain]
-        place = pick_place(atom, row_place, col_place, cores, units, held)
-        piece_ref[index] = all_ref[place]
+    for j, piece_ref in enumerate(pieces):
+        for s in range(piece_ref.shape[0]):
+            atom = atoms_ref[s, col_place * len(pieces) + j]
+            place = pick_place(atom, row_place, col_place, cores, units, held)
+            piece_ref[s] = all_ref[place]
 
 
 def pass_kernel(block_ref, *refs):
@@ -135,13 +134,14 @@
     return jnp.where(turn == 0, 0, jnp.where((place + turn) == jnp.bitwise_xor(place, 1), 1, 2))
 
 
-def couple_kernel(scale, partner_hbm, value_hbm, occupied_hbm, virtual_hbm, kept_hbm, inter_hbm, *refs):
+def couple_kernel(
+    partner_hbm, value_hbm, occupied_hbm, virtual_hbm, inter_ref, turned_ref, factor_ref, *refs,
+):
     exchange_ref, blocks = refs[0], refs[1:6]
-    base_ref, factor_ref, flat_ref, wide_ref, mats_ref, inters_ref, inter_ref = refs[6:13]
-    partner_ref, value_ref, occupied_ref, virtual_ref, kept_ref, sems, inter_sems = refs[13:]
-    row_count, column_count, terms, size = inter_ref.shape
+    base_ref, wide_ref, mats_ref = refs[6:9]
+    partner_ref, value_ref, occupied_ref, virtual_ref, sems = refs[9:]
+    row_count, column_count, terms, npno, _ = inter_ref.shape
     chunks, lanes = base_ref.shape[2:]
-    npno = lanes // 2
     partners = terms // 2
     row_place, col_place = lax.axis_index("row"), lax.axis_index("col")
     first_row = row_place * row_count
@@ -154,49 +154,26 @@
                 (value_hbm, value_ref),
                 (occupied_hbm, occupied_ref),
                 (virtual_hbm, virtual_ref),
-                (kept_hbm, kept_ref),
             ]
         )
     ]
-
-    def fetch_inter(i):
-        return pltpu.make_async_copy(inter_hbm.at[i], inter_ref.at[i], inter_sems.at[i])
-
     for fetch in fetches:
         fetch.start()
-    for i in range(row_count):
-        fetch_inter(i).start()
-    def square(lines):
-        wide_ref[pl.ds(0, chunks, 2), :] = lines
-        wide_ref[pl.ds(1, chunks, 2), :] = pltpu.roll(lines, npno, 1)
-        return wide_ref[:, :npno]
 
     for index, block in enumerate(blocks):
-
-        def one_block(i, carry, index=index, block=block):
+        for i in range(row_count):
             for j in range(column_count):
-                mats_ref[index * row_count + i, j] = square(block[i, j].astype(F32)).astype(BF16)
-            return carry
-
-        lax.fori_loop(0, row_count, one_block, 0)
+                lines = block[i, j].astype(F32)
+                wide = wide_ref.at[(i * column_count + j) % wide_ref.shape[0]]
+                wide[pl.ds(0, chunks, 2), :] = lines
+                wide[pl.ds(1, chunks, 2), :] = pltpu.roll(lines, npno, 1)
+                mats_ref[index * row_count + i, j] = wide[:, :npno].astype(BF16)
     for fetch in fetches:
         fetch.wait()
-
-    place = lax.broadcasted_iota(jnp.int32, (chunks, lanes), 0)
     lane = lax.broadcasted_iota(jnp.int32, (chunks, lanes), 1)
-    first = 2 * place + jnp.where(lane < npno, 0, 1)
-    second = jnp.where(lane < npno, lane, lane - npno)
 
     def one_row(i, carry):
-        fetch_inter(i).wait()
-        for j in range(column_count):
-            for q in range(chunks):
-                flat_ref[q] = inter_ref[i, j, :, q * lanes : (q + 1) * lanes].astype(F32)
-            turned = []
-            for n in range(terms):
-                inter = square(flat_ref[:, n, :])
-                inters_ref[n] = inter.astype(BF16)
-                turned.append(inter.T.astype(BF16))
+        for j in range(column_count):
             total = jnp.zeros((npno, npno), F32)
             for n in range(terms):
                 if n < partners:
@@ -212,17 +189,16 @@
                     index = jnp.where(index == 0, 0, index + 2) * row_count + i
                     weight = value_ref[n - partners, first_col + j]
                     partner = mats_ref[index, away % column_count]
-                half = dot(inters_ref[n], partner).astype(BF16)
-                total = total + weight * dot(half, turned[n])
+                half = dot(inter_ref[i, j, n], partner).astype(BF16)
+                total = total + weight * dot(half, turned_ref[i, j, n])
             levels = jnp.broadcast_to(virtual_ref[i, pl.ds(j, 1)], (npno, npno))
             shift = levels + levels.T - occupied_ref[first_row + i] - occupied_ref[first_col + j]
-            result = exchange_ref[i, j] + shift * mats_ref[i, j].astype(F32) - total
-            wide_ref[:, :npno] = result
-            even = wide_ref[pl.ds(0, chunks, 2), :]
-            odd = pltpu.roll(wide_ref[pl.ds(1, chunks, 2), :], npno, 1)
-            keep = (first < kept_ref[j, i]) & (second < kept_ref[j, i])
-            base_ref[i, j] = jnp.where(keep, jnp.where(lane < npno, even, odd), 0.0)
-            factor_ref[i, j] = jnp.where(keep, scale, 0.0)
+            wide = wide_ref.at[j]
+            wide[:, :npno] = exchange_ref[i, j] + shift * mats_ref[i, j].astype(F32) - total
+            even = wide[pl.ds(0, chunks, 2), :]
+            odd = pltpu.roll(wide[pl.ds(1, chunks, 2), :], npno, 1)
+            result = jnp.where(lane < npno, even, odd)
+            base_ref[i, j] = jnp.where(factor_ref[i, j] == 0.0, 0.0, result)
         return carry
 
     lax.fori_loop(0, row_count, one_row, 0)
@@ -249,6 +225,49 @@
         for j in range(column_count):
             for s in range(domain):
                 turned_ref[j, s, i * npno : (i + 1) * npno] = coef_ref[i, j, s].T[:npno]
+
+
+def square_kernel(
+    scale, kept_hbm, inter_hbm, mats_ref, turned_mats_ref, factor_ref,
+    inter_ref, flat_ref, wide_ref, kept_ref, inter_sems, kept_sem,
+):
+    row_count, column_count, terms, npno, _ = mats_ref.shape
+    chunks, lanes = factor_ref.shape[2:]
+
+    def fetch_inter(i):
+        return pltpu.make_async_copy(inter_hbm.at[i], inter_ref.at[i], inter_sems.at[i])
+
+    kept_copy = pltpu.make_async_copy(kept_hbm, kept_ref, kept_sem)
+    kept_copy.start()
+    for i in range(row_count):
+        fetch_inter(i).start()
+
+    def one_row(i, carry):
+        fetch_inter(i).wait()
+        for j in range(column_count):
+            for q in range(chunks):
+                flat_ref[j, q] = inter_ref[i, j, :, q * lanes : (q + 1) * lanes].astype(F32)
+            for n in range(terms):
+                lines = flat_ref[j, :, n, :]
+                wide_ref[j, n, pl.ds(0, chunks, 2), :] = lines
+                wide_ref[j, n, pl.ds(1, chunks, 2), :] = pltpu.roll(lines, npno, 1)
+        for j in range(column_count):
+            for n in range(terms):
+                inter = wide_ref[j, n, :, :npno]
+                mats_ref[i, j, n] = inter.astype(BF16)
+                turned_mats_ref[i, j, n] = inter.T.astype(BF16)
+        return carry
+
+    lax.fori_loop(0, row_count, one_row, 0)
+    kept_copy.wait()
+    place = lax.broadcasted_iota(jnp.int32, (chunks, lanes), 0)
+    lane = lax.broadcasted_iota(jnp.int32, (chunks, lanes), 1)
+    first = 2 * place + jnp.where(lane < npno, 0, 1)
+    second = jnp.where(lane < npno, lane, lane - npno)
+    most = jnp.maximum(first, second)
+    for i in range(row_count):
+        for j in range(column_count):
+            factor_ref[i, j] = jnp.where(most < kept_ref[j, i], scale, 0.0)
 
 
 def row_kernel(cores, units, held, scale, atoms_ref, coef_ref, turned_ref, all_ref, out_ref, metric_ref):
@@ -300,13 +319,16 @@
 
 
 def column_kernel(
-    takers, coef_ref, turned_ref, base_ref, factor_ref, held_ref, got_ref,
-    out_hbm, packed_ref, metric_ref, wide_ref, flat_ref, out_ref, sems,
+    takers, coef_ref, turned_ref, base_ref, factor_ref, *refs,
 ):
     row_count, column_count, domain, pao, lanes = coef_ref.shape
+    held, got = refs[:column_count], refs[column_count : 2 * column_count]
+    out_hbm, packed_ref, metric_ref, wide_ref, flat_ref, out_ref, sems = refs[2 * column_count :]
     npno = lanes // 2
     chunks = npno // 2
-    merge_into(takers, column_count, row_count, held_ref, got_ref, packed_ref)
+    for j in range(column_count):
+        target = packed_ref.at[pl.ds(j * domain, domain)]
+        merge_into(takers, column_count, row_count, held[j], got[j], target)
     slots = column_count * domain
     lows = [unpack(packed_ref[index], metric_ref.at[index]) for index in range(slots)]
     products = []
@@ -347,21 +369,21 @@
     )
 
 
-def partners_of(size, first):
-    pairs = [(n, n + 1) for n in range(first, size - 1, 2)]
-    alone = [(n, n) for n in range(size) if n < first or n >= first + 2 * len(pairs)]
-    return pairs, pairs + [(b, a) for a, b in pairs] + alone
-
-
-def neighbours(block, axis):
-    size = lax.axis_size(axis)
-    even = lax.ppermute(block, axis, partners_of(size, 0)[1])
-    pairs, route = partners_of(size, 1)
-    if size % 4 == 0 and axis == "row" and all(a ^ b == 3 for a, b in pairs):
-        odd = lax.ppermute(block, axis, [(n, n ^ 3) for n in range(size)])
-    else:
-        odd = lax.ppermute(block, axis, route)
-    return [even, odd]
+def neighbours(block, axis, other):
+    size, rest = lax.axis_size(axis), lax.axis_size(other)
+    even = lax.ppermute(block, axis, [(n, n ^ 1) for n in range(size)])
+    pairs = [(n, n + 1) for n in range(1, size - 1, 2)]
+    if axis == "row" and size == 2 * len(pairs) + 2 and all(a ^ b == 3 for a, b in pairs):
+        return [even, lax.ppermute(block, axis, [(n, n ^ 3) for n in range(size)])]
+    joint = pairs + [(b, a) for a, b in pairs]
+    alone = [n for n in range(size) if n not in dict(joint)]
+    route = [((m, a), (m, b)) for m in range(rest) for a, b in joint]
+    route += [((m, a), (m ^ 1, a)) for m in range(rest) for a in alone]
+
+    def place(m, n):
+        return n * rest + m if axis == "row" else m * size + n
+
+    return [even, lax.ppermute(block, ("row", "col"), [(place(*a), place(*b)) for a, b in route])]
 
 
 def after(block, others):
@@ -410,7 +432,7 @@
     return buffers
 
 
-def spread(piece, sources, column_count, row_count, first):
+def spread(pieces, sources, column_count, row_count, first):
     rows, columns = lax.axis_size("row"), len(sources)
     bits = rows.bit_length() - 1
     assert rows == 1 << bits
@@ -426,19 +448,22 @@
             ]
             takers.append([away ^ bit for away in reached[turn]])
             reached[turn] = reached[turn] + takers[turn]
-        got = lax.ppermute(piece, ("row", "col"), pairs)
+        got = [lax.ppermute(piece, ("row", "col"), pairs) for piece in pieces]
         if step < bits - 1:
-            piece = call(
-                functools.partial(merge_kernel, takers, column_count, row_count),
-                jax.ShapeDtypeStruct(piece.shape, piece.dtype),
-                [VMEM, VMEM] + [ANY] * len(first),
-                VMEM,
-                [],
-                "merge",
-                0,
-                0,
-            )(piece, got, *first)
-    return piece, got, takers
+            pieces = [
+                call(
+                    functools.partial(merge_kernel, takers, column_count, row_count),
+                    jax.ShapeDtypeStruct(piece.shape, piece.dtype),
+                    [VMEM, VMEM] + [ANY] * len(others),
+                    VMEM,
+                    [],
+                    "merge",
+                    0,
+                    0,
+                )(piece, block, *others)
+                for piece, block, others in zip(pieces, got, first)
+            ]
+    return pieces + got, takers
 
 
 def on_device(
@@ -503,8 +528,8 @@
         2 * held * aux * pao * pao,
         fitting.size * 2,
     )(atoms_table, own_block, fit)
-    row_halos = neighbours(lines, "row")
-    col_halos = neighbours(lines, "col")
+    row_halos = neighbours(lines, "row", "col")
+    col_halos = neighbours(lines, "col", "row")
     shape = (row_count, column_count, domain, pao, lanes)
     own_coefficients, column_coefficients, own_turned, turned = call(
         prepare_kernel,
@@ -521,15 +546,36 @@
         0,
         coefficients.size * 4,
     )(coefs)
-    buffers = gather_metrics(packed, cores, units, row_halos, [own_turned])
+    mats = jax.ShapeDtypeStruct((row_count, column_count, terms, npno, npno), BF16)
+    flat = jax.ShapeDtypeStruct((row_count, column_count, chunks, lanes), F32)
+    mats, turned_mats, factor = call(
+        functools.partial(square_kernel, scale),
+        (mats, mats, flat),
+        [HBM] * 2,
+        (VMEM,) * 3,
+        [
+            pltpu.VMEM(intersections.shape, BF16),
+            pltpu.VMEM((column_count, chunks, terms, lanes), F32),
+            pltpu.VMEM((column_count, terms, npno, lanes), F32),
+            pltpu.SMEM(kept_count.shape[::-1], jnp.int32),
+            pltpu.SemaphoreType.DMA((row_count,)),
+            pltpu.SemaphoreType.DMA(()),
+        ],
+        "square",
+        0,
+        intersections.size * 4,
+    )(kept, inter)
+    buffers = gather_metrics(packed, cores, units, row_halos + [turned_mats], [own_turned])
     blocks = [lines] + row_halos + col_halos
     wanted = column_count * domain
     atoms = len(buffers) * held
-    piece, metrics = call(
+    *pieces, metrics = call(
         functools.partial(select_kernel, cores, units),
-        tuple(jax.ShapeDtypeStruct((n, depth, half), BF16) for n in (wanted, atoms)),
+        tuple(
+            jax.ShapeDtypeStruct((n, depth, half), BF16) for n in [domain] * column_count + [atoms]
+        ),
         [SMEM] + [VMEM] * len(buffers),
-        (VMEM,) * 2,
+        (VMEM,) * (column_count + 1),
         [],
         "select_column_atoms",
         0,
@@ -547,36 +593,32 @@
     )(table, own_coefficients, own_turned, metrics)
 
     sources = [c * column_count // row_count for c in range(columns)]
-    piece, got, takers = spread(piece, sources, column_count, row_count, [exchange] + col_halos)
-
-    base, factor = call(
-        functools.partial(couple_kernel, scale),
-        (jax.ShapeDtypeStruct((row_count, column_count, chunks, lanes), F32),) * 2,
-        [HBM] * 6 + [VMEM] * (1 + len(blocks)),
-        (VMEM,) * 2,
+    first = [[]] * (column_count - 1) + [[exchange] + col_halos]
+    pieces, takers = spread(pieces, sources, column_count, row_count, first)
+
+    base = call(
+        couple_kernel,
+        flat,
+        [HBM] * 4 + [VMEM] * (4 + len(blocks)),
+        VMEM,
         [
-            pltpu.VMEM((chunks, terms, lanes), F32),
-            pltpu.VMEM((npno, lanes), F32),
+            pltpu.VMEM((row_count * column_count, npno, lanes), F32),
             pltpu.VMEM((len(blocks) * row_count, column_count, npno, npno), BF16),
-            pltpu.VMEM((terms, npno, npno), BF16),
-            pltpu.VMEM(intersections.shape, BF16),
             pltpu.SMEM(fock_partner.shape[::-1], jnp.int32),
             pltpu.SMEM(fock_value.shape[::-1], F32),
             pltpu.SMEM(occupied_energy.shape, F32),
             pltpu.VMEM(virtual_energy.shape, F32),
-            pltpu.SMEM(kept_count.shape[::-1], jnp.int32),
-            pltpu.SemaphoreType.DMA((5,)),
-            pltpu.SemaphoreType.DMA((row_count,)),
+            pltpu.SemaphoreType.DMA((4,)),
         ],
         "couple",
         4 * row_count * column_count * terms * npno**3,
         intersections.size * 4,
-    )(partner, value, occupied, virtual, kept, inter, exchange, *blocks)
+    )(partner, value, occupied, virtual, mats, turned_mats, factor, exchange, *blocks)
 
     return call(
         functools.partial(column_kernel, takers),
         jax.ShapeDtypeStruct(amplitudes.shape, F32),
-        [VMEM] * 6,
+        [VMEM] * (4 + len(pieces)),
         HBM,
         [
             pltpu.VMEM((wanted, depth, half), BF16),
@@ -589,7 +631,7 @@
         "column_exchange",
         2 * row_count * column_count * domain * pao * npno * (pao + npno),
         coefficients.size,
-    )(column_coefficients, turned, base, factor, piece, got)
+    )(column_coefficients, turned, base, factor, *pieces)
 
 
 def solution(mesh):

time: 38.3 us -> 37 us (0.966)
  waiting for transfers between devices: 9.2 us -> 6.32 us
  starting transfers between devices: 14 us -> 15.9 us
    ppermute x6 -> x8, waiting for transfers between devices: 6.64 us -> 3.69 us  [the longest x4 2.32 us: spread(): got = [lax.ppermute(piece, ('row', 'col'), pairs) for piece in pieces]]
    ppermute x6 -> x8, starting transfers between devices: 6.21 us -> 8.2 us  [the longest x4 3.72 us: spread(): got = [lax.ppermute(piece, ('row', 'col'), pairs) for piece in pieces]]
    pallas_call x1 -> x2, Pallas kernels: 5.53 us -> 5.16 us  [the longest x1 2.77 us: on_device(): call(couple_kernel, flat, [HBM] * 4 + [VMEM] * (4 + len(blocks)), VMEM, [...]
  transfers between devices with their start and end apart: 13 -> 15, of which waited for: 5 -> 5; matrix products, arithmetic and copies ran while one was open for 0% -> 0% of each run, Pallas kernels for 29% -> 29%
where the time goes in v6:
time: 37 us; the launch traced here: 36.9 us
  starting transfers between devices  15.9 us (43%)
  Pallas kernels  14.5 us (39%)
  waiting for transfers between devices  6.32 us (17%)
    ppermute x2, starting transfers between devices, gather_metrics(): up = lax.ppermute(up, 'col', forward)  5.61 us
    ppermute x4, starting transfers between devices, spread(): got = [lax.ppermute(piece, ('row', 'col'), pairs) for piece in pieces]  3.72 us
    pallas_call x1, Pallas kernels, on_device(): call(functools.partial(row_kernel, cores, units, held, scale), jax.ShapeD...  3.11 us
    pallas_call x1, Pallas kernels, on_device(): call(couple_kernel, flat, [HBM] * 4 + [VMEM] * (4 + len(blocks)), VMEM, [...  2.77 us
    pallas_call x1, Pallas kernels, on_device(): call(functools.partial(square_kernel, scale), (mats, mats, flat), [HBM] *...  2.39 us
    ppermute x4, waiting for transfers between devices, spread(): got = [lax.ppermute(piece, ('row', 'col'), pairs) for piece in pieces]  2.32 us
    pallas_call x1, Pallas kernels, on_device(): call(prepare_kernel, (jax.ShapeDtypeStruct(shape, BF16), jax.ShapeDtypeSt...  2.25 us
    pallas_call x1, Pallas kernels, on_device(): call(functools.partial(column_kernel, takers), jax.ShapeDtypeStruct(ampli...  1.61 us
  transfers between devices with their start and end apart: 15, of which 5 were waited for; matrix products, arithmetic and copies ran while one was open for 0% of the time, Pallas kernels for 29%

profile of v6, /device:TPU:0, one launch (start us, length us, event | category | flops | bytes accessed | tf_op | source)
XLA Modules:
  0.0 36.9 jit_solution(2407549978544141752)
XLA Ops:
  0.0 1.5 %pack_metric.1 = (bf16[2,272,128]{2,1,0:T(8,128)(2,1)S(1)}, s32[3,16]{1,0:T(4,128)S(1)}, bf16[4,2,32,128]{3,2,1,0:T(8,128)(2,1)S(1)}) custom-call(s32[3,16]{1,0:T(4,128)} %bitcast.4, bf16[4,2,4096]{2,1,0:T(2,128)(2,1)} %block_hbm.1, bf16[2,512,256]{2,1,0:T(8,128)(2,1)} %fit_ref.1), custom_call_target="tpu_custom_call" | custom-call | flops 134217728 | bytes 524288 | tf_op jit(solution)/shard_map/pack_metric/pallas_call | solution.py:510
  1.5 3.1 %collective-permute-start.1 = (bf16[2,272,128]{2,1,0:T(8,128)(2,1)S(1)}, bf16[2,272,128]{2,1,0:T(8,128)(2,1)S(1)}, u32[]{:S(2)}, u32[]{:S(2)}) collective-permute-start(bf16[2,272,128]{2,1,0:T(8,128)(2,1)S(1)} %get-tuple-element.26.refs_0_), channel_id=1, source_target_pairs={{0,2},{1,3},{2,6},{3,7},{6,4},{7,5},{4,0},{5,1},{8,10},{9,11},{10,... | collective-permute-start | bytes 417800 | tf_op jit(solution)/shard_map/ppermute | solution.py:415
  4.6 1.5 %collective-permute-start.3 = (bf16[4,2,32,128]{3,2,1,0:T(8,128)(2,1)S(1)}, bf16[4,2,32,128]{3,2,1,0:T(8,128)(2,1)S(1)}, u32[]{:S(2)}, u32[]{:S(2)}) collective-permute-start(bf16[4,2,32,128]{3,2,1,0:T(8,128)(2,1)S(1)} %get-tuple-element.27.refs_1_), channel_id=1, source_target_pairs={{0,8},{8,0},{16,24},{24,16},{1,9},{9,1},{17,25},{25,17},{2,10},{10... | collective-permute-start | bytes 196616 | tf_op jit(solution)/shard_map/ppermute | solution.py:374
  6.1 1.5 %collective-permute-start.4 = (bf16[4,2,32,128]{3,2,1,0:T(8,128)(2,1)S(1)}, bf16[4,2,32,128]{3,2,1,0:T(8,128)(2,1)S(1)}, u32[]{:S(2)}, u32[]{:S(2)}) collective-permute-start(bf16[4,2,32,128]{3,2,1,0:T(8,128)(2,1)S(1)} %get-tuple-element.27.refs_1_), channel_id=1, source_target_pairs={{0,24},{8,16},{16,8},{24,0},{1,25},{9,17},{17,9},{25,1},{2,26},{10... | collective-permute-start | bytes 196616 | tf_op jit(solution)/shard_map/ppermute | solution.py:377
  7.6 1.3 %collective-permute-start.7 = (bf16[2,272,128]{2,1,0:T(8,128)(2,1)S(1)}, bf16[2,272,128]{2,1,0:T(8,128)(2,1)S(1)}, u32[]{:S(2)}, u32[]{:S(2)}) collective-permute-start(bf16[2,272,128]{2,1,0:T(8,128)(2,1)S(1)} %get-tuple-element.26.refs_0_), channel_id=1, source_target_pairs={{2,0},{3,1},{6,2},{7,3},{4,6},{5,7},{0,4},{1,5},{10,8},{11,9},{14,... | collective-permute-start | bytes 417800 | tf_op jit(solution)/shard_map/ppermute | solution.py:420
  8.9 2.4 %square.1 = (bf16[4,2,8,64,64]{4,3,2,1,0:T(8,128)(2,1)S(1)}, bf16[4,2,8,64,64]{4,3,2,1,0:T(8,128)(2,1)S(1)}, f32[4,2,32,128]{3,2,1,0:T(8,128)S(1)}) custom-call(s32[2,4]{1,0:T(2,128)} %bitcast.7, bf16[4,2,8,4096]{3,2,1,0:T(8,128)(2,1)} %inter_hbm.1), custom_call_target="tpu_custom_call" | custom-call | bytes 1048576 | tf_op jit(solution)/shard_map/square/pallas_call | solution.py:551
  11.3 0.0 collective-permute-done.3.refs_0_.refs_2_
  11.3 0.0 collective-permute-done.4.refs_1_.refs_3_
  11.3 0.0 collective-permute-done.1.block_ref.refs_2_
  11.4 2.5 %collective-permute-start.5 = (bf16[2,272,128]{2,1,0:T(8,128)(2,1)S(1)}, bf16[2,272,128]{2,1,0:T(8,128)(2,1)S(1)}, u32[]{:S(2)}, u32[]{:S(2)}) collective-permute-start(bf16[2,272,128]{2,1,0:T(8,128)(2,1)S(1)} %after_others.2), channel_id=1, source_target_pairs={{0,2},{1,3},{2,6},{3,7},{6,4},{7,5},{4,0},{5,1},{8,10},{9,11},{10,... | collective-permute-start | bytes 417800 | tf_op jit(solution)/shard_map/ppermute | solution.py:415
  13.9 0.0 collective-permute-start
  13.9 2.2 %prepare.1 = (bf16[4,2,3,256,128]{4,3,2,1,0:T(8,128)(2,1)S(1)}, bf16[4,2,3,256,128]{4,3,2,1,0:T(8,128)(2,1)S(1)}, bf16[4,3,128,256]{3,2,1,0:T(8,128)(2,1)S(1)}, bf16[2,3,256,256]{3,2,1,0:T(8,128)(2,1)S(1)}) custom-call(bf16[4,2,6,256,128]{4,3,2,1,0:T(8,128)(2,1)} %coef_hbm.1), custom_call_target="tpu_custom_call" | custom-call | bytes 6291456 | tf_op jit(solution)/shard_map/prepare/pallas_call | solution.py:534
  16.2 0.6 %collective-permute-start.2 = (bf16[2,272,128]{2,1,0:T(8,128)(2,1)S(1)}, bf16[2,272,128]{2,1,0:T(8,128)(2,1)S(1)}, u32[]{:S(2)}, u32[]{:S(2)}) collective-permute-start(bf16[2,272,128]{2,1,0:T(8,128)(2,1)S(1)} %collective-permute-done.1.block_ref.refs_2_), channel_id=1, source_target_pairs={{0,1},{1,0},{2,3},{3,2},{4,5},{5,4},{6,7},{7,6},{8,9},{9,8},{10,11... | collective-permute-start | bytes 417800 | tf_op jit(solution)/shard_map/ppermute | solution.py:431
  16.7 0.0 collective-permute-done.7.refs_6_
  16.7 0.1 collective-permute-start.8
  16.8 1.3 %collective-permute-done.5.block_ref = bf16[2,272,128]{2,1,0:T(8,128)(2,1)S(1)} collective-permute-done((bf16[2,272,128]{2,1,0:T(8,128)(2,1)S(1)}, bf16[2,272,128]{2,1,0:T(8,128)(2,1)S(1)}, u32[]{:S(2)}, u32[]{:S(2)}) %collective-permute-start.5) | collective-permute-done | bytes 139296 | tf_op jit(solution)/shard_map/ppermute | solution.py:415
  18.1 0.1 collective-permute-start.6
  18.2 0.0 collective-permute-done.refs_1_
  18.2 0.0 collective-permute-done.2.refs_3_
  18.2 0.0 collective-permute-done.8.refs_7_
  18.3 1.3 %collective-permute-done.6.refs_5_ = bf16[2,272,128]{2,1,0:T(8,128)(2,1)S(1)} collective-permute-done((bf16[2,272,128]{2,1,0:T(8,128)(2,1)S(1)}, bf16[2,272,128]{2,1,0:T(8,128)(2,1)S(1)}, u32[]{:S(2)}, u32[]{:S(2)}) %collective-permute-start.6) | collective-permute-done | bytes 139296 | tf_op jit(solution)/shard_map/ppermute | solution.py:431
  19.6 0.8 %select_column_atoms.1 = (bf16[3,272,128]{2,1,0:T(8,128)(2,1)S(1)}, bf16[3,272,128]{2,1,0:T(8,128)(2,1)S(1)}, bf16[16,272,128]{2,1,0:T(8,128)(2,1)S(1)}) custom-call(s32[3,16]{1,0:T(4,128)S(1)} %get-tuple-element.23.atoms_ref, bf16[2,272,128]{2,1,0:T(8,128)(2,1)S(1)} %get-tuple-element.26.refs_0_, bf16[2,272,128]{2,1,0:T(8,128)(2,1)S(1)} %collective-permute-done.refs_1_, ...), custom_call_target="tpu_custom_call" | custom-call | bytes 5292032 | tf_op jit(solution)/shard_map/select_column_atoms/pallas_call | solution.py:572
  20.4 1.6 %collective-permute-start.11 = (bf16[3,272,128]{2,1,0:T(8,128)(2,1)S(1)}, bf16[3,272,128]{2,1,0:T(8,128)(2,1)S(1)}, u32[]{:S(2)}, u32[]{:S(2)}) collective-permute-start(bf16[3,272,128]{2,1,0:T(8,128)(2,1)S(1)} %get-tuple-element.29.kept_ref), channel_id=1, source_target_pairs={{0,8},{8,0},{16,24},{24,16},{2,10},{10,2},{18,26},{26,18},{4,12},{... | collective-permute-start | bytes 626696 | tf_op jit(solution)/shard_map/ppermute | solution.py:451
  21.9 0.5 %collective-permute-start.12 = (bf16[3,272,128]{2,1,0:T(8,128)(2,1)S(1)}, bf16[3,272,128]{2,1,0:T(8,128)(2,1)S(1)}, u32[]{:S(2)}, u32[]{:S(2)}) collective-permute-start(bf16[3,272,128]{2,1,0:T(8,128)(2,1)S(1)} %get-tuple-element.30.kept_ref), channel_id=1, source_target_pairs={{0,8},{8,0},{16,24},{24,16},{2,10},{10,2},{18,26},{26,18},{4,12},{... | collective-permute-start | bytes 626696 | tf_op jit(solution)/shard_map/ppermute | solution.py:451
  22.5 0.0 collective-permute-start.9
  22.5 1.5 %collective-permute-start.10 = (bf16[4,2,32,128]{3,2,1,0:T(8,128)(2,1)S(1)}, bf16[4,2,32,128]{3,2,1,0:T(8,128)(2,1)S(1)}, u32[]{:S(2)}, u32[]{:S(2)}) collective-permute-start(bf16[4,2,32,128]{3,2,1,0:T(8,128)(2,1)S(1)} %get-tuple-element.27.refs_1_), channel_id=1, source_target_pairs={{1,2},{3,4},{5,6},{2,1},{4,3},{6,5},{9,10},{11,12},{13,14},{10,9},... | collective-permute-start | bytes 196616 | tf_op jit(solution)/shard_map/ppermute | solution.py:386
  24.0 3.1 %row_exchange.1.refs_0_ = f32[4,2,64,64]{3,2,1,0:T(8,128)S(1)} custom-call(s32[3,16]{1,0:T(4,128)S(1)} %get-tuple-element.23.atoms_ref, bf16[4,2,3,256,128]{4,3,2,1,0:T(8,128)(2,1)S(1)} %get-tuple-element.24.coef_ref, bf16[4,3,128,256]{3,2,1,0:T(8,128)(2,1)S(1)} %get-tuple-element.25.refs_0_.turned_ref, bf16[16,272,128]{2,1,0:T(8,128)(2,1)S(1)} %get-tuple-element.28.all_ref), custom_call_target="tpu_custom_call" | custom-call | flops 251658240 | bytes 1572864 | tf_op jit(solution)/shard_map/row_exchange/pallas_call | solution.py:584
  27.1 0.0 collective-permute-done.11.got_ref
  27.1 0.7 %collective-permute-start.13 = (bf16[3,272,128]{2,1,0:T(8,128)(2,1)S(1)}, bf16[3,272,128]{2,1,0:T(8,128)(2,1)S(1)}, u32[]{:S(2)}, u32[]{:S(2)}) collective-permute-start(bf16[3,272,128]{2,1,0:T(8,128)(2,1)S(1)} %merge.2.refs_0_), channel_id=1, source_target_pairs={{0,16},{8,24},{16,0},{24,8},{2,18},{10,26},{18,2},{26,10},{4,20},{... | collective-permute-start | bytes 626696 | tf_op jit(solution)/shard_map/ppermute | solution.py:451
  27.8 0.0 collective-permute-done.9.refs_4_.refs_1_
  27.8 1.4 %collective-permute-done.10.refs_5_.refs_2_ = bf16[4,2,32,128]{3,2,1,0:T(8,128)(2,1)S(1)} collective-permute-done((bf16[4,2,32,128]{3,2,1,0:T(8,128)(2,1)S(1)}, bf16[4,2,32,128]{3,2,1,0:T(8,128)(2,1)S(1)}, u32[]{:S(2)}, u32[]{:S(2)}) %collective-permute-start.10) | collective-permute-done | bytes 65568 | tf_op jit(solution)/shard_map/ppermute | solution.py:386
  29.2 0.0 collective-permute-done.12.got_ref
  29.2 0.9 %collective-permute-start.14 = (bf16[3,272,128]{2,1,0:T(8,128)(2,1)S(1)}, bf16[3,272,128]{2,1,0:T(8,128)(2,1)S(1)}, u32[]{:S(2)}, u32[]{:S(2)}) collective-permute-start(bf16[3,272,128]{2,1,0:T(8,128)(2,1)S(1)} %merge.3.refs_1_), channel_id=1, source_target_pairs={{0,16},{8,24},{16,0},{24,8},{2,18},{10,26},{18,2},{26,10},{4,20},{... | collective-permute-start | bytes 626696 | tf_op jit(solution)/shard_map/ppermute | solution.py:451
  30.1 2.8 %couple.1.base_ref = f32[4,2,32,128]{3,2,1,0:T(8,128)S(1)} custom-call(s32[4,16]{1,0:T(4,128)} %bitcast.5, f32[4,16]{1,0:T(4,128)} %bitcast.6, f32[16]{0:T(128)} %occupied_hbm.1, f32[4,2,64]{2,1,0:T(2,128)} %virtual_hbm.1, bf16[4,2,8,64,64]{4,3,2,1,0:T(8,128)(2,1)S(1)} %get-tuple-element.20.inter_ref, ...), custom_call_target="tpu_custom_call" | custom-call | flops 67108864 | bytes 1048576 | tf_op jit(solution)/shard_map/couple/pallas_call | solution.py:599
  32.9 0.1 collective-permute-done.13.refs_2_
  33.0 2.2 %collective-permute-done.14.refs_3_ = bf16[3,272,128]{2,1,0:T(8,128)(2,1)S(1)} collective-permute-done((bf16[3,272,128]{2,1,0:T(8,128)(2,1)S(1)}, bf16[3,272,128]{2,1,0:T(8,128)(2,1)S(1)}, u32[]{:S(2)}, u32[]{:S(2)}) %collective-permute-start.14) | collective-permute-done | bytes 208928 | tf_op jit(solution)/shard_map/ppermute | solution.py:451
  35.2 1.6 %column_exchange.1 = f32[4,2,4096]{2,1,0:T(2,128)} custom-call(bf16[4,2,3,256,128]{4,3,2,1,0:T(8,128)(2,1)S(1)} %get-tuple-element.18.coef_ref, bf16[2,3,256,256]{3,2,1,0:T(8,128)(2,1)S(1)} %get-tuple-element.19.turned_ref, f32[4,2,32,128]{3,2,1,0:T(8,128)S(1)} %couple.1.base_ref, f32[4,2,32,128]{3,2,1,0:T(8,128)S(1)} %get-tuple-element.22.factor_ref, ...), custom_call_target="tpu_custom_call" | custom-call | flops 251658240 | bytes 1572864 | tf_op jit(solution)/shard_map/column_exchange/pallas_call | solution.py:618
  (4 shorter events, 0.1 us)
Async XLA Ops:
  1.5 9.8 %collective-permute-start.1 = (bf16[2,272,128]{2,1,0:T(8,128)(2,1)S(1)}, bf16[2,272,128]{2,1,0:T(8,128)(2,1)S(1)}, u32[]{:S(2)}, u32[]{:S(2)}) collective-permute-start(bf16[2,272,128]{2,1,0:T(8,128)(2,1)S(1)} %get-tuple-element.26.refs_0_), channel_id=1, source_target_pairs={{0,2},{1,3},{2,6},{3,7},{6,4},{7,5},{4,0},{5,1},{8,10},{9,11},{10,... | collective-permute-start | bytes 417800 | tf_op jit(solution)/shard_map/ppermute | solution.py:415
  4.6 6.7 %collective-permute-start.3 = (bf16[4,2,32,128]{3,2,1,0:T(8,128)(2,1)S(1)}, bf16[4,2,32,128]{3,2,1,0:T(8,128)(2,1)S(1)}, u32[]{:S(2)}, u32[]{:S(2)}) collective-permute-start(bf16[4,2,32,128]{3,2,1,0:T(8,128)(2,1)S(1)} %get-tuple-element.27.refs_1_), channel_id=1, source_target_pairs={{0,8},{8,0},{16,24},{24,16},{1,9},{9,1},{17,25},{25,17},{2,10},{10... | collective-permute-start | bytes 196616 | tf_op jit(solution)/shard_map/ppermute | solution.py:374
  6.1 5.3 %collective-permute-start.4 = (bf16[4,2,32,128]{3,2,1,0:T(8,128)(2,1)S(1)}, bf16[4,2,32,128]{3,2,1,0:T(8,128)(2,1)S(1)}, u32[]{:S(2)}, u32[]{:S(2)}) collective-permute-start(bf16[4,2,32,128]{3,2,1,0:T(8,128)(2,1)S(1)} %get-tuple-element.27.refs_1_), channel_id=1, source_target_pairs={{0,24},{8,16},{16,8},{24,0},{1,25},{9,17},{17,9},{25,1},{2,26},{10... | collective-permute-start | bytes 196616 | tf_op jit(solution)/shard_map/ppermute | solution.py:377
  7.6 9.2 %collective-permute-start.7 = (bf16[2,272,128]{2,1,0:T(8,128)(2,1)S(1)}, bf16[2,272,128]{2,1,0:T(8,128)(2,1)S(1)}, u32[]{:S(2)}, u32[]{:S(2)}) collective-permute-start(bf16[2,272,128]{2,1,0:T(8,128)(2,1)S(1)} %get-tuple-element.26.refs_0_), channel_id=1, source_target_pairs={{2,0},{3,1},{6,2},{7,3},{4,6},{5,7},{0,4},{1,5},{10,8},{11,9},{14,... | collective-permute-start | bytes 417800 | tf_op jit(solution)/shard_map/ppermute | solution.py:420
  11.4 6.8 %collective-permute-start.5 = (bf16[2,272,128]{2,1,0:T(8,128)(2,1)S(1)}, bf16[2,272,128]{2,1,0:T(8,128)(2,1)S(1)}, u32[]{:S(2)}, u32[]{:S(2)}) collective-permute-start(bf16[2,272,128]{2,1,0:T(8,128)(2,1)S(1)} %after_others.2), channel_id=1, source_target_pairs={{0,2},{1,3},{2,6},{3,7},{6,4},{7,5},{4,0},{5,1},{8,10},{9,11},{10,... | collective-permute-start | bytes 417800 | tf_op jit(solution)/shard_map/ppermute | solution.py:415
  13.9 4.3 %collective-permute-start = (bf16[2,272,128]{2,1,0:T(8,128)(2,1)S(1)}, bf16[2,272,128]{2,1,0:T(8,128)(2,1)S(1)}, u32[]{:S(2)}, u32[]{:S(2)}) collective-permute-start(bf16[2,272,128]{2,1,0:T(8,128)(2,1)S(1)} %get-tuple-element.26.refs_0_), channel_id=1, source_target_pairs={{0,1},{1,0},{2,3},{3,2},{4,5},{5,4},{6,7},{7,6},{8,9},{9,8},{10,11... | collective-permute-start | bytes 417800 | tf_op jit(solution)/shard_map/ppermute | solution.py:431
  16.2 2.1 %collective-permute-start.2 = (bf16[2,272,128]{2,1,0:T(8,128)(2,1)S(1)}, bf16[2,272,128]{2,1,0:T(8,128)(2,1)S(1)}, u32[]{:S(2)}, u32[]{:S(2)}) collective-permute-start(bf16[2,272,128]{2,1,0:T(8,128)(2,1)S(1)} %collective-permute-done.1.block_ref.refs_2_), channel_id=1, source_target_pairs={{0,1},{1,0},{2,3},{3,2},{4,5},{5,4},{6,7},{7,6},{8,9},{9,8},{10,11... | collective-permute-start | bytes 417800 | tf_op jit(solution)/shard_map/ppermute | solution.py:431
  16.7 1.5 %collective-permute-start.8 = (bf16[2,272,128]{2,1,0:T(8,128)(2,1)S(1)}, bf16[2,272,128]{2,1,0:T(8,128)(2,1)S(1)}, u32[]{:S(2)}, u32[]{:S(2)}) collective-permute-start(bf16[2,272,128]{2,1,0:T(8,128)(2,1)S(1)} %collective-permute-done.7.refs_6_), channel_id=1, source_target_pairs={{0,1},{1,0},{2,3},{3,2},{4,5},{5,4},{6,7},{7,6},{8,9},{9,8},{10,11... | collective-permute-start | bytes 417800 | tf_op jit(solution)/shard_map/ppermute | solution.py:431
  18.1 1.4 %collective-permute-start.6 = (bf16[2,272,128]{2,1,0:T(8,128)(2,1)S(1)}, bf16[2,272,128]{2,1,0:T(8,128)(2,1)S(1)}, u32[]{:S(2)}, u32[]{:S(2)}) collective-permute-start(bf16[2,272,128]{2,1,0:T(8,128)(2,1)S(1)} %after_others.3.refs_4_), channel_id=1, source_target_pairs={{0,1},{1,0},{2,3},{3,2},{4,5},{5,4},{6,7},{7,6},{8,9},{9,8},{10,11... | collective-permute-start | bytes 417800 | tf_op jit(solution)/shard_map/ppermute | solution.py:431
  20.4 6.7 %collective-permute-start.11 = (bf16[3,272,128]{2,1,0:T(8,128)(2,1)S(1)}, bf16[3,272,128]{2,1,0:T(8,128)(2,1)S(1)}, u32[]{:S(2)}, u32[]{:S(2)}) collective-permute-start(bf16[3,272,128]{2,1,0:T(8,128)(2,1)S(1)} %get-tuple-element.29.kept_ref), channel_id=1, source_target_pairs={{0,8},{8,0},{16,24},{24,16},{2,10},{10,2},{18,26},{26,18},{4,12},{... | collective-permute-start | bytes 626696 | tf_op jit(solution)/shard_map/ppermute | solution.py:451
  21.9 7.3 %collective-permute-start.12 = (bf16[3,272,128]{2,1,0:T(8,128)(2,1)S(1)}, bf16[3,272,128]{2,1,0:T(8,128)(2,1)S(1)}, u32[]{:S(2)}, u32[]{:S(2)}) collective-permute-start(bf16[3,272,128]{2,1,0:T(8,128)(2,1)S(1)} %get-tuple-element.30.kept_ref), channel_id=1, source_target_pairs={{0,8},{8,0},{16,24},{24,16},{2,10},{10,2},{18,26},{26,18},{4,12},{... | collective-permute-start | bytes 626696 | tf_op jit(solution)/shard_map/ppermute | solution.py:451
  22.5 5.4 %collective-permute-start.9 = (bf16[4,2,32,128]{3,2,1,0:T(8,128)(2,1)S(1)}, bf16[4,2,32,128]{3,2,1,0:T(8,128)(2,1)S(1)}, u32[]{:S(2)}, u32[]{:S(2)}) collective-permute-start(bf16[4,2,32,128]{3,2,1,0:T(8,128)(2,1)S(1)} %get-tuple-element.27.refs_1_), channel_id=1, source_target_pairs={{0,1},{1,0},{2,3},{3,2},{4,5},{5,4},{6,7},{7,6},{8,9},{9,8},{10,11... | collective-permute-start | bytes 196616 | tf_op jit(solution)/shard_map/ppermute | solution.py:374
  22.5 6.7 %collective-permute-start.10 = (bf16[4,2,32,128]{3,2,1,0:T(8,128)(2,1)S(1)}, bf16[4,2,32,128]{3,2,1,0:T(8,128)(2,1)S(1)}, u32[]{:S(2)}, u32[]{:S(2)}) collective-permute-start(bf16[4,2,32,128]{3,2,1,0:T(8,128)(2,1)S(1)} %get-tuple-element.27.refs_1_), channel_id=1, source_target_pairs={{1,2},{3,4},{5,6},{2,1},{4,3},{6,5},{9,10},{11,12},{13,14},{10,9},... | collective-permute-start | bytes 196616 | tf_op jit(solution)/shard_map/ppermute | solution.py:386
  27.1 5.9 %collective-permute-start.13 = (bf16[3,272,128]{2,1,0:T(8,128)(2,1)S(1)}, bf16[3,272,128]{2,1,0:T(8,128)(2,1)S(1)}, u32[]{:S(2)}, u32[]{:S(2)}) collective-permute-start(bf16[3,272,128]{2,1,0:T(8,128)(2,1)S(1)} %merge.2.refs_0_), channel_id=1, source_target_pairs={{0,16},{8,24},{16,0},{24,8},{2,18},{10,26},{18,2},{26,10},{4,20},{... | collective-permute-start | bytes 626696 | tf_op jit(solution)/shard_map/ppermute | solution.py:451
  29.2 6.0 %collective-permute-start.14 = (bf16[3,272,128]{2,1,0:T(8,128)(2,1)S(1)}, bf16[3,272,128]{2,1,0:T(8,128)(2,1)S(1)}, u32[]{:S(2)}, u32[]{:S(2)}) collective-permute-start(bf16[3,272,128]{2,1,0:T(8,128)(2,1)S(1)} %merge.3.refs_1_), channel_id=1, source_target_pairs={{0,16},{8,24},{16,0},{24,8},{2,18},{10,26},{18,2},{26,10},{4,20},{... | collective-permute-start | bytes 626696 | tf_op jit(solution)/shard_map/ppermute | solution.py:451

commit v7 on v6

--- a/solution.py
+++ b/solution.py
@@ -271,29 +271,27 @@
 
 
 def row_kernel(cores, units, held, scale, atoms_ref, coef_ref, turned_ref, all_ref, out_ref, metric_ref):
-    row_count, column_count, domain = coef_ref.shape[:3]
-    npno = out_ref.shape[2]
+    row_count, column_count, domain, pao, lanes = coef_ref.shape
+    npno = lanes // 2
     row_place, col_place = lax.axis_index("row"), lax.axis_index("col")
-
-    def one_row(i, carry):
-        lows = []
+    lows = []
+    for i in range(row_count):
         for s in range(domain):
             atom = atoms_ref[s, row_place * row_count + i]
             place = pick_place(atom, row_place, col_place, cores, units, held)
-            lows.append(unpack(all_ref[place], metric_ref.at[s]))
-        products = []
+            lows.append(unpack(all_ref[place], metric_ref.at[i * domain + s]))
+    for i in range(row_count):
+        parts = []
         for s in range(domain):
             left = turned_ref[i, s]
-            product = dot(left, metric_ref[s]) + left.astype(F32) * lows[s]
-            products.append(product.astype(BF16))
-        for j in range(column_count):
-            total = dot(products[0][j * npno : (j + 1) * npno], coef_ref[i, j, 0])
-            for s in range(1, domain):
-                total = total + dot(products[s][j * npno : (j + 1) * npno], coef_ref[i, j, s])
+            part = dot(left, metric_ref[i * domain + s]) + left.astype(F32) * lows[i * domain + s]
+            parts.append(part.astype(BF16))
+        product = jnp.concatenate(parts, axis=1)
+        for j in range(column_count):
+            total = dot(
+                product[j * npno : (j + 1) * npno], coef_ref[i, j].reshape(domain * pao, lanes)
+            )
             out_ref[i, j] = total[:, npno:] * scale
-        return carry
-
-    lax.fori_loop(0, row_count, one_row, 0)
 
 
 def merge_into(takers, column_count, row_count, kept, got, target):
@@ -378,7 +376,8 @@
     joint = pairs + [(b, a) for a, b in pairs]
     alone = [n for n in range(size) if n not in dict(joint)]
     route = [((m, a), (m, b)) for m in range(rest) for a, b in joint]
-    route += [((m, a), (m ^ 1, a)) for m in range(rest) for a in alone]
+    trade = 1 if rest % 4 else 2
+    route += [((m, a), (m ^ trade, a)) for m in range(rest) for a in alone]
 
     def place(m, n):
         return n * rest + m if axis == "row" else m * size + n
@@ -586,7 +585,7 @@
         jax.ShapeDtypeStruct((row_count, column_count, npno, npno), F32),
         [SMEM] + [VMEM] * 3,
         VMEM,
-        [pltpu.VMEM((domain, pao, pao), BF16)],
+        [pltpu.VMEM((row_count * domain, pao, pao), BF16)],
         "row_exchange",
         2 * row_count * column_count * domain * pao * npno * (pao + npno),
         coefficients.size,

time: 37 us -> 36.2 us (0.978)
  Pallas kernels: 14.5 us -> 13.4 us
  waiting for transfers between devices: 6.32 us -> 6.98 us
  starting transfers between devices: 15.9 us -> 15.5 us
    ppermute x4, waiting for transfers between devices: 2.32 us -> 4.03 us  [spread(): got = [lax.ppermute(piece, ('row', 'col'), pairs) for piece in pieces]]
    pallas_call x1, Pallas kernels: 3.11 us -> 2 us  [on_device(): call(functools.partial(row_kernel, cores, units, held, scale), jax.ShapeD...]
    ppermute x1, waiting for transfers between devices: 1.35 us -> 0.31 us  [neighbours(): lax.ppermute(block, ('row', 'col'), [(place(*a), place(*b)) for a, b in r...]
    ppermute x1, starting transfers between devices: 1.49 us -> 0.87 us  [neighbours(): lax.ppermute(block, ('row', 'col'), [(place(*a), place(*b)) for a, b in r...]
  transfers between devices with their start and end apart: 15 -> 15, of which waited for: 5 -> 6; matrix products, arithmetic and copies ran while one was open for 0% -> 0% of each run, Pallas kernels for 29% -> 26%
where the time goes in v7:
time: 36.2 us; the launch traced here: 36 us
  starting transfers between devices  15.5 us (43%)
  Pallas kernels  13.4 us (37%)
  waiting for transfers between devices  6.98 us (19%)
    ppermute x2, starting transfers between devices, gather_metrics(): up = lax.ppermute(up, 'col', forward)  5.61 us
    ppermute x4, waiting for transfers between devices, spread(): got = [lax.ppermute(piece, ('row', 'col'), pairs) for piece in pieces]  4.03 us
    ppermute x4, starting transfers between devices, spread(): got = [lax.ppermute(piece, ('row', 'col'), pairs) for piece in pieces]  3.96 us
    pallas_call x1, Pallas kernels, on_device(): call(couple_kernel, flat, [HBM] * 4 + [VMEM] * (4 + len(blocks)), VMEM, [...  2.77 us
    pallas_call x1, Pallas kernels, on_device(): call(functools.partial(square_kernel, scale), (mats, mats, flat), [HBM] *...  2.39 us
    pallas_call x1, Pallas kernels, on_device(): call(prepare_kernel, (jax.ShapeDtypeStruct(shape, BF16), jax.ShapeDtypeSt...  2.25 us
    pallas_call x1, Pallas kernels, on_device(): call(functools.partial(row_kernel, cores, units, held, scale), jax.ShapeD...  2 us
    pallas_call x1, Pallas kernels, on_device(): call(functools.partial(column_kernel, takers), jax.ShapeDtypeStruct(ampli...  1.61 us
  transfers between devices with their start and end apart: 15, of which 6 were waited for; matrix products, arithmetic and copies ran while one was open for 0% of the time, Pallas kernels for 26%

profile of v7, /device:TPU:0, one launch (start us, length us, event | category | flops | bytes accessed | tf_op | source)
XLA Modules:
  0.0 36.0 jit_solution(14828503780501018569)
XLA Ops:
  0.0 1.5 %pack_metric.1 = (bf16[2,272,128]{2,1,0:T(8,128)(2,1)S(1)}, s32[3,16]{1,0:T(4,128)S(1)}, bf16[4,2,32,128]{3,2,1,0:T(8,128)(2,1)S(1)}) custom-call(s32[3,16]{1,0:T(4,128)} %bitcast.4, bf16[4,2,4096]{2,1,0:T(2,128)(2,1)} %block_hbm.1, bf16[2,512,256]{2,1,0:T(8,128)(2,1)} %fit_ref.1), custom_call_target="tpu_custom_call" | custom-call | flops 134217728 | bytes 524288 | tf_op jit(solution)/shard_map/pack_metric/pallas_call | solution.py:509
  1.5 3.1 %collective-permute-start.1 = (bf16[2,272,128]{2,1,0:T(8,128)(2,1)S(1)}, bf16[2,272,128]{2,1,0:T(8,128)(2,1)S(1)}, u32[]{:S(2)}, u32[]{:S(2)}) collective-permute-start(bf16[2,272,128]{2,1,0:T(8,128)(2,1)S(1)} %get-tuple-element.26.refs_0_), channel_id=1, source_target_pairs={{0,2},{1,3},{2,6},{3,7},{6,4},{7,5},{4,0},{5,1},{8,10},{9,11},{10,... | collective-permute-start | bytes 417800 | tf_op jit(solution)/shard_map/ppermute | solution.py:414
  4.6 1.5 %collective-permute-start.3 = (bf16[4,2,32,128]{3,2,1,0:T(8,128)(2,1)S(1)}, bf16[4,2,32,128]{3,2,1,0:T(8,128)(2,1)S(1)}, u32[]{:S(2)}, u32[]{:S(2)}) collective-permute-start(bf16[4,2,32,128]{3,2,1,0:T(8,128)(2,1)S(1)} %get-tuple-element.27.refs_1_), channel_id=1, source_target_pairs={{0,8},{8,0},{16,24},{24,16},{1,9},{9,1},{17,25},{25,17},{2,10},{10... | collective-permute-start | bytes 196616 | tf_op jit(solution)/shard_map/ppermute | solution.py:372
  6.1 1.5 %collective-permute-start.4 = (bf16[4,2,32,128]{3,2,1,0:T(8,128)(2,1)S(1)}, bf16[4,2,32,128]{3,2,1,0:T(8,128)(2,1)S(1)}, u32[]{:S(2)}, u32[]{:S(2)}) collective-permute-start(bf16[4,2,32,128]{3,2,1,0:T(8,128)(2,1)S(1)} %get-tuple-element.27.refs_1_), channel_id=1, source_target_pairs={{0,24},{8,16},{16,8},{24,0},{1,25},{9,17},{17,9},{25,1},{2,26},{10... | collective-permute-start | bytes 196616 | tf_op jit(solution)/shard_map/ppermute | solution.py:375
  7.6 1.3 %collective-permute-start.7 = (bf16[2,272,128]{2,1,0:T(8,128)(2,1)S(1)}, bf16[2,272,128]{2,1,0:T(8,128)(2,1)S(1)}, u32[]{:S(2)}, u32[]{:S(2)}) collective-permute-start(bf16[2,272,128]{2,1,0:T(8,128)(2,1)S(1)} %get-tuple-element.26.refs_0_), channel_id=1, source_target_pairs={{2,0},{3,1},{6,2},{7,3},{4,6},{5,7},{0,4},{1,5},{10,8},{11,9},{14,... | collective-permute-start | bytes 417800 | tf_op jit(solution)/shard_map/ppermute | solution.py:419
  8.9 2.4 %square.1 = (bf16[4,2,8,64,64]{4,3,2,1,0:T(8,128)(2,1)S(1)}, bf16[4,2,8,64,64]{4,3,2,1,0:T(8,128)(2,1)S(1)}, f32[4,2,32,128]{3,2,1,0:T(8,128)S(1)}) custom-call(s32[2,4]{1,0:T(2,128)} %bitcast.7, bf16[4,2,8,4096]{3,2,1,0:T(8,128)(2,1)} %inter_hbm.1), custom_call_target="tpu_custom_call" | custom-call | bytes 1048576 | tf_op jit(solution)/shard_map/square/pallas_call | solution.py:550
  11.3 0.0 collective-permute-done.3.refs_0_.refs_2_
  11.3 0.0 collective-permute-done.4.refs_1_.refs_3_
  11.3 0.0 collective-permute-done.1.block_ref.refs_2_
  11.4 2.5 %collective-permute-start.5 = (bf16[2,272,128]{2,1,0:T(8,128)(2,1)S(1)}, bf16[2,272,128]{2,1,0:T(8,128)(2,1)S(1)}, u32[]{:S(2)}, u32[]{:S(2)}) collective-permute-start(bf16[2,272,128]{2,1,0:T(8,128)(2,1)S(1)} %after_others.2), channel_id=1, source_target_pairs={{0,2},{1,3},{2,6},{3,7},{6,4},{7,5},{4,0},{5,1},{8,10},{9,11},{10,... | collective-permute-start | bytes 417800 | tf_op jit(solution)/shard_map/ppermute | solution.py:414
  13.9 0.0 collective-permute-start
  13.9 2.2 %prepare.1 = (bf16[4,2,3,256,128]{4,3,2,1,0:T(8,128)(2,1)S(1)}, bf16[4,2,3,256,128]{4,3,2,1,0:T(8,128)(2,1)S(1)}, bf16[4,3,128,256]{3,2,1,0:T(8,128)(2,1)S(1)}, bf16[2,3,256,256]{3,2,1,0:T(8,128)(2,1)S(1)}) custom-call(bf16[4,2,6,256,128]{4,3,2,1,0:T(8,128)(2,1)} %coef_hbm.1), custom_call_target="tpu_custom_call" | custom-call | bytes 6291456 | tf_op jit(solution)/shard_map/prepare/pallas_call | solution.py:533
  16.2 0.6 %collective-permute-start.2 = (bf16[2,272,128]{2,1,0:T(8,128)(2,1)S(1)}, bf16[2,272,128]{2,1,0:T(8,128)(2,1)S(1)}, u32[]{:S(2)}, u32[]{:S(2)}) collective-permute-start(bf16[2,272,128]{2,1,0:T(8,128)(2,1)S(1)} %collective-permute-done.1.block_ref.refs_2_), channel_id=1, source_target_pairs={{0,1},{1,0},{2,3},{3,2},{4,5},{5,4},{6,7},{7,6},{8,9},{9,8},{10,11... | collective-permute-start | bytes 417800 | tf_op jit(solution)/shard_map/ppermute | solution.py:430
  16.7 0.0 collective-permute-done.7.refs_6_
  16.7 0.1 collective-permute-start.8
  16.8 1.3 %collective-permute-done.5.block_ref = bf16[2,272,128]{2,1,0:T(8,128)(2,1)S(1)} collective-permute-done((bf16[2,272,128]{2,1,0:T(8,128)(2,1)S(1)}, bf16[2,272,128]{2,1,0:T(8,128)(2,1)S(1)}, u32[]{:S(2)}, u32[]{:S(2)}) %collective-permute-start.5) | collective-permute-done | bytes 139296 | tf_op jit(solution)/shard_map/ppermute | solution.py:414
  18.1 0.1 collective-permute-start.6
  18.2 0.0 collective-permute-done.refs_1_
  18.2 0.0 collective-permute-done.2.refs_3_
  18.2 0.0 collective-permute-done.8.refs_7_
  18.3 1.3 %collective-permute-done.6.refs_5_ = bf16[2,272,128]{2,1,0:T(8,128)(2,1)S(1)} collective-permute-done((bf16[2,272,128]{2,1,0:T(8,128)(2,1)S(1)}, bf16[2,272,128]{2,1,0:T(8,128)(2,1)S(1)}, u32[]{:S(2)}, u32[]{:S(2)}) %collective-permute-start.6) | collective-permute-done | bytes 139296 | tf_op jit(solution)/shard_map/ppermute | solution.py:430
  19.6 0.8 %select_column_atoms.1 = (bf16[3,272,128]{2,1,0:T(8,128)(2,1)S(1)}, bf16[3,272,128]{2,1,0:T(8,128)(2,1)S(1)}, bf16[16,272,128]{2,1,0:T(8,128)(2,1)S(1)}) custom-call(s32[3,16]{1,0:T(4,128)S(1)} %get-tuple-element.23.atoms_ref, bf16[2,272,128]{2,1,0:T(8,128)(2,1)S(1)} %get-tuple-element.26.refs_0_, bf16[2,272,128]{2,1,0:T(8,128)(2,1)S(1)} %collective-permute-done.refs_1_, ...), custom_call_target="tpu_custom_call" | custom-call | bytes 5292032 | tf_op jit(solution)/shard_map/select_column_atoms/pallas_call | solution.py:571
  20.4 1.6 %collective-permute-start.11 = (bf16[3,272,128]{2,1,0:T(8,128)(2,1)S(1)}, bf16[3,272,128]{2,1,0:T(8,128)(2,1)S(1)}, u32[]{:S(2)}, u32[]{:S(2)}) collective-permute-start(bf16[3,272,128]{2,1,0:T(8,128)(2,1)S(1)} %get-tuple-element.29.kept_ref), channel_id=1, source_target_pairs={{0,8},{8,0},{16,24},{24,16},{2,10},{10,2},{18,26},{26,18},{4,12},{... | collective-permute-start | bytes 626696 | tf_op jit(solution)/shard_map/ppermute | solution.py:450
  21.9 0.5 %collective-permute-start.12 = (bf16[3,272,128]{2,1,0:T(8,128)(2,1)S(1)}, bf16[3,272,128]{2,1,0:T(8,128)(2,1)S(1)}, u32[]{:S(2)}, u32[]{:S(2)}) collective-permute-start(bf16[3,272,128]{2,1,0:T(8,128)(2,1)S(1)} %get-tuple-element.30.kept_ref), channel_id=1, source_target_pairs={{0,8},{8,0},{16,24},{24,16},{2,10},{10,2},{18,26},{26,18},{4,12},{... | collective-permute-start | bytes 626696 | tf_op jit(solution)/shard_map/ppermute | solution.py:450
  22.5 0.0 collective-permute-start.9
  22.5 0.9 %collective-permute-start.10 = (bf16[4,2,32,128]{3,2,1,0:T(8,128)(2,1)S(1)}, bf16[4,2,32,128]{3,2,1,0:T(8,128)(2,1)S(1)}, u32[]{:S(2)}, u32[]{:S(2)}) collective-permute-start(bf16[4,2,32,128]{3,2,1,0:T(8,128)(2,1)S(1)} %get-tuple-element.27.refs_1_), channel_id=1, source_target_pairs={{1,2},{3,4},{5,6},{2,1},{4,3},{6,5},{9,10},{11,12},{13,14},{10,9},... | collective-permute-start | bytes 196616 | tf_op jit(solution)/shard_map/ppermute | solution.py:385
  23.3 2.0 %row_exchange.1.refs_0_ = f32[4,2,64,64]{3,2,1,0:T(8,128)S(1)} custom-call(s32[3,16]{1,0:T(4,128)S(1)} %get-tuple-element.23.atoms_ref, bf16[4,2,3,256,128]{4,3,2,1,0:T(8,128)(2,1)S(1)} %get-tuple-element.24.coef_ref, bf16[4,3,128,256]{3,2,1,0:T(8,128)(2,1)S(1)} %get-tuple-element.25.refs_0_.turned_ref, bf16[16,272,128]{2,1,0:T(8,128)(2,1)S(1)} %get-tuple-element.28.all_ref), custom_call_target="tpu_custom_call" | custom-call | flops 251658240 | bytes 1572864 | tf_op jit(solution)/shard_map/row_exchange/pallas_call | solution.py:583
  25.3 0.9 %collective-permute-done.11.got_ref = bf16[3,272,128]{2,1,0:T(8,128)(2,1)S(1)} collective-permute-done((bf16[3,272,128]{2,1,0:T(8,128)(2,1)S(1)}, bf16[3,272,128]{2,1,0:T(8,128)(2,1)S(1)}, u32[]{:S(2)}, u32[]{:S(2)}) %collective-permute-start.11) | collective-permute-done | bytes 208928 | tf_op jit(solution)/shard_map/ppermute | solution.py:450
  26.3 0.9 %collective-permute-start.13 = (bf16[3,272,128]{2,1,0:T(8,128)(2,1)S(1)}, bf16[3,272,128]{2,1,0:T(8,128)(2,1)S(1)}, u32[]{:S(2)}, u32[]{:S(2)}) collective-permute-start(bf16[3,272,128]{2,1,0:T(8,128)(2,1)S(1)} %merge.2.refs_0_), channel_id=1, source_target_pairs={{0,16},{8,24},{16,0},{24,8},{2,18},{10,26},{18,2},{26,10},{4,20},{... | collective-permute-start | bytes 626696 | tf_op jit(solution)/shard_map/ppermute | solution.py:450
  27.2 0.0 collective-permute-done.9.refs_4_.refs_1_
  27.2 0.3 collective-permute-done.10.refs_5_.refs_2_
  27.5 1.0 %collective-permute-done.12.got_ref = bf16[3,272,128]{2,1,0:T(8,128)(2,1)S(1)} collective-permute-done((bf16[3,272,128]{2,1,0:T(8,128)(2,1)S(1)}, bf16[3,272,128]{2,1,0:T(8,128)(2,1)S(1)}, u32[]{:S(2)}, u32[]{:S(2)}) %collective-permute-start.12) | collective-permute-done | bytes 208928 | tf_op jit(solution)/shard_map/ppermute | solution.py:450
  28.5 0.9 %collective-permute-start.14 = (bf16[3,272,128]{2,1,0:T(8,128)(2,1)S(1)}, bf16[3,272,128]{2,1,0:T(8,128)(2,1)S(1)}, u32[]{:S(2)}, u32[]{:S(2)}) collective-permute-start(bf16[3,272,128]{2,1,0:T(8,128)(2,1)S(1)} %merge.3.refs_1_), channel_id=1, source_target_pairs={{0,16},{8,24},{16,0},{24,8},{2,18},{10,26},{18,2},{26,10},{4,20},{... | collective-permute-start | bytes 626696 | tf_op jit(solution)/shard_map/ppermute | solution.py:450
  29.4 2.8 %couple.1.base_ref = f32[4,2,32,128]{3,2,1,0:T(8,128)S(1)} custom-call(s32[4,16]{1,0:T(4,128)} %bitcast.5, f32[4,16]{1,0:T(4,128)} %bitcast.6, f32[16]{0:T(128)} %occupied_hbm.1, f32[4,2,64]{2,1,0:T(2,128)} %virtual_hbm.1, bf16[4,2,8,64,64]{4,3,2,1,0:T(8,128)(2,1)S(1)} %get-tuple-element.20.inter_ref, ...), custom_call_target="tpu_custom_call" | custom-call | flops 67108864 | bytes 1048576 | tf_op jit(solution)/shard_map/couple/pallas_call | solution.py:598
  32.2 0.0 collective-permute-done.13.refs_2_
  32.2 2.1 %collective-permute-done.14.refs_3_ = bf16[3,272,128]{2,1,0:T(8,128)(2,1)S(1)} collective-permute-done((bf16[3,272,128]{2,1,0:T(8,128)(2,1)S(1)}, bf16[3,272,128]{2,1,0:T(8,128)(2,1)S(1)}, u32[]{:S(2)}, u32[]{:S(2)}) %collective-permute-start.14) | collective-permute-done | bytes 208928 | tf_op jit(solution)/shard_map/ppermute | solution.py:450
  34.4 1.6 %column_exchange.1 = f32[4,2,4096]{2,1,0:T(2,128)} custom-call(bf16[4,2,3,256,128]{4,3,2,1,0:T(8,128)(2,1)S(1)} %get-tuple-element.18.coef_ref, bf16[2,3,256,256]{3,2,1,0:T(8,128)(2,1)S(1)} %get-tuple-element.19.turned_ref, f32[4,2,32,128]{3,2,1,0:T(8,128)S(1)} %couple.1.base_ref, f32[4,2,32,128]{3,2,1,0:T(8,128)S(1)} %get-tuple-element.22.factor_ref, ...), custom_call_target="tpu_custom_call" | custom-call | flops 251658240 | bytes 1572864 | tf_op jit(solution)/shard_map/column_exchange/pallas_call | solution.py:617
  (4 shorter events, 0.1 us)
Async XLA Ops:
  1.5 9.8 %collective-permute-start.1 = (bf16[2,272,128]{2,1,0:T(8,128)(2,1)S(1)}, bf16[2,272,128]{2,1,0:T(8,128)(2,1)S(1)}, u32[]{:S(2)}, u32[]{:S(2)}) collective-permute-start(bf16[2,272,128]{2,1,0:T(8,128)(2,1)S(1)} %get-tuple-element.26.refs_0_), channel_id=1, source_target_pairs={{0,2},{1,3},{2,6},{3,7},{6,4},{7,5},{4,0},{5,1},{8,10},{9,11},{10,... | collective-permute-start | bytes 417800 | tf_op jit(solution)/shard_map/ppermute | solution.py:414
  4.6 6.7 %collective-permute-start.3 = (bf16[4,2,32,128]{3,2,1,0:T(8,128)(2,1)S(1)}, bf16[4,2,32,128]{3,2,1,0:T(8,128)(2,1)S(1)}, u32[]{:S(2)}, u32[]{:S(2)}) collective-permute-start(bf16[4,2,32,128]{3,2,1,0:T(8,128)(2,1)S(1)} %get-tuple-element.27.refs_1_), channel_id=1, source_target_pairs={{0,8},{8,0},{16,24},{24,16},{1,9},{9,1},{17,25},{25,17},{2,10},{10... | collective-permute-start | bytes 196616 | tf_op jit(solution)/shard_map/ppermute | solution.py:372
  6.1 5.3 %collective-permute-start.4 = (bf16[4,2,32,128]{3,2,1,0:T(8,128)(2,1)S(1)}, bf16[4,2,32,128]{3,2,1,0:T(8,128)(2,1)S(1)}, u32[]{:S(2)}, u32[]{:S(2)}) collective-permute-start(bf16[4,2,32,128]{3,2,1,0:T(8,128)(2,1)S(1)} %get-tuple-element.27.refs_1_), channel_id=1, source_target_pairs={{0,24},{8,16},{16,8},{24,0},{1,25},{9,17},{17,9},{25,1},{2,26},{10... | collective-permute-start | bytes 196616 | tf_op jit(solution)/shard_map/ppermute | solution.py:375
  7.6 9.2 %collective-permute-start.7 = (bf16[2,272,128]{2,1,0:T(8,128)(2,1)S(1)}, bf16[2,272,128]{2,1,0:T(8,128)(2,1)S(1)}, u32[]{:S(2)}, u32[]{:S(2)}) collective-permute-start(bf16[2,272,128]{2,1,0:T(8,128)(2,1)S(1)} %get-tuple-element.26.refs_0_), channel_id=1, source_target_pairs={{2,0},{3,1},{6,2},{7,3},{4,6},{5,7},{0,4},{1,5},{10,8},{11,9},{14,... | collective-permute-start | bytes 417800 | tf_op jit(solution)/shard_map/ppermute | solution.py:419
  11.4 6.8 %collective-permute-start.5 = (bf16[2,272,128]{2,1,0:T(8,128)(2,1)S(1)}, bf16[2,272,128]{2,1,0:T(8,128)(2,1)S(1)}, u32[]{:S(2)}, u32[]{:S(2)}) collective-permute-start(bf16[2,272,128]{2,1,0:T(8,128)(2,1)S(1)} %after_others.2), channel_id=1, source_target_pairs={{0,2},{1,3},{2,6},{3,7},{6,4},{7,5},{4,0},{5,1},{8,10},{9,11},{10,... | collective-permute-start | bytes 417800 | tf_op jit(solution)/shard_map/ppermute | solution.py:414
  13.9 4.3 %collective-permute-start = (bf16[2,272,128]{2,1,0:T(8,128)(2,1)S(1)}, bf16[2,272,128]{2,1,0:T(8,128)(2,1)S(1)}, u32[]{:S(2)}, u32[]{:S(2)}) collective-permute-start(bf16[2,272,128]{2,1,0:T(8,128)(2,1)S(1)} %get-tuple-element.26.refs_0_), channel_id=1, source_target_pairs={{0,1},{1,0},{2,3},{3,2},{4,5},{5,4},{6,7},{7,6},{8,9},{9,8},{10,11... | collective-permute-start | bytes 417800 | tf_op jit(solution)/shard_map/ppermute | solution.py:430
  16.2 2.1 %collective-permute-start.2 = (bf16[2,272,128]{2,1,0:T(8,128)(2,1)S(1)}, bf16[2,272,128]{2,1,0:T(8,128)(2,1)S(1)}, u32[]{:S(2)}, u32[]{:S(2)}) collective-permute-start(bf16[2,272,128]{2,1,0:T(8,128)(2,1)S(1)} %collective-permute-done.1.block_ref.refs_2_), channel_id=1, source_target_pairs={{0,1},{1,0},{2,3},{3,2},{4,5},{5,4},{6,7},{7,6},{8,9},{9,8},{10,11... | collective-permute-start | bytes 417800 | tf_op jit(solution)/shard_map/ppermute | solution.py:430
  16.7 1.5 %collective-permute-start.8 = (bf16[2,272,128]{2,1,0:T(8,128)(2,1)S(1)}, bf16[2,272,128]{2,1,0:T(8,128)(2,1)S(1)}, u32[]{:S(2)}, u32[]{:S(2)}) collective-permute-start(bf16[2,272,128]{2,1,0:T(8,128)(2,1)S(1)} %collective-permute-done.7.refs_6_), channel_id=1, source_target_pairs={{0,1},{1,0},{2,3},{3,2},{4,5},{5,4},{6,7},{7,6},{8,9},{9,8},{10,11... | collective-permute-start | bytes 417800 | tf_op jit(solution)/shard_map/ppermute | solution.py:430
  18.1 1.4 %collective-permute-start.6 = (bf16[2,272,128]{2,1,0:T(8,128)(2,1)S(1)}, bf16[2,272,128]{2,1,0:T(8,128)(2,1)S(1)}, u32[]{:S(2)}, u32[]{:S(2)}) collective-permute-start(bf16[2,272,128]{2,1,0:T(8,128)(2,1)S(1)} %after_others.3.refs_4_), channel_id=1, source_target_pairs={{0,1},{1,0},{2,3},{3,2},{4,5},{5,4},{6,7},{7,6},{8,9},{9,8},{10,11... | collective-permute-start | bytes 417800 | tf_op jit(solution)/shard_map/ppermute | solution.py:430
  20.4 5.9 %collective-permute-start.11 = (bf16[3,272,128]{2,1,0:T(8,128)(2,1)S(1)}, bf16[3,272,128]{2,1,0:T(8,128)(2,1)S(1)}, u32[]{:S(2)}, u32[]{:S(2)}) collective-permute-start(bf16[3,272,128]{2,1,0:T(8,128)(2,1)S(1)} %get-tuple-element.29.kept_ref), channel_id=1, source_target_pairs={{0,8},{8,0},{16,24},{24,16},{2,10},{10,2},{18,26},{26,18},{4,12},{... | collective-permute-start | bytes 626696 | tf_op jit(solution)/shard_map/ppermute | solution.py:450
  21.9 6.5 %collective-permute-start.12 = (bf16[3,272,128]{2,1,0:T(8,128)(2,1)S(1)}, bf16[3,272,128]{2,1,0:T(8,128)(2,1)S(1)}, u32[]{:S(2)}, u32[]{:S(2)}) collective-permute-start(bf16[3,272,128]{2,1,0:T(8,128)(2,1)S(1)} %get-tuple-element.30.kept_ref), channel_id=1, source_target_pairs={{0,8},{8,0},{16,24},{24,16},{2,10},{10,2},{18,26},{26,18},{4,12},{... | collective-permute-start | bytes 626696 | tf_op jit(solution)/shard_map/ppermute | solution.py:450
  22.5 4.7 %collective-permute-start.9 = (bf16[4,2,32,128]{3,2,1,0:T(8,128)(2,1)S(1)}, bf16[4,2,32,128]{3,2,1,0:T(8,128)(2,1)S(1)}, u32[]{:S(2)}, u32[]{:S(2)}) collective-permute-start(bf16[4,2,32,128]{3,2,1,0:T(8,128)(2,1)S(1)} %get-tuple-element.27.refs_1_), channel_id=1, source_target_pairs={{0,1},{1,0},{2,3},{3,2},{4,5},{5,4},{6,7},{7,6},{8,9},{9,8},{10,11... | collective-permute-start | bytes 196616 | tf_op jit(solution)/shard_map/ppermute | solution.py:372
  22.5 5.0 %collective-permute-start.10 = (bf16[4,2,32,128]{3,2,1,0:T(8,128)(2,1)S(1)}, bf16[4,2,32,128]{3,2,1,0:T(8,128)(2,1)S(1)}, u32[]{:S(2)}, u32[]{:S(2)}) collective-permute-start(bf16[4,2,32,128]{3,2,1,0:T(8,128)(2,1)S(1)} %get-tuple-element.27.refs_1_), channel_id=1, source_target_pairs={{1,2},{3,4},{5,6},{2,1},{4,3},{6,5},{9,10},{11,12},{13,14},{10,9},... | collective-permute-start | bytes 196616 | tf_op jit(solution)/shard_map/ppermute | solution.py:385
  26.3 6.0 %collective-permute-start.13 = (bf16[3,272,128]{2,1,0:T(8,128)(2,1)S(1)}, bf16[3,272,128]{2,1,0:T(8,128)(2,1)S(1)}, u32[]{:S(2)}, u32[]{:S(2)}) collective-permute-start(bf16[3,272,128]{2,1,0:T(8,128)(2,1)S(1)} %merge.2.refs_0_), channel_id=1, source_target_pairs={{0,16},{8,24},{16,0},{24,8},{2,18},{10,26},{18,2},{26,10},{4,20},{... | collective-permute-start | bytes 626696 | tf_op jit(solution)/shard_map/ppermute | solution.py:450
  28.5 5.9 %collective-permute-start.14 = (bf16[3,272,128]{2,1,0:T(8,128)(2,1)S(1)}, bf16[3,272,128]{2,1,0:T(8,128)(2,1)S(1)}, u32[]{:S(2)}, u32[]{:S(2)}) collective-permute-start(bf16[3,272,128]{2,1,0:T(8,128)(2,1)S(1)} %merge.3.refs_1_), channel_id=1, source_target_pairs={{0,16},{8,24},{16,0},{24,8},{2,18},{10,26},{18,2},{26,10},{4,20},{... | collective-permute-start | bytes 626696 | tf_op jit(solution)/shard_map/ppermute | solution.py:450

commit v8 on v7

--- a/solution.py
+++ b/solution.py
@@ -316,40 +316,54 @@
     merge_into(takers, column_count, row_count, kept_ref, got_ref, refs[-1])
 
 
-def column_kernel(
-    takers, coef_ref, turned_ref, base_ref, factor_ref, *refs,
-):
+def one_column(takers, j, coef_ref, turned_ref, base_ref, factor_ref, held_ref, got_ref, scratch, store):
     row_count, column_count, domain, pao, lanes = coef_ref.shape
-    held, got = refs[:column_count], refs[column_count : 2 * column_count]
-    out_hbm, packed_ref, metric_ref, wide_ref, flat_ref, out_ref, sems = refs[2 * column_count :]
     npno = lanes // 2
     chunks = npno // 2
-    for j in range(column_count):
-        target = packed_ref.at[pl.ds(j * domain, domain)]
-        merge_into(takers, column_count, row_count, held[j], got[j], target)
-    slots = column_count * domain
-    lows = [unpack(packed_ref[index], metric_ref.at[index]) for index in range(slots)]
-    products = []
-    for j in range(column_count):
-        parts = []
-        for s in range(domain):
-            left = turned_ref[j, s]
-            part = dot(left, metric_ref[j * domain + s]) + left.astype(F32) * lows[j * domain + s]
-            parts.append(part.astype(BF16))
-        products.append(jnp.concatenate(parts, axis=1))
+    packed_ref, metric_ref, wide_ref = scratch
+    merge_into(takers, column_count, row_count, held_ref, got_ref, packed_ref)
+    lows = [unpack(packed_ref[s], metric_ref.at[s]) for s in range(domain)]
+    parts = []
+    for s in range(domain):
+        left = turned_ref[j, s]
+        part = dot(left, metric_ref[s]) + left.astype(F32) * lows[s]
+        parts.append(part.astype(BF16))
+    product = jnp.concatenate(parts, axis=1)
     lane = lax.broadcasted_iota(jnp.int32, (chunks, lanes), 1)
     for i in range(row_count):
-        for j in range(column_count):
-            wide_ref[i, j] = dot(
-                products[j][i * npno : (i + 1) * npno], coef_ref[i, j].reshape(domain * pao, lanes)
-            )
-            even = wide_ref[i, j, pl.ds(0, chunks, 2), :]
-            odd = wide_ref[i, j, pl.ds(1, chunks, 2), :]
-            total = jnp.where(lane < npno, pltpu.roll(even, npno, 1), odd)
-            flat_ref[i, j] = base_ref[i, j] + factor_ref[i, j] * total
+        wide_ref[i] = dot(
+            product[i * npno : (i + 1) * npno], coef_ref[i, j].reshape(domain * pao, lanes)
+        )
+        even = wide_ref[i, pl.ds(0, chunks, 2), :]
+        odd = wide_ref[i, pl.ds(1, chunks, 2), :]
+        total = jnp.where(lane < npno, pltpu.roll(even, npno, 1), odd)
+        store(i, base_ref[i, j] + factor_ref[i, j] * total)
+
+
+def first_columns_kernel(takers, j, *refs):
+    out_ref, scratch = refs[6], refs[7:]
+
+    def store(i, value):
+        out_ref[i] = value
+
+    one_column(takers, j, *refs[:6], scratch, store)
+
+
+def last_column_kernel(takers, *refs):
+    row_count, column_count, _, _, lanes = refs[0].shape
+    chunks = refs[2].shape[2]
+    done = refs[6 : 5 + column_count]
+    out_hbm, packed_ref, metric_ref, wide_ref, flat_ref, out_ref, sems = refs[5 + column_count :]
+
+    def store(i, value):
+        flat_ref[i, column_count - 1] = value
+        for j in range(column_count - 1):
+            flat_ref[i, j] = done[j][i]
         for q in range(chunks):
             out_ref[i, :, q * lanes : (q + 1) * lanes] = flat_ref[i, :, q, :]
         pltpu.make_async_copy(out_ref.at[i], out_hbm.at[i], sems.at[i]).start()
+
+    one_column(takers, column_count - 1, *refs[:6], (packed_ref, metric_ref, wide_ref), store)
     for i in range(row_count):
         pltpu.make_async_copy(out_ref.at[i], out_hbm.at[i], sems.at[i]).wait()
 
@@ -592,7 +606,7 @@
     )(table, own_coefficients, own_turned, metrics)
 
     sources = [c * column_count // row_count for c in range(columns)]
-    first = [[]] * (column_count - 1) + [[exchange] + col_halos]
+    first = [[exchange]] + [[]] * (column_count - 2) + [col_halos]
     pieces, takers = spread(pieces, sources, column_count, row_count, first)
 
     base = call(
@@ -614,23 +628,41 @@
         intersections.size * 4,
     )(partner, value, occupied, virtual, mats, turned_mats, factor, exchange, *blocks)
 
+    scratch = [
+        pltpu.VMEM((domain, depth, half), BF16),
+        pltpu.VMEM((domain, pao, pao), BF16),
+        pltpu.VMEM((row_count, npno, lanes), F32),
+    ]
+    cost = 2 * row_count * domain * pao * npno * (pao + npno)
+    whole = (column_coefficients, turned, base, factor)
+    done = [
+        call(
+            functools.partial(first_columns_kernel, takers, j),
+            jax.ShapeDtypeStruct((row_count, chunks, lanes), F32),
+            [VMEM] * 6,
+            VMEM,
+            scratch,
+            "first_column",
+            cost,
+            coefficients.size,
+        )(*whole, pieces[j], pieces[column_count + j])
+        for j in range(column_count - 1)
+    ]
     return call(
-        functools.partial(column_kernel, takers),
+        functools.partial(last_column_kernel, takers),
         jax.ShapeDtypeStruct(amplitudes.shape, F32),
-        [VMEM] * (4 + len(pieces)),
+        [VMEM] * (5 + column_count),
         HBM,
-        [
-            pltpu.VMEM((wanted, depth, half), BF16),
-            pltpu.VMEM((wanted, pao, pao), BF16),
-            pltpu.VMEM((row_count, column_count, npno, lanes), F32),
+        scratch
+        + [
             pltpu.VMEM((row_count, column_count, chunks, lanes), F32),
             pltpu.VMEM(amplitudes.shape, F32),
             pltpu.SemaphoreType.DMA((row_count,)),
         ],
-        "column_exchange",
-        2 * row_count * column_count * domain * pao * npno * (pao + npno),
+        "last_column",
+        cost,
         coefficients.size,
-    )(column_coefficients, turned, base, factor, *pieces)
+    )(*whole, pieces[column_count - 1], pieces[-1], *done)
 
 
 def solution(mesh):

time: 36.2 us -> 35.9 us (level)
  waiting for transfers between devices: 6.98 us -> 6.28 us
  Pallas kernels: 13.4 us -> 13.8 us
    ppermute x4, waiting for transfers between devices: 4.03 us -> 3.33 us  [spread(): got = [lax.ppermute(piece, ('row', 'col'), pairs) for piece in pieces]]
    pallas_call x1 -> x2, Pallas kernels: 1.61 us -> 2.08 us  [the longest x1 1.37 us: on_device(): call(functools.partial(last_column_kernel, takers), jax.ShapeDtypeStruct(...]
  transfers between devices with their start and end apart: 15 -> 15, of which waited for: 6 -> 6; matrix products, arithmetic and copies ran while one was open for 0% -> 0% of each run, Pallas kernels for 26% -> 28%
where the time goes in v8:
time: 35.9 us; the launch traced here: 35.7 us
  starting transfers between devices  15.5 us (43%)
  Pallas kernels  13.8 us (38%)
  waiting for transfers between devices  6.28 us (17%)
    ppermute x2, starting transfers between devices, gather_metrics(): up = lax.ppermute(up, 'col', forward)  5.61 us
    ppermute x4, starting transfers between devices, spread(): got = [lax.ppermute(piece, ('row', 'col'), pairs) for piece in pieces]  3.96 us
    ppermute x4, waiting for transfers between devices, spread(): got = [lax.ppermute(piece, ('row', 'col'), pairs) for piece in pieces]  3.33 us
    pallas_call x1, Pallas kernels, on_device(): call(couple_kernel, flat, [HBM] * 4 + [VMEM] * (4 + len(blocks)), VMEM, [...  2.77 us
    pallas_call x1, Pallas kernels, on_device(): call(functools.partial(square_kernel, scale), (mats, mats, flat), [HBM] *...  2.39 us
    pallas_call x1, Pallas kernels, on_device(): call(prepare_kernel, (jax.ShapeDtypeStruct(shape, BF16), jax.ShapeDtypeSt...  2.25 us
    pallas_call x1, Pallas kernels, on_device(): call(functools.partial(row_kernel, cores, units, held, scale), jax.ShapeD...  1.99 us
    pallas_call x1, Pallas kernels, on_device(): call(pack_kernel, (jax.ShapeDtypeStruct((held, depth, half), BF16), jax.S...  1.5 us
  transfers between devices with their start and end apart: 15, of which 6 were waited for; matrix products, arithmetic and copies ran while one was open for 0% of the time, Pallas kernels for 28%

profile of v8, /device:TPU:0, one launch (start us, length us, event | category | flops | bytes accessed | tf_op | source)
XLA Modules:
  0.0 35.7 jit_solution(7037642962484717104)
XLA Ops:
  0.0 1.5 %pack_metric.1 = (bf16[2,272,128]{2,1,0:T(8,128)(2,1)S(1)}, s32[3,16]{1,0:T(4,128)S(1)}, bf16[4,2,32,128]{3,2,1,0:T(8,128)(2,1)S(1)}) custom-call(s32[3,16]{1,0:T(4,128)} %bitcast.4, bf16[4,2,4096]{2,1,0:T(2,128)(2,1)} %block_hbm.1, bf16[2,512,256]{2,1,0:T(8,128)(2,1)} %fit_ref.1), custom_call_target="tpu_custom_call" | custom-call | flops 134217728 | bytes 524288 | tf_op jit(solution)/shard_map/pack_metric/pallas_call | solution.py:523
  1.5 3.1 %collective-permute-start.1 = (bf16[2,272,128]{2,1,0:T(8,128)(2,1)S(1)}, bf16[2,272,128]{2,1,0:T(8,128)(2,1)S(1)}, u32[]{:S(2)}, u32[]{:S(2)}) collective-permute-start(bf16[2,272,128]{2,1,0:T(8,128)(2,1)S(1)} %get-tuple-element.26.refs_0_), channel_id=1, source_target_pairs={{0,2},{1,3},{2,6},{3,7},{6,4},{7,5},{4,0},{5,1},{8,10},{9,11},{10,... | collective-permute-start | bytes 417800 | tf_op jit(solution)/shard_map/ppermute | solution.py:428
  4.6 1.5 %collective-permute-start.3 = (bf16[4,2,32,128]{3,2,1,0:T(8,128)(2,1)S(1)}, bf16[4,2,32,128]{3,2,1,0:T(8,128)(2,1)S(1)}, u32[]{:S(2)}, u32[]{:S(2)}) collective-permute-start(bf16[4,2,32,128]{3,2,1,0:T(8,128)(2,1)S(1)} %get-tuple-element.27.refs_1_), channel_id=1, source_target_pairs={{0,8},{8,0},{16,24},{24,16},{1,9},{9,1},{17,25},{25,17},{2,10},{10... | collective-permute-start | bytes 196616 | tf_op jit(solution)/shard_map/ppermute | solution.py:386
  6.1 1.5 %collective-permute-start.4 = (bf16[4,2,32,128]{3,2,1,0:T(8,128)(2,1)S(1)}, bf16[4,2,32,128]{3,2,1,0:T(8,128)(2,1)S(1)}, u32[]{:S(2)}, u32[]{:S(2)}) collective-permute-start(bf16[4,2,32,128]{3,2,1,0:T(8,128)(2,1)S(1)} %get-tuple-element.27.refs_1_), channel_id=1, source_target_pairs={{0,24},{8,16},{16,8},{24,0},{1,25},{9,17},{17,9},{25,1},{2,26},{10... | collective-permute-start | bytes 196616 | tf_op jit(solution)/shard_map/ppermute | solution.py:389
  7.6 1.3 %collective-permute-start.7 = (bf16[2,272,128]{2,1,0:T(8,128)(2,1)S(1)}, bf16[2,272,128]{2,1,0:T(8,128)(2,1)S(1)}, u32[]{:S(2)}, u32[]{:S(2)}) collective-permute-start(bf16[2,272,128]{2,1,0:T(8,128)(2,1)S(1)} %get-tuple-element.26.refs_0_), channel_id=1, source_target_pairs={{2,0},{3,1},{6,2},{7,3},{4,6},{5,7},{0,4},{1,5},{10,8},{11,9},{14,... | collective-permute-start | bytes 417800 | tf_op jit(solution)/shard_map/ppermute | solution.py:433
  8.9 2.4 %square.1 = (bf16[4,2,8,64,64]{4,3,2,1,0:T(8,128)(2,1)S(1)}, bf16[4,2,8,64,64]{4,3,2,1,0:T(8,128)(2,1)S(1)}, f32[4,2,32,128]{3,2,1,0:T(8,128)S(1)}) custom-call(s32[2,4]{1,0:T(2,128)} %bitcast.7, bf16[4,2,8,4096]{3,2,1,0:T(8,128)(2,1)} %inter_hbm.1), custom_call_target="tpu_custom_call" | custom-call | bytes 1048576 | tf_op jit(solution)/shard_map/square/pallas_call | solution.py:564
  11.3 0.0 collective-permute-done.3.refs_0_.refs_2_
  11.3 0.0 collective-permute-done.4.refs_1_.refs_3_
  11.3 0.0 collective-permute-done.1.block_ref.refs_2_
  11.4 2.5 %collective-permute-start.5 = (bf16[2,272,128]{2,1,0:T(8,128)(2,1)S(1)}, bf16[2,272,128]{2,1,0:T(8,128)(2,1)S(1)}, u32[]{:S(2)}, u32[]{:S(2)}) collective-permute-start(bf16[2,272,128]{2,1,0:T(8,128)(2,1)S(1)} %after_others.2), channel_id=1, source_target_pairs={{0,2},{1,3},{2,6},{3,7},{6,4},{7,5},{4,0},{5,1},{8,10},{9,11},{10,... | collective-permute-start | bytes 417800 | tf_op jit(solution)/shard_map/ppermute | solution.py:428
  13.9 0.0 collective-permute-start
  13.9 2.2 %prepare.1 = (bf16[4,2,3,256,128]{4,3,2,1,0:T(8,128)(2,1)S(1)}, bf16[4,2,3,256,128]{4,3,2,1,0:T(8,128)(2,1)S(1)}, bf16[4,3,128,256]{3,2,1,0:T(8,128)(2,1)S(1)}, bf16[2,3,256,256]{3,2,1,0:T(8,128)(2,1)S(1)}) custom-call(bf16[4,2,6,256,128]{4,3,2,1,0:T(8,128)(2,1)} %coef_hbm.1), custom_call_target="tpu_custom_call" | custom-call | bytes 6291456 | tf_op jit(solution)/shard_map/prepare/pallas_call | solution.py:547
  16.2 0.6 %collective-permute-start.2 = (bf16[2,272,128]{2,1,0:T(8,128)(2,1)S(1)}, bf16[2,272,128]{2,1,0:T(8,128)(2,1)S(1)}, u32[]{:S(2)}, u32[]{:S(2)}) collective-permute-start(bf16[2,272,128]{2,1,0:T(8,128)(2,1)S(1)} %collective-permute-done.1.block_ref.refs_2_), channel_id=1, source_target_pairs={{0,1},{1,0},{2,3},{3,2},{4,5},{5,4},{6,7},{7,6},{8,9},{9,8},{10,11... | collective-permute-start | bytes 417800 | tf_op jit(solution)/shard_map/ppermute | solution.py:444
  16.7 0.0 collective-permute-done.7.refs_6_
  16.7 0.1 collective-permute-start.8
  16.8 1.3 %collective-permute-done.5.block_ref = bf16[2,272,128]{2,1,0:T(8,128)(2,1)S(1)} collective-permute-done((bf16[2,272,128]{2,1,0:T(8,128)(2,1)S(1)}, bf16[2,272,128]{2,1,0:T(8,128)(2,1)S(1)}, u32[]{:S(2)}, u32[]{:S(2)}) %collective-permute-start.5) | collective-permute-done | bytes 139296 | tf_op jit(solution)/shard_map/ppermute | solution.py:428
  18.1 0.1 collective-permute-start.6
  18.2 0.0 collective-permute-done.refs_1_
  18.2 0.0 collective-permute-done.2.refs_3_
  18.2 0.0 collective-permute-done.8.refs_7_
  18.3 1.3 %collective-permute-done.6.refs_5_ = bf16[2,272,128]{2,1,0:T(8,128)(2,1)S(1)} collective-permute-done((bf16[2,272,128]{2,1,0:T(8,128)(2,1)S(1)}, bf16[2,272,128]{2,1,0:T(8,128)(2,1)S(1)}, u32[]{:S(2)}, u32[]{:S(2)}) %collective-permute-start.6) | collective-permute-done | bytes 139296 | tf_op jit(solution)/shard_map/ppermute | solution.py:444
  19.6 0.8 %select_column_atoms.1 = (bf16[3,272,128]{2,1,0:T(8,128)(2,1)S(1)}, bf16[3,272,128]{2,1,0:T(8,128)(2,1)S(1)}, bf16[16,272,128]{2,1,0:T(8,128)(2,1)S(1)}) custom-call(s32[3,16]{1,0:T(4,128)S(1)} %get-tuple-element.23.atoms_ref, bf16[2,272,128]{2,1,0:T(8,128)(2,1)S(1)} %get-tuple-element.26.refs_0_, bf16[2,272,128]{2,1,0:T(8,128)(2,1)S(1)} %collective-permute-done.refs_1_, ...), custom_call_target="tpu_custom_call" | custom-call | bytes 5292032 | tf_op jit(solution)/shard_map/select_column_atoms/pallas_call | solution.py:585
  20.4 1.6 %collective-permute-start.13 = (bf16[3,272,128]{2,1,0:T(8,128)(2,1)S(1)}, bf16[3,272,128]{2,1,0:T(8,128)(2,1)S(1)}, u32[]{:S(2)}, u32[]{:S(2)}) collective-permute-start(bf16[3,272,128]{2,1,0:T(8,128)(2,1)S(1)} %get-tuple-element.30.kept_ref), channel_id=1, source_target_pairs={{0,8},{8,0},{16,24},{24,16},{2,10},{10,2},{18,26},{26,18},{4,12},{... | collective-permute-start | bytes 626696 | tf_op jit(solution)/shard_map/ppermute | solution.py:464
  21.9 0.5 %collective-permute-start.11 = (bf16[3,272,128]{2,1,0:T(8,128)(2,1)S(1)}, bf16[3,272,128]{2,1,0:T(8,128)(2,1)S(1)}, u32[]{:S(2)}, u32[]{:S(2)}) collective-permute-start(bf16[3,272,128]{2,1,0:T(8,128)(2,1)S(1)} %get-tuple-element.29.kept_ref), channel_id=1, source_target_pairs={{0,8},{8,0},{16,24},{24,16},{2,10},{10,2},{18,26},{26,18},{4,12},{... | collective-permute-start | bytes 626696 | tf_op jit(solution)/shard_map/ppermute | solution.py:464
  22.5 0.0 collective-permute-start.9
  22.5 0.9 %collective-permute-start.10 = (bf16[4,2,32,128]{3,2,1,0:T(8,128)(2,1)S(1)}, bf16[4,2,32,128]{3,2,1,0:T(8,128)(2,1)S(1)}, u32[]{:S(2)}, u32[]{:S(2)}) collective-permute-start(bf16[4,2,32,128]{3,2,1,0:T(8,128)(2,1)S(1)} %get-tuple-element.27.refs_1_), channel_id=1, source_target_pairs={{1,2},{3,4},{5,6},{2,1},{4,3},{6,5},{9,10},{11,12},{13,14},{10,9},... | collective-permute-start | bytes 196616 | tf_op jit(solution)/shard_map/ppermute | solution.py:399
  23.3 2.0 %row_exchange.1.refs_0_ = f32[4,2,64,64]{3,2,1,0:T(8,128)S(1)} custom-call(s32[3,16]{1,0:T(4,128)S(1)} %get-tuple-element.23.atoms_ref, bf16[4,2,3,256,128]{4,3,2,1,0:T(8,128)(2,1)S(1)} %get-tuple-element.24.coef_ref, bf16[4,3,128,256]{3,2,1,0:T(8,128)(2,1)S(1)} %get-tuple-element.25.refs_0_.turned_ref, bf16[16,272,128]{2,1,0:T(8,128)(2,1)S(1)} %get-tuple-element.28.all_ref), custom_call_target="tpu_custom_call" | custom-call | flops 251658240 | bytes 1572864 | tf_op jit(solution)/shard_map/row_exchange/pallas_call | solution.py:597
  25.3 0.9 %collective-permute-done.13.got_ref = bf16[3,272,128]{2,1,0:T(8,128)(2,1)S(1)} collective-permute-done((bf16[3,272,128]{2,1,0:T(8,128)(2,1)S(1)}, bf16[3,272,128]{2,1,0:T(8,128)(2,1)S(1)}, u32[]{:S(2)}, u32[]{:S(2)}) %collective-permute-start.13) | collective-permute-done | bytes 208928 | tf_op jit(solution)/shard_map/ppermute | solution.py:464
  26.3 0.9 %collective-permute-start.14 = (bf16[3,272,128]{2,1,0:T(8,128)(2,1)S(1)}, bf16[3,272,128]{2,1,0:T(8,128)(2,1)S(1)}, u32[]{:S(2)}, u32[]{:S(2)}) collective-permute-start(bf16[3,272,128]{2,1,0:T(8,128)(2,1)S(1)} %merge.3.refs_4_), channel_id=1, source_target_pairs={{0,16},{8,24},{16,0},{24,8},{2,18},{10,26},{18,2},{26,10},{4,20},{... | collective-permute-start | bytes 626696 | tf_op jit(solution)/shard_map/ppermute | solution.py:464
  27.2 0.0 collective-permute-done.9.refs_4_.refs_0_
  27.2 0.3 collective-permute-done.10.refs_5_.refs_1_
  27.5 1.0 %collective-permute-done.11.got_ref = bf16[3,272,128]{2,1,0:T(8,128)(2,1)S(1)} collective-permute-done((bf16[3,272,128]{2,1,0:T(8,128)(2,1)S(1)}, bf16[3,272,128]{2,1,0:T(8,128)(2,1)S(1)}, u32[]{:S(2)}, u32[]{:S(2)}) %collective-permute-start.11) | collective-permute-done | bytes 208928 | tf_op jit(solution)/shard_map/ppermute | solution.py:464
  28.5 0.9 %collective-permute-start.12 = (bf16[3,272,128]{2,1,0:T(8,128)(2,1)S(1)}, bf16[3,272,128]{2,1,0:T(8,128)(2,1)S(1)}, u32[]{:S(2)}, u32[]{:S(2)}) collective-permute-start(bf16[3,272,128]{2,1,0:T(8,128)(2,1)S(1)} %merge.2.refs_4_), channel_id=1, source_target_pairs={{0,16},{8,24},{16,0},{24,8},{2,18},{10,26},{18,2},{26,10},{4,20},{... | collective-permute-start | bytes 626696 | tf_op jit(solution)/shard_map/ppermute | solution.py:464
  29.4 2.8 %couple.1.refs_2_ = f32[4,2,32,128]{3,2,1,0:T(8,128)S(1)} custom-call(s32[4,16]{1,0:T(4,128)} %bitcast.5, f32[4,16]{1,0:T(4,128)} %bitcast.6, f32[16]{0:T(128)} %occupied_hbm.1, f32[4,2,64]{2,1,0:T(2,128)} %virtual_hbm.1, bf16[4,2,8,64,64]{4,3,2,1,0:T(8,128)(2,1)S(1)} %get-tuple-element.20.inter_ref, ...), custom_call_target="tpu_custom_call" | custom-call | flops 67108864 | bytes 1048576 | tf_op jit(solution)/shard_map/couple/pallas_call | solution.py:612
  32.2 0.0 collective-permute-done.14.refs_5_
  32.2 0.7 %first_column.1.refs_6_ = f32[4,32,128]{2,1,0:T(8,128)S(1)} custom-call(bf16[4,2,3,256,128]{4,3,2,1,0:T(8,128)(2,1)S(1)} %get-tuple-element.18.refs_0_, bf16[2,3,256,256]{3,2,1,0:T(8,128)(2,1)S(1)} %get-tuple-element.19.refs_1_, f32[4,2,32,128]{3,2,1,0:T(8,128)S(1)} %couple.1.refs_2_, f32[4,2,32,128]{3,2,1,0:T(8,128)S(1)} %get-tuple-element.22.factor_ref.refs_3_, ...), custom_call_target="tpu_custom_call" | custom-call | flops 125829120 | bytes 1572864 | tf_op jit(solution)/shard_map/first_column/pallas_call | solution.py:639
  32.9 1.4 %collective-permute-done.12.refs_5_ = bf16[3,272,128]{2,1,0:T(8,128)(2,1)S(1)} collective-permute-done((bf16[3,272,128]{2,1,0:T(8,128)(2,1)S(1)}, bf16[3,272,128]{2,1,0:T(8,128)(2,1)S(1)}, u32[]{:S(2)}, u32[]{:S(2)}) %collective-permute-start.12) | collective-permute-done | bytes 208928 | tf_op jit(solution)/shard_map/ppermute | solution.py:464
  34.4 1.4 %last_column.1 = f32[4,2,4096]{2,1,0:T(2,128)} custom-call(bf16[4,2,3,256,128]{4,3,2,1,0:T(8,128)(2,1)S(1)} %get-tuple-element.18.refs_0_, bf16[2,3,256,256]{3,2,1,0:T(8,128)(2,1)S(1)} %get-tuple-element.19.refs_1_, f32[4,2,32,128]{3,2,1,0:T(8,128)S(1)} %couple.1.refs_2_, f32[4,2,32,128]{3,2,1,0:T(8,128)S(1)} %get-tuple-element.22.factor_ref.refs_3_, ...), custom_call_target="tpu_custom_call" | custom-call | flops 125829120 | bytes 1572864 | tf_op jit(solution)/shard_map/last_column/pallas_call | solution.py:651
  (4 shorter events, 0.1 us)
Async XLA Ops:
  1.5 9.8 %collective-permute-start.1 = (bf16[2,272,128]{2,1,0:T(8,128)(2,1)S(1)}, bf16[2,272,128]{2,1,0:T(8,128)(2,1)S(1)}, u32[]{:S(2)}, u32[]{:S(2)}) collective-permute-start(bf16[2,272,128]{2,1,0:T(8,128)(2,1)S(1)} %get-tuple-element.26.refs_0_), channel_id=1, source_target_pairs={{0,2},{1,3},{2,6},{3,7},{6,4},{7,5},{4,0},{5,1},{8,10},{9,11},{10,... | collective-permute-start | bytes 417800 | tf_op jit(solution)/shard_map/ppermute | solution.py:428
  4.6 6.7 %collective-permute-start.3 = (bf16[4,2,32,128]{3,2,1,0:T(8,128)(2,1)S(1)}, bf16[4,2,32,128]{3,2,1,0:T(8,128)(2,1)S(1)}, u32[]{:S(2)}, u32[]{:S(2)}) collective-permute-start(bf16[4,2,32,128]{3,2,1,0:T(8,128)(2,1)S(1)} %get-tuple-element.27.refs_1_), channel_id=1, source_target_pairs={{0,8},{8,0},{16,24},{24,16},{1,9},{9,1},{17,25},{25,17},{2,10},{10... | collective-permute-start | bytes 196616 | tf_op jit(solution)/shard_map/ppermute | solution.py:386
  6.1 5.3 %collective-permute-start.4 = (bf16[4,2,32,128]{3,2,1,0:T(8,128)(2,1)S(1)}, bf16[4,2,32,128]{3,2,1,0:T(8,128)(2,1)S(1)}, u32[]{:S(2)}, u32[]{:S(2)}) collective-permute-start(bf16[4,2,32,128]{3,2,1,0:T(8,128)(2,1)S(1)} %get-tuple-element.27.refs_1_), channel_id=1, source_target_pairs={{0,24},{8,16},{16,8},{24,0},{1,25},{9,17},{17,9},{25,1},{2,26},{10... | collective-permute-start | bytes 196616 | tf_op jit(solution)/shard_map/ppermute | solution.py:389
  7.6 9.2 %collective-permute-start.7 = (bf16[2,272,128]{2,1,0:T(8,128)(2,1)S(1)}, bf16[2,272,128]{2,1,0:T(8,128)(2,1)S(1)}, u32[]{:S(2)}, u32[]{:S(2)}) collective-permute-start(bf16[2,272,128]{2,1,0:T(8,128)(2,1)S(1)} %get-tuple-element.26.refs_0_), channel_id=1, source_target_pairs={{2,0},{3,1},{6,2},{7,3},{4,6},{5,7},{0,4},{1,5},{10,8},{11,9},{14,... | collective-permute-start | bytes 417800 | tf_op jit(solution)/shard_map/ppermute | solution.py:433
  11.4 6.8 %collective-permute-start.5 = (bf16[2,272,128]{2,1,0:T(8,128)(2,1)S(1)}, bf16[2,272,128]{2,1,0:T(8,128)(2,1)S(1)}, u32[]{:S(2)}, u32[]{:S(2)}) collective-permute-start(bf16[2,272,128]{2,1,0:T(8,128)(2,1)S(1)} %after_others.2), channel_id=1, source_target_pairs={{0,2},{1,3},{2,6},{3,7},{6,4},{7,5},{4,0},{5,1},{8,10},{9,11},{10,... | collective-permute-start | bytes 417800 | tf_op jit(solution)/shard_map/ppermute | solution.py:428
  13.9 4.3 %collective-permute-start = (bf16[2,272,128]{2,1,0:T(8,128)(2,1)S(1)}, bf16[2,272,128]{2,1,0:T(8,128)(2,1)S(1)}, u32[]{:S(2)}, u32[]{:S(2)}) collective-permute-start(bf16[2,272,128]{2,1,0:T(8,128)(2,1)S(1)} %get-tuple-element.26.refs_0_), channel_id=1, source_target_pairs={{0,1},{1,0},{2,3},{3,2},{4,5},{5,4},{6,7},{7,6},{8,9},{9,8},{10,11... | collective-permute-start | bytes 417800 | tf_op jit(solution)/shard_map/ppermute | solution.py:444
  16.2 2.1 %collective-permute-start.2 = (bf16[2,272,128]{2,1,0:T(8,128)(2,1)S(1)}, bf16[2,272,128]{2,1,0:T(8,128)(2,1)S(1)}, u32[]{:S(2)}, u32[]{:S(2)}) collective-permute-start(bf16[2,272,128]{2,1,0:T(8,128)(2,1)S(1)} %collective-permute-done.1.block_ref.refs_2_), channel_id=1, source_target_pairs={{0,1},{1,0},{2,3},{3,2},{4,5},{5,4},{6,7},{7,6},{8,9},{9,8},{10,11... | collective-permute-start | bytes 417800 | tf_op jit(solution)/shard_map/ppermute | solution.py:444
  16.7 1.5 %collective-permute-start.8 = (bf16[2,272,128]{2,1,0:T(8,128)(2,1)S(1)}, bf16[2,272,128]{2,1,0:T(8,128)(2,1)S(1)}, u32[]{:S(2)}, u32[]{:S(2)}) collective-permute-start(bf16[2,272,128]{2,1,0:T(8,128)(2,1)S(1)} %collective-permute-done.7.refs_6_), channel_id=1, source_target_pairs={{0,1},{1,0},{2,3},{3,2},{4,5},{5,4},{6,7},{7,6},{8,9},{9,8},{10,11... | collective-permute-start | bytes 417800 | tf_op jit(solution)/shard_map/ppermute | solution.py:444
  18.1 1.4 %collective-permute-start.6 = (bf16[2,272,128]{2,1,0:T(8,128)(2,1)S(1)}, bf16[2,272,128]{2,1,0:T(8,128)(2,1)S(1)}, u32[]{:S(2)}, u32[]{:S(2)}) collective-permute-start(bf16[2,272,128]{2,1,0:T(8,128)(2,1)S(1)} %after_others.3.refs_4_), channel_id=1, source_target_pairs={{0,1},{1,0},{2,3},{3,2},{4,5},{5,4},{6,7},{7,6},{8,9},{9,8},{10,11... | collective-permute-start | bytes 417800 | tf_op jit(solution)/shard_map/ppermute | solution.py:444
  20.4 5.9 %collective-permute-start.13 = (bf16[3,272,128]{2,1,0:T(8,128)(2,1)S(1)}, bf16[3,272,128]{2,1,0:T(8,128)(2,1)S(1)}, u32[]{:S(2)}, u32[]{:S(2)}) collective-permute-start(bf16[3,272,128]{2,1,0:T(8,128)(2,1)S(1)} %get-tuple-element.30.kept_ref), channel_id=1, source_target_pairs={{0,8},{8,0},{16,24},{24,16},{2,10},{10,2},{18,26},{26,18},{4,12},{... | collective-permute-start | bytes 626696 | tf_op jit(solution)/shard_map/ppermute | solution.py:464
  21.9 6.5 %collective-permute-start.11 = (bf16[3,272,128]{2,1,0:T(8,128)(2,1)S(1)}, bf16[3,272,128]{2,1,0:T(8,128)(2,1)S(1)}, u32[]{:S(2)}, u32[]{:S(2)}) collective-permute-start(bf16[3,272,128]{2,1,0:T(8,128)(2,1)S(1)} %get-tuple-element.29.kept_ref), channel_id=1, source_target_pairs={{0,8},{8,0},{16,24},{24,16},{2,10},{10,2},{18,26},{26,18},{4,12},{... | collective-permute-start | bytes 626696 | tf_op jit(solution)/shard_map/ppermute | solution.py:464
  22.5 4.7 %collective-permute-start.9 = (bf16[4,2,32,128]{3,2,1,0:T(8,128)(2,1)S(1)}, bf16[4,2,32,128]{3,2,1,0:T(8,128)(2,1)S(1)}, u32[]{:S(2)}, u32[]{:S(2)}) collective-permute-start(bf16[4,2,32,128]{3,2,1,0:T(8,128)(2,1)S(1)} %get-tuple-element.27.refs_1_), channel_id=1, source_target_pairs={{0,1},{1,0},{2,3},{3,2},{4,5},{5,4},{6,7},{7,6},{8,9},{9,8},{10,11... | collective-permute-start | bytes 196616 | tf_op jit(solution)/shard_map/ppermute | solution.py:386
  22.5 5.0 %collective-permute-start.10 = (bf16[4,2,32,128]{3,2,1,0:T(8,128)(2,1)S(1)}, bf16[4,2,32,128]{3,2,1,0:T(8,128)(2,1)S(1)}, u32[]{:S(2)}, u32[]{:S(2)}) collective-permute-start(bf16[4,2,32,128]{3,2,1,0:T(8,128)(2,1)S(1)} %get-tuple-element.27.refs_1_), channel_id=1, source_target_pairs={{1,2},{3,4},{5,6},{2,1},{4,3},{6,5},{9,10},{11,12},{13,14},{10,9},... | collective-permute-start | bytes 196616 | tf_op jit(solution)/shard_map/ppermute | solution.py:399
  26.3 6.0 %collective-permute-start.14 = (bf16[3,272,128]{2,1,0:T(8,128)(2,1)S(1)}, bf16[3,272,128]{2,1,0:T(8,128)(2,1)S(1)}, u32[]{:S(2)}, u32[]{:S(2)}) collective-permute-start(bf16[3,272,128]{2,1,0:T(8,128)(2,1)S(1)} %merge.3.refs_4_), channel_id=1, source_target_pairs={{0,16},{8,24},{16,0},{24,8},{2,18},{10,26},{18,2},{26,10},{4,20},{... | collective-permute-start | bytes 626696 | tf_op jit(solution)/shard_map/ppermute | solution.py:464
  28.5 5.9 %collective-permute-start.12 = (bf16[3,272,128]{2,1,0:T(8,128)(2,1)S(1)}, bf16[3,272,128]{2,1,0:T(8,128)(2,1)S(1)}, u32[]{:S(2)}, u32[]{:S(2)}) collective-permute-start(bf16[3,272,128]{2,1,0:T(8,128)(2,1)S(1)} %merge.2.refs_4_), channel_id=1, source_target_pairs={{0,16},{8,24},{16,0},{24,8},{2,18},{10,26},{18,2},{26,10},{4,20},{... | collective-permute-start | bytes 626696 | tf_op jit(solution)/shard_map/ppermute | solution.py:464
